TPU v7x, 128 devices: a whole 4x4x4 slice. The times are simulated.
128 devices in a mesh: gx: 16 (over z, x), gy: 8 (over y, core).
Axes of the slice: x: 4, y: 4, z: 4, core: 2. Of those that a mesh axis runs over, the one named last changes fastest.
Arguments:
- features: bfloat16 [256, 128, 128, 128], P('gx', 'gy'), may hold values from -30 to 30
- occupancy: int32 [256, 128, 128], P('gx', 'gy'), may hold values 0 or 1
- owner_map: int32 [32, 16, 16], P('gx', 'gy'), may hold values from -1 to 255, as said below
- kernel: bfloat16 [27, 128, 128], replicated, may hold values from -0.109375 to 0.109375
- norm_gain: float32 [128], replicated, may hold values from 0.25 to 1.75
- norm_bias: float32 [128], replicated, may hold values from -2.5 to 2.5
Outputs:
- result: bfloat16 [256, 8, 512, 128], P('gx', 'gy')
Inputs may be any that keep to these rules, and one draw needn't show every extreme that they name: `owner_map`: A value g >= 0 hands the brick to the device g // 16 along gx in the brick's own gy row, into its slot g % 16. In every gy row each value 0 to 255 occurs exactly once. One device holds at most 32 active bricks and hands at most 2 of them to one owner; both bounds are reached in every row.
All inputs are finite; a program needn't handle non-finite values. No bound on the sum of `occupancy` on one device may be relied on, other than what follows from the above.
Results may differ from a plain program's by a relative error of at most 0.007.
Values may be sent and summed in bfloat16 or wider, within the bound.
No kernel may reach another device: no remote copies, remote signals or barrier semaphores. Data moves between devices by JAX's collectives and lax.ppermute only.
A program may use at most 320 MiB of HBM per device.

v0:
```python
import jax
import jax.numpy as jnp
from jax import lax
from jax.sharding import PartitionSpec as P

O = 16


EPSILON = 1e-05


def with_halo(block, sides, width):
    for axis, dim in sides:
        count = lax.axis_size(axis)
        forward = [(i, i + 1) for i in range(count - 1)]
        backward = [(target, source) for source, target in forward]
        low = lax.ppermute(
            lax.slice_in_dim(block, block.shape[dim] - width, None, axis=dim), axis, forward
        )
        high = lax.ppermute(lax.slice_in_dim(block, 0, width, axis=dim), axis, backward)
        block = jnp.concatenate([low, block, high], axis=dim)
    return block


def brick_major(voxels, brick_grid, brick_edge):
    span_x, span_y, span_z = brick_grid
    shaped = voxels.reshape(span_x, brick_edge, span_y, brick_edge, span_z, brick_edge)
    return shaped.transpose(0, 2, 4, 1, 3, 5).reshape(span_x * span_y * span_z, brick_edge**3)


def cut_windows(padded, positions, brick_grid, brick_edge):
    span_y, span_z = (brick_grid[1], brick_grid[2])
    window_shape = (brick_edge + 2, brick_edge + 2, brick_edge + 2, padded.shape[3])

    def cut_one(position):
        along_x = position // (span_y * span_z)
        along_y = position // span_z % span_y
        along_z = position % span_z
        starts = (
            along_x * brick_edge,
            along_y * brick_edge,
            along_z * brick_edge,
            jnp.zeros((), jnp.int32),
        )
        return lax.dynamic_slice(padded, starts, window_shape)

    return jax.vmap(cut_one)(positions)


def convolve(windows, kernel, brick_edge):
    amount = windows.shape[0]
    channels = windows.shape[4]
    outputs = kernel.shape[2]
    rows_all = amount * brick_edge**3
    summed = jnp.zeros((rows_all, outputs), jnp.float32)
    for step_x in range(3):
        for step_y in range(3):
            slices = [
                windows[
                    :,
                    step_x : step_x + brick_edge,
                    step_y : step_y + brick_edge,
                    step_z : step_z + brick_edge,
                    :,
                ]
                for step_z in range(3)
            ]
            first_tap = step_x * 9 + step_y * 3
            for step_z in range(3):
                tap_slice = slices[step_z].reshape(rows_all, channels)
                summed = summed + jnp.dot(
                    tap_slice, kernel[first_tap + step_z], preferred_element_type=jnp.float32
                )
    return summed.reshape(amount, brick_edge**3, outputs)


def moments(convolved, occupied_centre):
    widened = convolved.astype(jnp.float32)
    summed = jnp.sum(widened, axis=(0, 1))
    squared = jnp.sum(widened * widened, axis=(0, 1))
    voxels_on = jnp.sum(occupied_centre.astype(jnp.float32))
    return lax.psum((summed, squared, voxels_on), ("gx", "gy"))


def finish(convolved, centre, occupied_centre, totals, norm_gain, norm_bias):
    summed, squared, voxels_on = totals
    mean_value = summed / voxels_on
    variance = squared / voxels_on - mean_value * mean_value
    factor = norm_gain / jnp.sqrt(variance + EPSILON)
    shifted = factor * (convolved.astype(jnp.float32) - mean_value) + norm_bias
    combined = centre.astype(jnp.float32) + occupied_centre[..., None].astype(
        jnp.float32
    ) * jax.nn.silu(shifted)
    return combined.astype(jnp.bfloat16)


def pick_received(slot_ids, payloads, owned):
    flat_ids = slot_ids.reshape(-1)
    matched = flat_ids[None, :] == jnp.arange(owned, dtype=jnp.int32)[:, None]
    source = jnp.sum(
        jnp.where(matched, jnp.arange(flat_ids.shape[0], dtype=jnp.int32)[None, :], 0), axis=1
    )
    return tuple(
        (
            jnp.take(payload.reshape((-1,) + payload.shape[2:]), source, axis=0)
            for payload in payloads
        )
    )


def on_device(features, occupancy, owner_map, kernel, norm_gain, norm_bias):
    span_x, span_y, span_z = owner_map.shape
    brick_grid = (span_x, span_y, span_z)
    brick_edge = features.shape[0] // span_x
    channels = features.shape[3]
    volume = brick_edge**3
    places = span_x * span_y * span_z
    owners = lax.axis_size("gx")
    capacity = (2 * O + owners - 1) // owners
    active = (owner_map >= 0).astype(jnp.int32)
    occupied_grid = (
        occupancy.reshape(span_x, brick_edge, span_y, brick_edge, span_z, brick_edge)
        * active[:, None, :, None, :, None]
    ).reshape(occupancy.shape)
    masked = features * occupied_grid[..., None].astype(jnp.bfloat16)
    lifted = jnp.pad(masked, ((0, 0), (0, 0), (1, 1), (0, 0)))
    padded = with_halo(lifted, (("gx", 0), ("gy", 1)), 1)
    occupied_bricks = brick_major(occupied_grid, brick_grid, brick_edge)
    flat_owner = owner_map.reshape(places)
    place_index = jnp.arange(places, dtype=jnp.int32)
    owner_of = jnp.where(flat_owner >= 0, flat_owner // O, -1)
    owner_hits = (owner_of[:, None] == jnp.arange(owners, dtype=jnp.int32)[None, :]).astype(
        jnp.int32
    )
    pair_rank = jnp.sum((jnp.cumsum(owner_hits, axis=0) - owner_hits) * owner_hits, axis=1)
    send_owner = jnp.repeat(jnp.arange(owners, dtype=jnp.int32), capacity)
    send_rank = jnp.tile(jnp.arange(capacity, dtype=jnp.int32), owners)
    chosen = (owner_of[None, :] == send_owner[:, None]) & (pair_rank[None, :] == send_rank[:, None])
    send_place = jnp.sum(jnp.where(chosen, place_index[None, :], 0), axis=1)
    send_valid = jnp.any(chosen, axis=1)
    slot_values = jnp.sum(jnp.where(chosen, (flat_owner % O)[None, :], 0), axis=1)
    send_slot = jnp.where(send_valid, slot_values, -1)
    windows = cut_windows(padded, send_place, brick_grid, brick_edge)
    windows = jnp.where(send_valid[:, None, None, None, None], windows, jnp.zeros((), jnp.bfloat16))
    sent_occupied = jnp.take(occupied_bricks, send_place, axis=0) * send_valid[:, None].astype(
        jnp.int32
    )
    window_shape = windows.shape[1:]
    arrivals = (
        lax.all_to_all(
            windows.reshape((owners, capacity) + window_shape),
            "gx",
            split_axis=0,
            concat_axis=0,
            tiled=True,
        ),
        lax.all_to_all(
            sent_occupied.reshape(owners, capacity, volume),
            "gx",
            split_axis=0,
            concat_axis=0,
            tiled=True,
        ),
        lax.all_to_all(
            send_slot.reshape(owners, capacity), "gx", split_axis=0, concat_axis=0, tiled=True
        ),
    )
    got_windows, got_occupied = pick_received(arrivals[2], (arrivals[0], arrivals[1]), O)
    convolved = (
        convolve(got_windows, kernel, brick_edge) * got_occupied[:, :, None].astype(jnp.float32)
    ).astype(jnp.bfloat16)
    totals = moments(convolved, got_occupied)
    centre = got_windows[:, 1:-1, 1:-1, 1:-1, :].reshape(O, volume, channels)
    result = finish(convolved, centre, got_occupied, totals, norm_gain, norm_bias)
    return result.reshape(O, 1, volume, channels)


def solution(mesh):
    in_specs = (P("gx", "gy", None, None), P("gx", "gy", None), P("gx", "gy", None), P(), P(), P())
    out_specs = P("gx", "gy", None, None)
    return jax.shard_map(
        on_device, mesh=mesh, in_specs=in_specs, out_specs=out_specs, check_vma=False
    )
```

profile of v0, /device:TPU:0, one launch (start us, length us, event | category | flops | bytes accessed | tf_op | source)
XLA Modules:
  0.0 602.6 jit_solution(10346331571777308014)
XLA Ops:
  2.3 8.1 %copy_multiply_fusion = bf16[16,16,128,128]{3,1,2,0:T(8,128)(2,1)S(1)} fusion(bf16[16,16,128,128]{3,2,1,0:T(8,128)(2,1)} %param.6, bf16[16,16,128]{1,2,0:T(8,128)(2,1)S(1)} %copy.60), kind=kLoop, calls=%fused_computation.35 | loop fusion | flops 4194304 | bytes 16842752 | tf_op jit(solution)/shard_map/mul | solution.py:125
  14.1 3.5 collective-permute-start
  20.6 9.0 %all-to-all-start = ((s32[16,1,2]{2,1,0:T(1,128)}), s32[16,1,2]{2,1,0:T(1,128)S(1)}, u32[]{:S(2)}, u32[]{:S(2)}) async-start(s32[16,1,2]{2,1,0:T(1,128)} %bitcast), calls=%async_computation | async-start | bytes 16384 | tf_op jit(solution)/shard_map/all_to_all | solution.py:164
  32.1 8.2 %pad.4 = bf16[16,16,130,128]{3,1,2,0:T(8,128)(2,1)} pad(bf16[16,16,128,128]{3,1,2,0:T(8,128)(2,1)} %copy-done.1, bf16[]{:T(256)} %constant.122.clone.1), padding=0_0x0_0x1_1x0_0 | pad | bytes 16908290 | tf_op jit(solution)/shard_map/jit(_pad)/pad | solution.py:126
  42.2 5.5 pad_maximum_fusion.3
  61.2 15.2 %pad_maximum_fusion = bf16[18,18,130,128]{3,1,2,0:T(8,128)(2,1)} fusion(bf16[18,1,130,128]{3,1,2,0:T(2,128)(2,1)S(1)} %copy.65, bf16[1,16,130,128]{3,1,2,0:T(8,128)(2,1)S(1)} %copy-done.30, bf16[16,16,130,128]{3,1,2,0:T(8,128)(2,1)} %pad.4, bf16[1,16,130,128]{3,1,2,0:T(8,128)(2,1)S(1)} %copy-done.28, bf16[18,1,130,128]{3,1,2,0:T(2,128)(2,1)S(1)} %copy.64), kind=kLoop, calls=%fused_computation.8 | loop fusion | flops 53913600 | bytes 21565440 | tf_op jit(solution)/shard_map/concatenate | solution.py:21
  76.4 146.5 %while.1 = (s32[]{:T(128)}, bf16[18,18,130,128]{3,1,2,0:T(8,128)(2,1)}, s32[32,4]{0,1:T(4,128)S(1)}, bf16[32,10,10,10,128]{4,3,2,1,0:T(8,128)(2,1)}, s32[]{:T(128)}) while((s32[]{:T(128)}, bf16[18,18,130,128]{3,1,2,0:T(8,128)(2,1)}, s32[32,4]{0,1:T(4,128)S(1)}, bf16[32,10,10,10,128]{4,3,2,1,0:T(8,128)(2,1)}, s32[]{:T(128)}) %tuple.61), condition=%wide.while_cond, body=%wide.while_body.sunk | while | flops 2 | bytes 1178245 | solution.py:45
  86.1 3.1 constant_dynamic-slice_fusion.5
  90.7 3.1 constant_dynamic-slice_fusion.5
  95.3 3.1 constant_dynamic-slice_fusion.5
  99.9 3.1 constant_dynamic-slice_fusion.5
  113.5 3.1 constant_dynamic-slice_fusion.5
  118.1 3.1 constant_dynamic-slice_fusion.5
  122.7 3.1 constant_dynamic-slice_fusion.5
  136.4 3.1 constant_dynamic-slice_fusion.5
  154.6 3.1 constant_dynamic-slice_fusion.5
  209.6 3.1 constant_dynamic-slice_fusion.5
  222.9 17.4 %copy.67 = bf16[32,10,10,10,128]{4,0,3,2,1:T(8,128)(2,1)} copy(bf16[32,10,10,10,128]{4,3,2,1,0:T(8,128)(2,1)} %get-tuple-element.12) | data formatting | bytes 16384000 | tf_op jit(solution)/shard_map/vmap()/gather | solution.py:45
  240.3 7.3 %all-to-all-start.2 = ((s32[16,2,512]{2,1,0:T(2,128)}), s32[16,2,512]{2,1,0:T(2,128)S(1)}, u32[]{:S(2)}, u32[]{:S(2)}) async-start(s32[16,2,512]{2,1,0:T(2,128)} %select_multiply_fusion), calls=%async_computation.2 | async-start | bytes 131072 | tf_op jit(solution)/shard_map/all_to_all | solution.py:157
  247.6 9.2 %broadcast_select_fusion = bf16[16,2,10,10,10,128]{5,1,0,4,3,2:T(2,128)(2,1)S(1)} fusion(bf16[16,2,10,10,10,128]{5,1,0,4,3,2:T(2,128)(2,1)} %bitcast.200, pred[16,2]{1,0:T(8,128)(4,1)S(1)} %broadcast_in_dim.110), kind=kLoop, calls=%fused_computation.7 | loop fusion | flops 4096000 | bytes 16384032 | tf_op jit(solution)/shard_map/jit(_where)/select_n | solution.py:144
  256.8 8.4 %copy.68 = bf16[16,2,10,10,10,128]{5,1,4,3,2,0:T(2,128)(2,1)} copy(bf16[16,2,10,10,10,128]{5,1,0,4,3,2:T(2,128)(2,1)S(1)} %broadcast_select_fusion) | data formatting | bytes 16384000 | tf_op jit(solution)/shard_map/jit(_where)/select_n | solution.py:144
  265.2 7.5 %all-to-all-start.1 = ((bf16[16,2,10,10,10,128]{5,1,4,3,2,0:T(2,128)(2,1)}), bf16[16,2,10,10,10,128]{5,1,4,3,2,0:T(2,128)(2,1)}, u32[]{:S(2)}, u32[]{:S(2)}) async-start(bf16[16,2,10,10,10,128]{5,1,4,3,2,0:T(2,128)(2,1)} %copy.68), calls=%async_computation.1 | async-start | bytes 16384000 | tf_op jit(solution)/shard_map/all_to_all | solution.py:150
  276.7 110.2 %all-to-all-done.1 = bf16[16,2,10,10,10,128]{5,1,4,3,2,0:T(2,128)(2,1)} async-done(((bf16[16,2,10,10,10,128]{5,1,4,3,2,0:T(2,128)(2,1)}), bf16[16,2,10,10,10,128]{5,1,4,3,2,0:T(2,128)(2,1)}, u32[]{:S(2)}, u32[]{:S(2)}) %all-to-all-start.1) | async-done | bytes 8192032 | tf_op jit(solution)/shard_map/all_to_all | solution.py:150
  386.9 11.0 %copy.69 = bf16[16,2,10,10,10,128]{5,1,0,4,3,2:T(2,128)(2,1)S(1)} copy(bf16[16,2,10,10,10,128]{5,1,4,3,2,0:T(2,128)(2,1)} %all-to-all-done.1) | data formatting | bytes 16384000 | tf_op jit(solution)/shard_map/all_to_all | solution.py:150
  397.9 16.1 %copy.70 = bf16[32,10,10,10,128]{4,3,2,1,0:T(8,128)(2,1)} copy(bf16[32,10,10,10,128]{4,0,3,2,1:T(8,128)(2,1)S(1)} %bitcast.201) | data formatting | bytes 16384000 | tf_op jit(solution)/shard_map/reshape | solution.py:105
  414.1 8.8 %gather_fusion = bf16[16,10,10,10,128]{4,3,2,1,0:T(8,128)(2,1)} fusion(bf16[32,10,10,10,128]{4,3,2,1,0:T(8,128)(2,1)} %copy.70, s32[1024]{0:T(1024)S(1)} %pad_clamp_fusion.1), kind=kCustom, calls=%fused_computation | custom fusion | bytes 8192064 | tf_op jit(solution)/shard_map/jit(_take)/gather | solution.py:105
  422.8 3.5 broadcast_select_fusion.1
  429.1 6.2 %fusion.69 = (bf16[16,8,8,8,128]{4,3,2,1,0:T(8,128)(2,1)}, bf16[16,8,8,8,128]{4,3,2,1,0:T(8,128)(2,1)}, bf16[16,8,8,8,128]{4,3,2,1,0:T(8,128)(2,1)}, bf16[16,8,8...) fusion(bf16[16,10,10,10,128]{4,3,2,1,0:T(8,128)(2,1)S(1)} %broa, ...), kind=kLoop, calls=%fused_computation.160 | loop fusion | bytes 33554432 | tf_op jit(solution)/shard_map/slice | solution.py:59
  435.3 36.4 %fusion.68 = (bf16[16,8,8,8,128]{4,3,2,1,0:T(8,128)(2,1)}, bf16[16,8,8,8,128]{4,3,2,1,0:T(8,128)(2,1)}, bf16[16,8,8,8,128]{4,3,2,1,0:T(8,128)(2,1)}, bf16[16,8,8...) fusion(bf16[16,10,10,10,128]{4,3,2,1,0:T(8,128)(2,1)} %copy-done), kind=kLoop, calls=%fused_computation.159 | loop fusion | bytes 79691776 | tf_op jit(solution)/shard_map/slice | solution.py:59
  513.0 4.7 fusion.1
  517.7 78.7 %all-reduce.1 = (f32[128]{0:T(128)S(1)}, f32[]{:T(128)}, f32[128]{0:T(128)S(1)}) all-reduce(f32[128]{0:T(128)S(1)} %get-tuple-element.34, f32[]{:T(128)} %get-tuple-element.50, f32[128]{0:T(128)S(1)} %get-tuple-element.33), channel_id=1, replica_groups=mesh['gx'=16,'gy'=8] {'gx','gy'}, use_global_device_ids=true, to_apply=%region_11.12 | all-reduce | flops 257 | bytes 2056 | tf_op jit(solution)/shard_map/psum | solution.py:82
  597.2 5.3 fusion.2
  (283 shorter events, 190.3 us)
Async XLA Ops:
  0.0 2.0 copy-start.32
  10.4 3.6 copy-start.1
  10.5 8.4 %copy-start.36 = (s32[2,2,16]{2,1,0:T(2,128)S(1)}, s32[2,2,16]{2,1,0:T(2,128)}, u32[]{:S(2)}) copy-start(s32[2,2,16]{2,1,0:T(2,128)} %param.8) | copy-start | bytes 772
  14.1 28.1 %collective-permute-start = (bf16[1,16,130,128]{3,1,2,0:T(8,128)(2,1)}, bf16[1,16,130,128]{3,1,2,0:T(8,128)(2,1)S(1)}, u32[]{:S(2)}, u32[]{:S(2)}) collective-permute-start(bf16[1,16,130,128]{3,1,2,0:T(8,128)(2,1)} %get-tuple-element.57), channel_id=1, source_target_pairs={{0,8},{8,16},{16,24},{24,32},{32,40},{40,48},{48,56},{56,64},{64,7... | collective-permute-start | bytes 1597448 | tf_op jit(solution)/shard_map/ppermute | solution.py:17
  17.6 24.6 %collective-permute-start.1 = (bf16[1,16,130,128]{3,1,2,0:T(8,128)(2,1)}, bf16[1,16,130,128]{3,1,2,0:T(8,128)(2,1)S(1)}, u32[]{:S(2)}, u32[]{:S(2)}) collective-permute-start(bf16[1,16,130,128]{3,1,2,0:T(8,128)(2,1)} %get-tuple-element.58), channel_id=1, source_target_pairs={{8,0},{16,8},{24,16},{32,24},{40,32},{48,40},{56,48},{64,56},{72,6... | collective-permute-start | bytes 1597448 | tf_op jit(solution)/shard_map/ppermute | solution.py:20
  20.6 219.7 %all-to-all-start = ((s32[16,1,2]{2,1,0:T(1,128)}), s32[16,1,2]{2,1,0:T(1,128)S(1)}, u32[]{:S(2)}, u32[]{:S(2)}) async-start(s32[16,1,2]{2,1,0:T(1,128)} %bitcast), calls=%async_computation | async-start | bytes 16384 | tf_op jit(solution)/shard_map/all_to_all | solution.py:164
  42.2 5.6 copy-start.27
  42.2 5.6 copy-start.29
  48.7 8.4 %collective-permute-start.2 = (bf16[18,1,130,128]{3,2,1,0:T(8,128)(2,1)}, bf16[18,1,130,128]{3,2,1,0:T(8,128)(2,1)}, u32[]{:S(2)}, u32[]{:S(2)}) collective-permute-start(bf16[18,1,130,128]{3,2,1,0:T(8,128)(2,1)} %copy.62), channel_id=1, source_target_pairs={{0,1},{1,2},{2,3},{3,4},{4,5},{5,6},{6,7},{8,9},{9,10},{10,11},{11... | collective-permute-start | bytes 1797128 | tf_op jit(solution)/shard_map/ppermute | solution.py:17
  51.7 7.4 %collective-permute-start.3 = (bf16[18,1,130,128]{3,2,1,0:T(8,128)(2,1)}, bf16[18,1,130,128]{3,2,1,0:T(8,128)(2,1)}, u32[]{:S(2)}, u32[]{:S(2)}) collective-permute-start(bf16[18,1,130,128]{3,2,1,0:T(8,128)(2,1)} %copy.63), channel_id=1, source_target_pairs={{1,0},{2,1},{3,2},{4,3},{5,4},{6,5},{7,6},{9,8},{10,9},{11,10},{12... | collective-permute-start | bytes 1797128 | tf_op jit(solution)/shard_map/ppermute | solution.py:20
  54.7 6.4 %copy-start.28 = (bf16[1,16,130,128]{3,1,2,0:T(8,128)(2,1)S(1)}, bf16[1,16,130,128]{3,1,2,0:T(8,128)(2,1)}, u32[]{:S(2)}) copy-start(bf16[1,16,130,128]{3,1,2,0:T(8,128)(2,1)} %copy-done.27) | copy-start | bytes 1597444
  54.8 6.4 %copy-start.30 = (bf16[1,16,130,128]{3,1,2,0:T(8,128)(2,1)S(1)}, bf16[1,16,130,128]{3,1,2,0:T(8,128)(2,1)}, u32[]{:S(2)}) copy-start(bf16[1,16,130,128]{3,1,2,0:T(8,128)(2,1)} %copy-done.29) | copy-start | bytes 1597444
  240.3 24.9 %all-to-all-start.2 = ((s32[16,2,512]{2,1,0:T(2,128)}), s32[16,2,512]{2,1,0:T(2,128)S(1)}, u32[]{:S(2)}, u32[]{:S(2)}) async-start(s32[16,2,512]{2,1,0:T(2,128)} %select_multiply_fusion), calls=%async_computation.2 | async-start | bytes 131072 | tf_op jit(solution)/shard_map/all_to_all | solution.py:157
  265.2 121.6 %all-to-all-start.1 = ((bf16[16,2,10,10,10,128]{5,1,4,3,2,0:T(2,128)(2,1)}), bf16[16,2,10,10,10,128]{5,1,4,3,2,0:T(2,128)(2,1)}, u32[]{:S(2)}, u32[]{:S(2)}) async-start(bf16[16,2,10,10,10,128]{5,1,4,3,2,0:T(2,128)(2,1)} %copy.68), calls=%async_computation.1 | async-start | bytes 16384000 | tf_op jit(solution)/shard_map/all_to_all | solution.py:150
  426.4 2.8 copy-start
  435.3 36.4 %copy-start.31 = (bf16[27,128,128]{2,1,0:T(8,128)(2,1)S(1)}, bf16[27,128,128]{2,1,0:T(8,128)(2,1)}, u32[]{:S(2)}) copy-start(bf16[27,128,128]{2,1,0:T(8,128)(2,1)} %param.9) | copy-start | bytes 2654212
  471.7 2.4 copy-start.25
  474.1 1.6 copy-start.24
  475.7 1.6 copy-start.23
  477.3 1.6 copy-start.22
  478.9 1.6 copy-start.21
  480.5 1.6 copy-start.19
  482.1 1.6 copy-start.20
  483.7 1.6 copy-start.18
  485.3 1.6 copy-start.17
  486.8 1.6 copy-start.16
  492.3 1.6 copy-start.13
  493.9 1.6 copy-start.12
  511.4 1.6 copy-start.35
  513.0 83.5 %copy-start.38 = (f32[128]{0:T(128)S(1)}, f32[128]{0:T(128)}, u32[]{:S(2)}) copy-start(f32[128]{0:T(128)} %param.10) | copy-start | bytes 1540
  513.0 84.1 %copy-start.34 = (f32[16,512]{1,0:T(8,128)S(1)}, f32[16,512]{1,0:T(8,128)}, u32[]{:S(2)}) copy-start(f32[16,512]{1,0:T(8,128)} %copy-done.33) | copy-start | bytes 98308
  513.0 84.1 %copy-start.37 = (f32[128]{0:T(128)S(1)}, f32[128]{0:T(128)}, u32[]{:S(2)}) copy-start(f32[128]{0:T(128)} %param.11) | copy-start | bytes 1540
  (14 other events, 21.3 us)
where the time goes:
time: 613 us; the launch traced here: 603 us
  local copies, waits for them, and re-layouts  302 us (49%)
  waiting for transfers between devices  110 us (18%)
  blocking collectives  78.7 us (13%)
  other arithmetic  53.1 us (9%)
  starting transfers between devices  32.5 us (5%)
  matrix products  24.5 us (4%)
    gather x128, local copies, waits for them, and re-layouts  146 us
    all_to_all x1, waiting for transfers between devices, on_device(): lax.all_to_all(windows.reshape((owners, capacity) + window_shape), 'gx',...  110 us
    psum x1, blocking collectives, moments(): return lax.psum((summed, squared, voxels_on), ('gx', 'gy'))  78.7 us
    slice x2, local copies, waits for them, and re-layouts, convolve(): windows[:, step_x:step_x + brick_edge, step_y:step_y + brick_edge, step_z...  42.5 us
    unnamed x79, local copies, waits for them, and re-layouts  27.6 us
    dot_general x27, matrix products, convolve(): jnp.dot(tap_slice, kernel[first_tap + step_z], preferred_element_type=jnp...  24.5 us
    gather x1, local copies, waits for them, and re-layouts, cut_one(): return lax.dynamic_slice(padded, starts, window_shape)  17.4 us
    reshape x2, local copies, waits for them, and re-layouts, pick_received(): payload.reshape((-1,) + payload.shape[2:])  16.2 us
  transfers between devices with their start and end apart: 7, of which 1 were waited for; matrix products, arithmetic and copies ran while one was open for 38% of the time, Pallas kernels for 0%

commit v1 on v0

v1 whole, which is shorter than its diff:
```python
import functools

import jax
import jax.numpy as jnp
from jax import lax
from jax.experimental import pallas as pl
from jax.experimental.pallas import tpu as pltpu
from jax.sharding import PartitionSpec as P

O = 16
E = 8
C = 128
GROUP = 4
ABSENT = -1e30
EPSILON = 1e-05
MIB = 1 << 20


def conv_kernel(
    place_ref,
    count_ref,
    masked_ref,
    x_low_ref,
    x_high_ref,
    y_low_ref,
    y_high_ref,
    corner_ref,
    occupied_ref,
    weight_ref,
    conv_ref,
    centre_ref,
    sums_ref,
    padded,
    shifted,
    total,
    sems,
):
    step = pl.program_id(0)

    @pl.when(step == 0)
    def _():
        copies = [
            pltpu.make_async_copy(
                masked_ref, padded.at[1:17, 1:17, 8:136, :], sems.at[0]
            ),
            pltpu.make_async_copy(x_low_ref, padded.at[0:1, 1:17, 8:136, :], sems.at[1]),
            pltpu.make_async_copy(x_high_ref, padded.at[17:18, 1:17, 8:136, :], sems.at[2]),
            pltpu.make_async_copy(y_low_ref, padded.at[1:17, 0:1, 8:136, :], sems.at[3]),
            pltpu.make_async_copy(y_high_ref, padded.at[1:17, 17:18, 8:136, :], sems.at[4]),
        ]
        for i in range(4):
            copies.append(
                pltpu.make_async_copy(
                    corner_ref.at[i],
                    padded.at[17 * (i // 2), 17 * (i % 2), 8:136, :],
                    sems.at[5 + i],
                )
            )
        for copy in copies:
            copy.start()
        padded[:, :, 0:8, :] = jnp.zeros((18, 18, 8, C), jnp.float32)
        padded[:, :, 136:144, :] = jnp.zeros((18, 18, 8, C), jnp.float32)
        sums_ref[...] = jnp.zeros_like(sums_ref)
        for copy in copies:
            copy.wait()

    @pl.when(step * GROUP < count_ref[0])
    def _():
        row = lax.broadcasted_iota(jnp.int32, (E, C), 0)
        lane = lax.broadcasted_iota(jnp.int32, (E, C), 1)

        def place_of(b):
            place = place_ref[step * GROUP + b]
            return place // 32, place // 16 % 2, place % 16

        def prepare(b, carry):
            bx, by, bz = place_of(b)
            for dz in range(3):
                for xx in range(10):
                    lines = [
                        padded[bx * E + xx, by * E + yy, pl.ds(bz * E + 7 + dz, E), :]
                        for yy in range(10)
                    ]
                    for parity in range(2):
                        for yp in range(5 - parity):
                            pair = jnp.concatenate(
                                [lines[2 * yp + parity], lines[2 * yp + parity + 1]], axis=0
                            )
                            shifted[parity, dz, xx % 2, b, xx // 2, yp] = pair.astype(jnp.bfloat16)
            return carry

        lax.fori_loop(0, GROUP, prepare, 0)

        for dy in range(3):
            parity, first = dy % 2, dy // 2
            parts = []
            for dz in range(3):
                for j in range(4):
                    part = shifted[
                        parity, dz, j % 2, :, j // 2 : j // 2 + 4, first : first + 4, :, :
                    ]
                    parts.append(part.reshape(GROUP * 256, C))
            product = jnp.dot(
                jnp.concatenate(parts, axis=1),
                weight_ref[dy],
                preferred_element_type=jnp.float32,
            )
            if dy == 0:
                total[...] = product
            else:
                total[...] += product

        ones = jnp.ones((C, C), jnp.bfloat16)

        def finish(b, carry):
            bx, by, bz = place_of(b)
            valid = jnp.where(step * GROUP + b < count_ref[0], 1.0, 0.0)
            eye = jnp.where(lane == bz * E + row, valid, 0.0)
            summed = jnp.zeros((E, C), jnp.float32)
            squared = jnp.zeros((E, C), jnp.float32)
            counted = jnp.zeros((E, C), jnp.float32)
            for x in range(E):
                lines = occupied_ref[pl.ds((bx * E + x) * 16 + by * E, E), :]
                spread = (lines[:, None, :] * eye[None, :, :]).reshape(E * E, C)
                live = jnp.dot(
                    spread.astype(jnp.bfloat16), ones, preferred_element_type=jnp.float32
                )
                block = total[pl.ds(b * 256 + (x // 2) * 64, 64), (x % 2) * C : (x % 2 + 1) * C]
                value = (block * live).astype(jnp.bfloat16)
                wide = value.astype(jnp.float32)
                summed += jnp.sum(wide.reshape(E, E, C), axis=0)
                squared += jnp.sum((wide * wide).reshape(E, E, C), axis=0)
                counted += jnp.sum(live.reshape(E, E, C), axis=0)
                conv_ref[b, x * 64 : (x + 1) * 64, :] = jnp.where(
                    live > 0.5, wide, ABSENT
                ).astype(jnp.bfloat16)
                centre_ref[b, x * 64 : (x + 1) * 64, :] = shifted[
                    1, 1, (x + 1) % 2, b, (x + 1) // 2, 0:4
                ].reshape(64, C)
            sums_ref[0] += summed
            sums_ref[1] += squared
            sums_ref[2] += counted
            return carry

        lax.fori_loop(0, GROUP, finish, 0)


def convolve(places, count, masked, halos, occupied, weight):
    any_spec = pl.BlockSpec(memory_space=pl.ANY)
    whole = pl.BlockSpec(memory_space=pltpu.VMEM)
    return pl.pallas_call(
        conv_kernel,
        grid_spec=pltpu.PrefetchScalarGridSpec(
            num_scalar_prefetch=2,
            grid=(32 // GROUP,),
            in_specs=[any_spec] * 6 + [whole, whole],
            out_specs=[
                pl.BlockSpec((GROUP, 512, C), lambda i, *_: (i, 0, 0)),
                pl.BlockSpec((GROUP, 512, C), lambda i, *_: (i, 0, 0)),
                pl.BlockSpec((3, E, C), lambda i, *_: (0, 0, 0)),
            ],
            scratch_shapes=[
                pltpu.VMEM((18, 18, 144, C), jnp.float32),
                pltpu.VMEM((2, 3, 2, GROUP, 5, 5, 16, C), jnp.bfloat16),
                pltpu.VMEM((GROUP * 256, 2 * C), jnp.float32),
                pltpu.SemaphoreType.DMA((9,)),
            ],
        ),
        out_shape=[
            jax.ShapeDtypeStruct((32, 512, C), jnp.bfloat16),
            jax.ShapeDtypeStruct((32, 512, C), jnp.bfloat16),
            jax.ShapeDtypeStruct((3, E, C), jnp.float32),
        ],
        compiler_params=pltpu.CompilerParams(vmem_limit_bytes=56 * MIB),
        cost_estimate=pl.CostEstimate(
            flops=2 * 32 * 256 * 4608 * 256, bytes_accessed=30 * MIB, transcendentals=0
        ),
    )(places, count, masked, *halos, occupied, weight)


def finish_kernel(index_ref, valid_ref, conv_ref, centre_ref, norm_ref, out_ref):
    @pl.when(valid_ref[pl.program_id(0)] > 0)
    def _():
        mean, factor, bias = norm_ref[0:1, :], norm_ref[1:2, :], norm_ref[2:3, :]
        for i in range(0, 512, 64):
            conv = conv_ref[0, i : i + 64, :].astype(jnp.float32)
            scaled = factor * (conv - mean) + bias
            silu = scaled * (0.5 + 0.5 * jnp.tanh(0.5 * scaled))
            silu = jnp.where(conv > 0.5 * ABSENT, silu, 0.0)
            centre = centre_ref[0, i : i + 64, :].astype(jnp.float32)
            out_ref[0, i : i + 64, :] = (centre + silu).astype(jnp.bfloat16)


def finish(index, valid, conv, centre, norm):
    return pl.pallas_call(
        finish_kernel,
        grid_spec=pltpu.PrefetchScalarGridSpec(
            num_scalar_prefetch=2,
            grid=(32,),
            in_specs=[
                pl.BlockSpec((1, 512, C), lambda i, index, valid: (index[i], 0, 0)),
                pl.BlockSpec((1, 512, C), lambda i, index, valid: (index[i], 0, 0)),
                pl.BlockSpec((8, C), lambda i, index, valid: (0, 0)),
            ],
            out_specs=pl.BlockSpec((1, 512, C), lambda i, index, valid: (i, 0, 0)),
        ),
        out_shape=jax.ShapeDtypeStruct((32, 512, C), jnp.bfloat16),
    )(index, valid, conv, centre, norm)


def pick_kernel(index_ref, in_ref, out_ref):
    out_ref[...] = in_ref[...]


def pick(index, received):
    return pl.pallas_call(
        pick_kernel,
        grid_spec=pltpu.PrefetchScalarGridSpec(
            num_scalar_prefetch=1,
            grid=(O,),
            in_specs=[pl.BlockSpec((1, 512, C), lambda i, index: (index[i], 0, 0))],
            out_specs=pl.BlockSpec((1, 512, C), lambda i, index: (i, 0, 0)),
        ),
        out_shape=jax.ShapeDtypeStruct((O, 512, C), jnp.bfloat16),
    )(index, received)


def summed_over(values, axis):
    count = lax.axis_size(axis)
    spread = jnp.broadcast_to(values[None], (count,) + values.shape)
    return jnp.sum(lax.all_to_all(spread, axis, 0, 0, tiled=True), axis=0)


def exchange_faces(features, occupied):
    def face(x, y):
        return features[x, y] * occupied[x, y][..., None]

    gx, gy = lax.axis_size("gx"), lax.axis_size("gy")

    def send(block, dx, dy):
        pairs = [
            (i * gy + j, (i + dx) * gy + j + dy)
            for i in range(gx)
            for j in range(gy)
            if 0 <= i + dx < gx and 0 <= j + dy < gy
        ]
        return lax.ppermute(block, ("gx", "gy"), pairs)

    every, first, last = slice(None), slice(0, 1), slice(15, 16)
    x_low = send(face(last, every), 1, 0)
    x_high = send(face(first, every), -1, 0)
    y_low = send(face(every, last), 0, 1)
    y_high = send(face(every, first), 0, -1)
    corners = jnp.concatenate(
        [
            send(face(last, last), 1, 1),
            send(face(last, first), 1, -1),
            send(face(first, last), -1, 1),
            send(face(first, first), -1, -1),
        ]
    ).reshape(4, 128, C)
    return tuple(h.astype(jnp.float32) for h in (x_low, x_high, y_low, y_high, corners))


def routes(owner_map):
    flat = owner_map.reshape(-1)
    index = jnp.arange(flat.shape[0], dtype=jnp.int32)
    active = flat >= 0
    owner = jnp.where(active, flat // O, -1)
    earlier = (index[None, :] < index[:, None]) & active[None, :]
    rank = jnp.sum(earlier.astype(jnp.int32), axis=1)
    pair_rank = jnp.sum((earlier & (owner[None, :] == owner[:, None])).astype(jnp.int32), axis=1)
    slot = jnp.where(active, owner * 2 + pair_rank, -1)
    slots = jnp.arange(32, dtype=jnp.int32)
    here = slot[None, :] == slots[:, None]
    compact = jnp.sum(jnp.where(here, rank[None, :], 0), axis=1)
    valid = jnp.sum(here.astype(jnp.int32), axis=1)
    sent = jnp.sum(jnp.where(here, (flat % O)[None, :] + 1, 0), axis=1) - 1
    ordered = active[None, :] & (rank[None, :] == slots[:, None])
    places = jnp.sum(jnp.where(ordered, index[None, :], 0), axis=1)
    count = jnp.sum(active.astype(jnp.int32)).reshape(1)
    return places, count, compact, valid, sent


def on_device(features, occupancy, owner_map, kernel, norm_gain, norm_bias):
    active = (owner_map >= 0).astype(jnp.int32)
    occupied_grid = (
        occupancy.reshape(2, E, 2, E, 16, E) * active[:, None, :, None, :, None]
    ).reshape(occupancy.shape)
    occupied = occupied_grid.astype(jnp.bfloat16)
    halos = exchange_faces(features, occupied)
    masked = features.astype(jnp.float32) * occupied_grid.astype(jnp.float32)[..., None]
    places, count, compact, valid, sent = routes(owner_map)
    received_slots = lax.all_to_all(
        sent.reshape(16, 1, 2), "gx", split_axis=0, concat_axis=0, tiled=True
    ).reshape(32)
    taps = kernel.reshape(3, 3, 3, C, C)
    blank = jnp.zeros((1, 3, 3, C, C), kernel.dtype)
    weight = jnp.concatenate(
        [jnp.concatenate([taps, blank]), jnp.concatenate([blank, taps])], axis=4
    )
    weight = weight.transpose(1, 2, 0, 3, 4).reshape(3, 12 * C, 2 * C)
    conv, centre, sums = convolve(
        places, count, masked, halos, occupied_grid.astype(jnp.float32).reshape(256, 128), weight
    )
    sums = jnp.sum(sums, axis=1)
    sums = summed_over(summed_over(jnp.pad(sums, ((0, 5), (0, 0))), "gx"), "gy")
    mean = sums[0] / sums[2]
    variance = sums[1] / sums[2] - mean * mean
    factor = norm_gain / jnp.sqrt(variance + EPSILON)
    norm = jnp.pad(jnp.stack([mean, factor, norm_bias]), ((0, 5), (0, 0)))
    result = finish(compact, valid, conv, centre, norm)
    received = lax.all_to_all(
        result.reshape(16, 2, 512, C), "gx", split_axis=0, concat_axis=0, tiled=True
    ).reshape(32, 512, C)
    slots = jnp.arange(O, dtype=jnp.int32)
    source = jnp.sum(
        jnp.where(
            received_slots[None, :] == slots[:, None], jnp.arange(32, dtype=jnp.int32)[None, :], 0
        ),
        axis=1,
    )
    return pick(source, received).reshape(O, 1, 512, C)


def solution(mesh):
    in_specs = (P("gx", "gy", None, None), P("gx", "gy", None), P("gx", "gy", None), P(), P(), P())
    out_specs = P("gx", "gy", None, None)
    return jax.shard_map(
        on_device, mesh=mesh, in_specs=in_specs, out_specs=out_specs, check_vma=False
    )
```

time: 613 us -> 235 us (0.38); the launches traced: 603 us -> 234 us
  local copies, waits for them, and re-layouts: 302 us -> 3.36 us
  Pallas kernels: 0 us -> 73.8 us
  blocking collectives: 78.7 us -> 17.5 us
  waiting for transfers between devices: 110 us -> 73.6 us
  matrix products: 24.5 us -> 0 us
  other arithmetic: 53.1 us -> 30.4 us
    gather x133 -> x0, local copies, waits for them, and re-layouts: 174 us -> none
    psum x1 -> x0, blocking collectives: 78.7 us -> none  [moments(): return lax.psum((summed, squared, voxels_on), ('gx', 'gy'))]
    pallas_call x0 -> x3, Pallas kernels: none -> 73.8 us  [the longest x1 42.9 us: convolve(): pl.pallas_call(conv_kernel, grid_spec=pltpu.PrefetchScalarGridSpec(num_sc...]
    slice x5 -> x1, local copies, waits for them, and re-layouts: 45.7 us -> 0.02 us  [face(): return features[x, y] * occupied[x, y][..., None]]
    all_to_all x3, waiting for transfers between devices: 110 us -> 65.2 us  [the longest x1 60.4 us: on_device(): lax.all_to_all(result.reshape(16, 2, 512, C), 'gx', split_axis=0, concat_...]
    unnamed x79 -> x17, local copies, waits for them, and re-layouts: 27.6 us -> 0.03 us
    dot_general x27 -> x0, matrix products: 24.5 us -> none  [convolve(): jnp.dot(tap_slice, kernel[first_tap + step_z], preferred_element_type=jnp...]
    reshape x6 -> x1, local copies, waits for them, and re-layouts: 19.6 us -> 0.08 us  [routes(): flat = owner_map.reshape(-1)]
  transfers between devices with their start and end apart: 7 -> 11, of which waited for: 1 -> 3; matrix products, arithmetic and copies ran while one was open for 38% -> 11% of each run, Pallas kernels for 0% -> 9%
where the time goes in v1:
time: 235 us; the launch traced here: 234 us
  Pallas kernels  73.8 us (31%)
  waiting for transfers between devices  73.6 us (31%)
  starting transfers between devices  34.6 us (15%)
  other arithmetic  30.4 us (13%)
  blocking collectives  17.5 us (7%)
  local copies, waits for them, and re-layouts  3.36 us (1%)
    all_to_all x1, waiting for transfers between devices, on_device(): lax.all_to_all(result.reshape(16, 2, 512, C), 'gx', split_axis=0, concat_...  60.4 us
    pallas_call x1, Pallas kernels, convolve(): pl.pallas_call(conv_kernel, grid_spec=pltpu.PrefetchScalarGridSpec(num_sc...  42.9 us
    pallas_call x1, Pallas kernels, finish(): pl.pallas_call(finish_kernel, grid_spec=pltpu.PrefetchScalarGridSpec(num_...  20.8 us
    ppermute x8, starting transfers between devices, send(): return lax.ppermute(block, ('gx', 'gy'), pairs)  18.9 us
    all_to_all x1, blocking collectives, summed_over(): return jnp.sum(lax.all_to_all(spread, axis, 0, 0, tiled=True), axis=0)  17.5 us
    mul x1, other arithmetic, on_device(): features.astype(jnp.float32) * occupied_grid.astype(jnp.float32)[..., None]  10.2 us
    pallas_call x1, Pallas kernels, pick(): pl.pallas_call(pick_kernel, grid_spec=pltpu.PrefetchScalarGridSpec(num_sc...  10.1 us
    ppermute x8, waiting for transfers between devices, send(): return lax.ppermute(block, ('gx', 'gy'), pairs)  8.45 us
  transfers between devices with their start and end apart: 11, of which 3 were waited for; matrix products, arithmetic and copies ran while one was open for 11% of the time, Pallas kernels for 9%

profile of v1, /device:TPU:0, one launch (start us, length us, event | category | flops | bytes accessed | tf_op | source)
XLA Modules:
  0.0 233.6 jit_solution(8160525585811072104)
XLA Ops:
  0.0 0.8 compare_convert_fusion
  1.0 1.0 mul.116
  2.1 0.9 multiply_convert_fusion
  3.0 1.6 bitcast_multiply_fusion.3
  4.7 2.9 %collective-permute-start.4 = (bf16[1,1,128,128]{3,2,0,1:T(8,128)(2,1)}, bf16[1,1,128,128]{3,2,0,1:T(8,128)(2,1)S(1)}, u32[]{:S(2)}, u32[]{:S(2)}) collective-permute-start(bf16[1,1,128,128]{3,2,0,1:T(8,128)(2,1)} %get-tuple-element.19), channel_id=1, source_target_pairs={{0,9},{1,10},{2,11},{3,12},{4,13},{5,14},{6,15},{8,17},{9,18},{10,... | collective-permute-start | bytes 98312 | tf_op jit(solution)/shard_map/ppermute | solution.py:247
  7.6 1.3 collective-permute-start.6
  8.8 2.4 %slice_multiply_fusion.2 = (bf16[1,16,128,128]{3,2,1,0:T(8,128)(2,1)}, bf16[1,16,128,128]{3,2,1,0:T(8,128)(2,1)S(1)}) fusion(bf16[16,16,128,128]{3,2,1,0:T(8,128)(2,1)} %param.6, bf16[16,128]{1,0:T(8,128)(2,1)S(1)} %get-tuple-element.35, bf16[16,128]{1,0:T(8,128)(2,1)S(1)} %get-tuple-element.36), kind=kLoop, calls=%fused_computation.8 | loop fusion | flops 524288 | bytes 2105344 | tf_op jit(solution)/shard_map/mul | solution.py:236
  11.2 1.3 collective-permute-start.1
  12.5 7.1 %collective-permute-start = (bf16[1,16,128,128]{3,2,1,0:T(8,128)(2,1)S(1)}, bf16[1,16,128,128]{3,2,1,0:T(8,128)(2,1)S(1)}, u32[]{:S(2)}, u32[]{:S(2)}) collective-permute-start(bf16[1,16,128,128]{3,2,1,0:T(8,128)(2,1)S(1)} %get-tuple-element.26), channel_id=1, source_target_pairs={{0,8},{1,9},{2,10},{3,11},{4,12},{5,13},{6,14},{7,15},{8,16},{9,17... | collective-permute-start | bytes 1572872 | tf_op jit(solution)/shard_map/ppermute | solution.py:247
  19.7 2.5 %slice_multiply_fusion = (bf16[16,1,128,128]{3,2,1,0:T(8,128)(2,1)}, bf16[16,1,128,128]{3,2,1,0:T(8,128)(2,1)}) fusion(bf16[16,16,128,128]{3,2,1,0:T(8,128)(2,1)} %param.6, bf16[16,128]{1,0:T(8,128)(2,1)S(1)} %get-tuple-element.39, bf16[16,128]{1,0:T(8,128)(2,1)S(1)} %get-tuple-element.40), kind=kLoop, calls=%fused_computation.6 | loop fusion | flops 524288 | bytes 2105344 | tf_op jit(solution)/shard_map/mul | solution.py:236
  22.2 1.3 collective-permute-start.3
  23.7 1.8 fusion.2
  25.5 10.2 %convert_multiply_fusion.masked_ref = f32[16,16,128,128]{3,2,1,0:T(8,128)} fusion(bf16[16,16,128,128]{3,2,1,0:T(8,128)(2,1)} %param.6, f32[16,16,128]{2,1,0:T(8,128)S(1)} %get-tuple-element.28), kind=kLoop, calls=%fused_computation | loop fusion | flops 8388608 | bytes 25296896 | tf_op jit(solution)/shard_map/mul | solution.py:292
  35.9 3.1 %collective-permute-start.2 = (bf16[16,1,128,128]{3,2,1,0:T(8,128)(2,1)S(1)}, bf16[16,1,128,128]{3,2,1,0:T(8,128)(2,1)S(1)}, u32[]{:S(2)}, u32[]{:S(2)}) collective-permute-start(bf16[16,1,128,128]{3,2,1,0:T(8,128)(2,1)S(1)} %copy-done.2), channel_id=1, source_target_pairs={{0,1},{1,2},{2,3},{3,4},{4,5},{5,6},{6,7},{8,9},{9,10},{10,11},{11... | collective-permute-start | bytes 1572872 | tf_op jit(solution)/shard_map/ppermute | solution.py:247
  39.6 0.7 select_reduce_fusion
  40.4 1.3 collective-permute-start.7
  42.3 8.4 %collective-permute-done.7 = bf16[1,1,128,128]{3,2,0,1:T(8,128)(2,1)S(1)} collective-permute-done((bf16[1,1,128,128]{3,2,0,1:T(8,128)(2,1)S(1)}, bf16[1,1,128,128]{3,2,0,1:T(8,128)(2,1)S(1)}, u32[]{:S(2)}, u32[]{:S(2)}) %collective-permute-start.7) | collective-permute-done | bytes 32800 | tf_op jit(solution)/shard_map/ppermute | solution.py:247
  50.8 1.5 fusion.3.corner_ref
  52.3 1.1 convert_element_type.52.x_high_ref
  53.3 1.1 convert_element_type.51.x_low_ref
  54.4 1.2 convert_element_type.54.y_high_ref
  55.6 1.1 convert_element_type.53.y_low_ref
  56.7 42.9 %shard_map.64 = (bf16[32,512,128]{2,1,0:T(8,128)(2,1)}, bf16[32,512,128]{2,1,0:T(8,128)(2,1)}, f32[3,8,128]{2,1,0:T(8,128)}) custom-call(s32[32]{0:T(128)} %get-tuple-element.11.place_ref, s32[1]{0:T(128)} %bitcast.1.count_ref, f32[16,16,128,128]{3,2,1,0:T(8,128)} %convert_multiply_fusion.masked_ref, f32[1,16,128,128]{3,2,1,0:T(8,128)} %convert_element_type.51.x_low_ref, ...), custom_call_target="tpu_custom_call" | custom-call | flops 19327352832 | bytes 31457280 | tf_op jit(solution)/shard_map/pallas_call | solution.py:151
  99.6 0.7 reduce_sum.107
  100.4 17.5 %all_to_all.20 = f32[16,8,128]{2,1,0:T(8,128)S(1)} all-to-all(f32[16,8,128]{2,1,0:T(8,128)S(1)} %broadcast_in_dim.45), channel_id=1, replica_groups=mesh['gx'=16,'gy'=8] {'gx'}, dimensions={0} | all-to-all | bytes 131072 | tf_op jit(solution)/shard_map/all_to_all | solution.py:231
  118.5 5.2 %all-to-all-start.2 = ((f32[8,8,128]{2,1,0:T(8,128)}), f32[8,8,128]{2,1,0:T(8,128)S(1)}, u32[]{:S(2)}, u32[]{:S(2)}) async-start(f32[8,8,128]{2,1,0:T(8,128)} %broadcast_in_dim.46), calls=%async_computation.2 | async-start | bytes 65536 | tf_op jit(solution)/shard_map/all_to_all | solution.py:231
  124.4 4.8 %all-to-all-done.2 = f32[8,8,128]{2,1,0:T(8,128)S(1)} async-done(((f32[8,8,128]{2,1,0:T(8,128)}), f32[8,8,128]{2,1,0:T(8,128)S(1)}, u32[]{:S(2)}, u32[]{:S(2)}) %all-to-all-start.2) | async-done | bytes 32800 | tf_op jit(solution)/shard_map/all_to_all | solution.py:231
  129.1 3.4 %all-to-all-start = ((s32[16,1,2]{2,1,0:T(1,128)}), s32[16,1,2]{2,1,0:T(1,128)S(1)}, u32[]{:S(2)}, u32[]{:S(2)}) async-start(s32[16,1,2]{2,1,0:T(1,128)} %bitcast), calls=%async_computation | async-start | bytes 16384 | tf_op jit(solution)/shard_map/all_to_all | solution.py:294
  133.2 20.8 %shard_map.65 = bf16[32,512,128]{2,1,0:T(8,128)(2,1)} custom-call(s32[32]{0:T(128)} %get-tuple-element.12.index_ref, s32[32]{0:T(128)} %get-tuple-element.13.valid_ref, bf16[32,512,128]{2,1,0:T(8,128)(2,1)} %get-tuple-element.8.conv_ref, bf16[32,512,128]{2,1,0:T(8,128)(2,1)} %get-tuple-element.9.centre_ref, f32[8,128]{1,0:T(8,128)} %select_maximum_fusion.norm_ref), custom_call_target="tpu_custom_call" | custom-call | tf_op jit(solution)/shard_map/pallas_call | solution.py:195
  154.0 7.2 %all-to-all-start.3 = ((bf16[16,2,512,128]{3,2,1,0:T(8,128)(2,1)}), bf16[16,2,512,128]{3,2,1,0:T(8,128)(2,1)}, u32[]{:S(2)}, u32[]{:S(2)}) async-start(bf16[16,2,512,128]{3,2,1,0:T(8,128)(2,1)} %bitcast.50), calls=%async_computation.3 | async-start | bytes 8388608 | tf_op jit(solution)/shard_map/all_to_all | solution.py:313
  163.1 60.4 %all-to-all-done.3 = bf16[16,2,512,128]{3,2,1,0:T(8,128)(2,1)} async-done(((bf16[16,2,512,128]{3,2,1,0:T(8,128)(2,1)}), bf16[16,2,512,128]{3,2,1,0:T(8,128)(2,1)}, u32[]{:S(2)}, u32[]{:S(2)}) %all-to-all-start.3) | async-done | bytes 4194336 | tf_op jit(solution)/shard_map/all_to_all | solution.py:313
  223.5 10.1 %shard_map.66 = bf16[16,512,128]{2,1,0:T(8,128)(2,1)} custom-call(s32[16]{0:T(128)} %select_reduce_fusion.3.index_ref, bf16[32,512,128]{2,1,0:T(8,128)(2,1)} %bitcast.17.in_ref), custom_call_target="tpu_custom_call" | custom-call | tf_op jit(solution)/shard_map/pallas_call | solution.py:216
  (49 shorter events, 5.8 us)
Async XLA Ops:
  0.0 23.5 %copy-start.5 = (s32[2,2,16]{2,1,0:T(2,128)S(1)}, s32[2,2,16]{2,1,0:T(2,128)}, u32[]{:S(2)}) copy-start(s32[2,2,16]{2,1,0:T(2,128)} %param.8) | copy-start | bytes 772
  0.0 23.7 %copy-start = (bf16[27,128,128]{2,1,0:T(8,128)(2,1)S(1)}, bf16[27,128,128]{2,1,0:T(8,128)(2,1)}, u32[]{:S(2)}) copy-start(bf16[27,128,128]{2,1,0:T(8,128)(2,1)} %param.9) | copy-start | bytes 2654212
  3.0 32.7 %copy-start.1 = (f32[16,16,128]{2,1,0:T(8,128)}, f32[16,16,128]{2,1,0:T(8,128)S(1)}, u32[]{:S(2)}) copy-start(f32[16,16,128]{2,1,0:T(8,128)S(1)} %get-tuple-element.28) | copy-start | bytes 393220
  4.7 31.2 %collective-permute-start.4 = (bf16[1,1,128,128]{3,2,0,1:T(8,128)(2,1)}, bf16[1,1,128,128]{3,2,0,1:T(8,128)(2,1)S(1)}, u32[]{:S(2)}, u32[]{:S(2)}) collective-permute-start(bf16[1,1,128,128]{3,2,0,1:T(8,128)(2,1)} %get-tuple-element.19), channel_id=1, source_target_pairs={{0,9},{1,10},{2,11},{3,12},{4,13},{5,14},{6,15},{8,17},{9,18},{10,... | collective-permute-start | bytes 98312 | tf_op jit(solution)/shard_map/ppermute | solution.py:247
  7.6 31.4 %collective-permute-start.6 = (bf16[1,1,128,128]{3,2,0,1:T(8,128)(2,1)}, bf16[1,1,128,128]{3,2,0,1:T(8,128)(2,1)}, u32[]{:S(2)}, u32[]{:S(2)}) collective-permute-start(bf16[1,1,128,128]{3,2,0,1:T(8,128)(2,1)} %get-tuple-element.20), channel_id=1, source_target_pairs={{8,1},{9,2},{10,3},{11,4},{12,5},{13,6},{14,7},{16,9},{17,10},{18,... | collective-permute-start | bytes 98312 | tf_op jit(solution)/shard_map/ppermute | solution.py:247
  11.2 41.0 %collective-permute-start.1 = (bf16[1,16,128,128]{3,2,1,0:T(8,128)(2,1)}, bf16[1,16,128,128]{3,2,1,0:T(8,128)(2,1)S(1)}, u32[]{:S(2)}, u32[]{:S(2)}) collective-permute-start(bf16[1,16,128,128]{3,2,1,0:T(8,128)(2,1)} %get-tuple-element.25), channel_id=1, source_target_pairs={{8,0},{9,1},{10,2},{11,3},{12,4},{13,5},{14,6},{15,7},{16,8},{17,9... | collective-permute-start | bytes 1572872 | tf_op jit(solution)/shard_map/ppermute | solution.py:247
  12.5 40.8 %collective-permute-start = (bf16[1,16,128,128]{3,2,1,0:T(8,128)(2,1)S(1)}, bf16[1,16,128,128]{3,2,1,0:T(8,128)(2,1)S(1)}, u32[]{:S(2)}, u32[]{:S(2)}) collective-permute-start(bf16[1,16,128,128]{3,2,1,0:T(8,128)(2,1)S(1)} %get-tuple-element.26), channel_id=1, source_target_pairs={{0,8},{1,9},{2,10},{3,11},{4,12},{5,13},{6,14},{7,15},{8,16},{9,17... | collective-permute-start | bytes 1572872 | tf_op jit(solution)/shard_map/ppermute | solution.py:247
  22.2 32.2 %collective-permute-start.3 = (bf16[16,1,128,128]{3,2,1,0:T(8,128)(2,1)}, bf16[16,1,128,128]{3,2,1,0:T(8,128)(2,1)S(1)}, u32[]{:S(2)}, u32[]{:S(2)}) collective-permute-start(bf16[16,1,128,128]{3,2,1,0:T(8,128)(2,1)} %get-tuple-element.23), channel_id=1, source_target_pairs={{1,0},{2,1},{3,2},{4,3},{5,4},{6,5},{7,6},{9,8},{10,9},{11,10},{12... | collective-permute-start | bytes 1572872 | tf_op jit(solution)/shard_map/ppermute | solution.py:247
  25.5 10.4 %copy-start.2 = (bf16[16,1,128,128]{3,2,1,0:T(8,128)(2,1)S(1)}, bf16[16,1,128,128]{3,2,1,0:T(8,128)(2,1)}, u32[]{:S(2)}) copy-start(bf16[16,1,128,128]{3,2,1,0:T(8,128)(2,1)} %get-tuple-element.24) | copy-start | bytes 1572868
  25.5 13.5 %copy-start.4 = (bf16[1,1,128,128]{3,2,0,1:T(8,128)(2,1)S(1)}, bf16[1,1,128,128]{3,2,0,1:T(8,128)(2,1)}, u32[]{:S(2)}) copy-start(bf16[1,1,128,128]{3,2,0,1:T(8,128)(2,1)} %get-tuple-element.21) | copy-start | bytes 98308
  25.5 14.9 %copy-start.3 = (bf16[1,1,128,128]{3,2,0,1:T(8,128)(2,1)S(1)}, bf16[1,1,128,128]{3,2,0,1:T(8,128)(2,1)}, u32[]{:S(2)}) copy-start(bf16[1,1,128,128]{3,2,0,1:T(8,128)(2,1)} %get-tuple-element.22) | copy-start | bytes 98308
  35.9 19.7 %collective-permute-start.2 = (bf16[16,1,128,128]{3,2,1,0:T(8,128)(2,1)S(1)}, bf16[16,1,128,128]{3,2,1,0:T(8,128)(2,1)S(1)}, u32[]{:S(2)}, u32[]{:S(2)}) collective-permute-start(bf16[16,1,128,128]{3,2,1,0:T(8,128)(2,1)S(1)} %copy-done.2), channel_id=1, source_target_pairs={{0,1},{1,2},{2,3},{3,4},{4,5},{5,6},{6,7},{8,9},{9,10},{10,11},{11... | collective-permute-start | bytes 1572872 | tf_op jit(solution)/shard_map/ppermute | solution.py:247
  39.0 1.4 collective-permute-start.5
  40.4 10.4 %collective-permute-start.7 = (bf16[1,1,128,128]{3,2,0,1:T(8,128)(2,1)S(1)}, bf16[1,1,128,128]{3,2,0,1:T(8,128)(2,1)S(1)}, u32[]{:S(2)}, u32[]{:S(2)}) collective-permute-start(bf16[1,1,128,128]{3,2,0,1:T(8,128)(2,1)S(1)} %copy-done.3), channel_id=1, source_target_pairs={{9,0},{10,1},{11,2},{12,3},{13,4},{14,5},{15,6},{17,8},{18,9},{19,... | collective-permute-start | bytes 98312 | tf_op jit(solution)/shard_map/ppermute | solution.py:247
  56.7 75.9 %copy-start.6 = (f32[128]{0:T(128)S(1)}, f32[128]{0:T(128)}, u32[]{:S(2)}) copy-start(f32[128]{0:T(128)} %param.10) | copy-start | bytes 1540
  56.7 75.9 %copy-start.7 = (f32[128]{0:T(128)S(1)}, f32[128]{0:T(128)}, u32[]{:S(2)}) copy-start(f32[128]{0:T(128)} %param.11) | copy-start | bytes 1540
  118.5 10.6 %all-to-all-start.2 = ((f32[8,8,128]{2,1,0:T(8,128)}), f32[8,8,128]{2,1,0:T(8,128)S(1)}, u32[]{:S(2)}, u32[]{:S(2)}) async-start(f32[8,8,128]{2,1,0:T(8,128)} %broadcast_in_dim.46), calls=%async_computation.2 | async-start | bytes 65536 | tf_op jit(solution)/shard_map/all_to_all | solution.py:231
  129.1 24.8 %all-to-all-start = ((s32[16,1,2]{2,1,0:T(1,128)}), s32[16,1,2]{2,1,0:T(1,128)S(1)}, u32[]{:S(2)}, u32[]{:S(2)}) async-start(s32[16,1,2]{2,1,0:T(1,128)} %bitcast), calls=%async_computation | async-start | bytes 16384 | tf_op jit(solution)/shard_map/all_to_all | solution.py:294
  154.0 69.5 %all-to-all-start.3 = ((bf16[16,2,512,128]{3,2,1,0:T(8,128)(2,1)}), bf16[16,2,512,128]{3,2,1,0:T(8,128)(2,1)}, u32[]{:S(2)}, u32[]{:S(2)}) async-start(bf16[16,2,512,128]{3,2,1,0:T(8,128)(2,1)} %bitcast.50), calls=%async_computation.3 | async-start | bytes 8388608 | tf_op jit(solution)/shard_map/all_to_all | solution.py:313

commit v2 on v1

v2 whole, which is shorter than its diff:
```python
import functools

import jax
import jax.numpy as jnp
from jax import lax
from jax.experimental import pallas as pl
from jax.experimental.pallas import tpu as pltpu
from jax.sharding import PartitionSpec as P

O = 16
E = 8
C = 128
GROUP = 4
ABSENT = -1e30
EPSILON = 1e-05
MIB = 1 << 20


def shifted_scratch():
    return pltpu.VMEM((2, 3, 2, GROUP, 5, 5, 16, C), jnp.bfloat16)


def conv_kernel(
    place_ref,
    count_ref,
    masked_ref,
    y_low_ref,
    y_high_ref,
    occupied_ref,
    weight_ref,
    conv_ref,
    centre_ref,
    face_ref,
    sums_ref,
    padded,
    shifted_a,
    shifted_b,
    total_a,
    total_b,
    sems,
):
    step = pl.program_id(0)
    count, early, steps = count_ref[0], count_ref[1], count_ref[2]
    halves = [
        pltpu.make_async_copy(
            masked_ref.at[lo:hi], padded.at[1 + lo : 1 + hi, 1:17, 8:136, :], sems.at[i]
        )
        for i, (lo, hi) in enumerate(((0, 9), (9, 16)))
    ]
    row = lax.broadcasted_iota(jnp.int32, (E, C), 0)
    lane = lax.broadcasted_iota(jnp.int32, (E, C), 1)

    def place_of(k):
        place = place_ref[k]
        return place // 32, place // 16 % 2, place % 16

    def prepare(group, shifted):
        for b in range(GROUP):
            bx, by, bz = place_of(group * GROUP + b)
            for dz in range(3):
                for xx in range(10):
                    lines = [
                        padded[bx * E + xx, by * E + yy, pl.ds(bz * E + 7 + dz, E), :]
                        for yy in range(10)
                    ]
                    for parity in range(2):
                        for yp in range(5 - parity):
                            pair = jnp.concatenate(
                                [lines[2 * yp + parity], lines[2 * yp + parity + 1]], axis=0
                            )
                            shifted[parity, dz, xx % 2, b, xx // 2, yp] = pair.astype(jnp.bfloat16)

    def multiply(shifted, total):
        for dy in range(3):
            parity, first = dy % 2, dy // 2
            parts = []
            for dz in range(3):
                for j in range(4):
                    part = shifted[
                        parity, dz, j % 2, :, j // 2 : j // 2 + 4, first : first + 4, :, :
                    ]
                    parts.append(part.reshape(GROUP * 256, C))
            product = jnp.dot(
                jnp.concatenate(parts, axis=1),
                weight_ref[dy],
                preferred_element_type=jnp.float32,
            )
            if dy == 0:
                total[...] = product
            else:
                total[...] += product

    def emit(group, shifted, total, at):
        ones = jnp.ones((C, C), jnp.bfloat16)
        summed = jnp.zeros((E, C), jnp.float32)
        squared = jnp.zeros((E, C), jnp.float32)
        counted = jnp.zeros((E, C), jnp.float32)
        for b in range(GROUP):
            k = group * GROUP + b
            bx, by, bz = place_of(k)
            valid = jnp.where(k < count, 1.0, 0.0)
            eye = jnp.where(lane == bz * E + row, valid, 0.0)
            for x in range(E):
                lines = occupied_ref[pl.ds((bx * E + x) * 16 + by * E, E), :]
                spread = (lines[:, None, :] * eye[None, :, :]).reshape(E * E, C)
                live = jnp.dot(
                    spread.astype(jnp.bfloat16), ones, preferred_element_type=jnp.float32
                )
                block = total[b * 256 + (x // 2) * 64 : b * 256 + (x // 2) * 64 + 64,
                              (x % 2) * C : (x % 2 + 1) * C]
                value = (block * live).astype(jnp.bfloat16)
                wide = value.astype(jnp.float32)
                kept = wide
                if x == 0:
                    kept = wide * jnp.where(bx == 0, 0.0, 1.0)
                    face_low = block
                if x == E - 1:
                    kept = wide * jnp.where(bx == 0, 1.0, 0.0)
                    face_ref[at + b] = jnp.where(bx == 0, face_low, block)
                summed += jnp.sum(kept.reshape(E, E, C), axis=0)
                squared += jnp.sum((kept * kept).reshape(E, E, C), axis=0)
                counted += jnp.sum(live.reshape(E, E, C), axis=0)
                conv_ref[at + b, x * 64 : (x + 1) * 64, :] = jnp.where(
                    live > 0.5, wide, ABSENT
                ).astype(jnp.bfloat16)
                centre_ref[at + b, x * 64 : (x + 1) * 64, :] = shifted[
                    1, 1, (x + 1) % 2, b, (x + 1) // 2, 0:4
                ].reshape(64, C)
        sums_ref[0] += summed
        sums_ref[1] += squared
        sums_ref[2] += counted

    @pl.when(step == 0)
    def _():
        for half in halves:
            half.start()
        edge = jnp.zeros((18, 18, E, C), jnp.float32)
        padded[:, :, 0:8, :] = edge
        padded[:, :, 136:144, :] = edge
        side = jnp.zeros((18, 128, C), jnp.float32)
        padded[0, :, 8:136, :] = side
        padded[17, :, 8:136, :] = side
        padded[1:17, 0, 8:136, :] = y_low_ref[...].reshape(16, 128, C).astype(jnp.float32)
        padded[1:17, 17, 8:136, :] = y_high_ref[...].reshape(16, 128, C).astype(jnp.float32)
        sums_ref[...] = jnp.zeros_like(sums_ref)
        halves[0].wait()

    @pl.when(((step == 0) & (early < 3 * GROUP)) | ((step == 1) & (early >= 3 * GROUP)))
    def _():
        halves[1].wait()

    @pl.when((step == 0) & (steps > 0))
    def _():
        prepare(0, shifted_a)

    @pl.when((step > 0) & (step <= steps))
    def _():
        emit(2 * step - 1, shifted_b, total_b, 0)

    @pl.when(step < steps)
    def _():
        prepare(2 * step + 1, shifted_b)
        multiply(shifted_a, total_a)
        multiply(shifted_b, total_b)
        emit(2 * step, shifted_a, total_a, GROUP)
        prepare(2 * step + 2, shifted_a)


def convolve(places, count, masked, y_low, y_high, occupied, weight):
    any_spec = pl.BlockSpec(memory_space=pl.ANY)
    whole = pl.BlockSpec(memory_space=pltpu.VMEM)

    def block(i, places, count):
        return (jnp.minimum(i, count[2]), 0, 0)

    rows = 2 * GROUP * (16 // GROUP + 1)
    return pl.pallas_call(
        conv_kernel,
        grid_spec=pltpu.PrefetchScalarGridSpec(
            num_scalar_prefetch=2,
            grid=(16 // GROUP + 1,),
            in_specs=[any_spec, whole, whole, whole, whole],
            out_specs=[
                pl.BlockSpec((2 * GROUP, 512, C), block),
                pl.BlockSpec((2 * GROUP, 512, C), block),
                pl.BlockSpec((2 * GROUP, 64, C), block),
                pl.BlockSpec((3, E, C), lambda i, *_: (0, 0, 0)),
            ],
            scratch_shapes=[
                pltpu.VMEM((18, 18, 144, C), jnp.float32),
                shifted_scratch(),
                shifted_scratch(),
                pltpu.VMEM((GROUP * 256, 2 * C), jnp.float32),
                pltpu.VMEM((GROUP * 256, 2 * C), jnp.float32),
                pltpu.SemaphoreType.DMA((2,)),
            ],
        ),
        out_shape=[
            jax.ShapeDtypeStruct((rows, 512, C), jnp.bfloat16),
            jax.ShapeDtypeStruct((rows, 512, C), jnp.bfloat16),
            jax.ShapeDtypeStruct((rows, 64, C), jnp.float32),
            jax.ShapeDtypeStruct((3, E, C), jnp.float32),
        ],
        compiler_params=pltpu.CompilerParams(vmem_limit_bytes=56 * MIB),
        cost_estimate=pl.CostEstimate(
            flops=2 * 32 * 256 * 4608 * 256, bytes_accessed=30 * MIB, transcendentals=0
        ),
    )(places, count, masked, y_low, y_high, occupied, weight)


def face_kernel(
    place_ref,
    count_ref,
    x_low_ref,
    x_high_ref,
    partial_ref,
    sums_ref,
    occupied_ref,
    weight_ref,
    out_ref,
    norm_ref,
    padded,
    shifted,
    added,
):
    count = count_ref[0]
    row = lax.broadcasted_iota(jnp.int32, (E, C), 0)
    lane = lax.broadcasted_iota(jnp.int32, (E, C), 1)
    ones = jnp.ones((C, C), jnp.bfloat16)
    padded[:, 0:8, :] = jnp.zeros((18, E, C), jnp.float32)
    padded[:, 136:144, :] = jnp.zeros((18, E, C), jnp.float32)
    for side, ref in enumerate((x_low_ref, x_high_ref)):
        padded[:, 8:136, :] = ref[0].astype(jnp.float32)
        for dz in range(3):
            shifted[dz] = padded[:, 7 + dz : 135 + dz, :].astype(jnp.bfloat16).reshape(
                9, 2, 128, C
            )
        parts = []
        for dz in range(3):
            for j in range(4):
                parts.append(shifted[dz, j // 2 : j // 2 + 8, j % 2].reshape(1024, C))
        added[side] = jnp.dot(
            jnp.concatenate(parts, axis=1), weight_ref[side], preferred_element_type=jnp.float32
        )

    def one(k, carry):
        summed, squared = carry
        place = place_ref[k]
        bx, by, bz = place // 32, place // 16 % 2, place % 16
        eye = jnp.where(lane == bz * E + row, 1.0, 0.0)
        lines = occupied_ref[pl.ds(bx * 240 + by * E, E), :]
        spread = (lines[:, None, :] * eye[None, :, :]).reshape(E * E, C)
        live = jnp.dot(spread.astype(jnp.bfloat16), ones, preferred_element_type=jnp.float32)
        pieces = []
        for y in range(E):
            start = pl.multiple_of((by * 4 + y // 2) * 128 + bz * E, E)
            pieces.append(added[bx, pl.ds(start, E), (y % 2) * C : (y % 2 + 1) * C])
        block = partial_ref[k + GROUP] + jnp.concatenate(pieces, axis=0)
        wide = (block * live).astype(jnp.bfloat16).astype(jnp.float32)
        out_ref[k] = jnp.where(live > 0.5, wide, ABSENT).astype(jnp.bfloat16)
        summed += jnp.sum(wide.reshape(E, E, C), axis=0)
        squared += jnp.sum((wide * wide).reshape(E, E, C), axis=0)
        return summed, squared

    summed, squared = lax.fori_loop(0, count, one, (sums_ref[0], sums_ref[1]))
    table = jnp.concatenate(
        [
            jnp.sum(summed, axis=0, keepdims=True),
            jnp.sum(squared, axis=0, keepdims=True),
            jnp.sum(sums_ref[2], axis=0, keepdims=True),
            jnp.zeros((5, C), jnp.float32),
        ],
        axis=0,
    )
    norm_ref[...] = jnp.broadcast_to(table[None], norm_ref.shape)


def correct_faces(places, count, x_low, x_high, partial, sums, occupied, weight):
    whole = pl.BlockSpec(memory_space=pltpu.VMEM)
    scalars = pl.BlockSpec(memory_space=pltpu.SMEM)
    return pl.pallas_call(
        face_kernel,
        in_specs=[scalars, scalars] + [whole] * 6,
        out_specs=[whole, whole],
        out_shape=[
            jax.ShapeDtypeStruct((32, 64, C), jnp.bfloat16),
            jax.ShapeDtypeStruct((16, E, C), jnp.float32),
        ],
        scratch_shapes=[
            pltpu.VMEM((18, 144, C), jnp.float32),
            pltpu.VMEM((3, 9, 2, 128, C), jnp.bfloat16),
            pltpu.VMEM((2, 1024, 2 * C), jnp.float32),
        ],
        compiler_params=pltpu.CompilerParams(vmem_limit_bytes=32 * MIB),
    )(places, count, x_low, x_high, partial, sums, occupied, weight)


def finish_kernel(
    slot_ref,
    place_ref,
    count_ref,
    conv_ref,
    centre_ref,
    face_ref,
    sums_ref,
    gain_ref,
    bias_ref,
    out_ref,
    buffer,
    sems,
):
    step = pl.program_id(0)
    count = count_ref[0]

    def copy(k, half, b):
        return pltpu.make_async_copy(
            buffer.at[half, b], out_ref.at[slot_ref[k]], sems.at[half, b]
        )

    def drain(at):
        for b in range(GROUP):
            k = at * GROUP + b

            @pl.when((at >= 0) & (k < count))
            def _():
                copy(k, at % 2, b).wait()

    drain(step - 2)

    @pl.when(step * GROUP < count)
    def _():
        sums = jnp.sum(sums_ref[...], axis=0)
        mean = sums[0:1] / sums[2:3]
        variance = sums[1:2] / sums[2:3] - mean * mean
        factor = gain_ref[...] / jnp.sqrt(variance + EPSILON)
        bias = bias_ref[...]
        for b in range(GROUP):
            k = step * GROUP + b

            @pl.when(k < count)
            def _():
                bx = place_ref[k] // 32
                for x in range(E):
                    conv = conv_ref[b, x * 64 : (x + 1) * 64, :].astype(jnp.float32)
                    if x in (0, E - 1):
                        own = face_ref[b].astype(jnp.float32)
                        conv = jnp.where(bx == (0 if x == 0 else 1), own, conv)
                    scaled = factor * (conv - mean) + bias
                    silu = scaled * (0.5 + 0.5 * jnp.tanh(0.5 * scaled))
                    silu = jnp.where(conv > 0.5 * ABSENT, silu, 0.0)
                    centre = centre_ref[b, x * 64 : (x + 1) * 64, :].astype(jnp.float32)
                    buffer[step % 2, b, x * 64 : (x + 1) * 64, :] = (centre + silu).astype(
                        jnp.bfloat16
                    )
                copy(k, step % 2, b).start()

    @pl.when(step == pl.num_programs(0) - 1)
    def _():
        drain(step - 1)
        drain(step)


def finish(slots, places, count, conv, centre, face, sums, gain, bias):
    whole = pl.BlockSpec(memory_space=pltpu.VMEM)

    def last(i, count):
        return jnp.minimum(i, jnp.maximum((count[0] - 1) // GROUP, 0))

    def shifted_block(i, slots, places, count):
        return (last(i, count) + 1, 0, 0)

    def block(i, slots, places, count):
        return (last(i, count), 0, 0)

    return pl.pallas_call(
        finish_kernel,
        grid_spec=pltpu.PrefetchScalarGridSpec(
            num_scalar_prefetch=3,
            grid=(32 // GROUP,),
            in_specs=[
                pl.BlockSpec((GROUP, 512, C), shifted_block),
                pl.BlockSpec((GROUP, 512, C), shifted_block),
                pl.BlockSpec((GROUP, 64, C), block),
                whole,
                whole,
                whole,
            ],
            out_specs=pl.BlockSpec(memory_space=pl.ANY),
            scratch_shapes=[
                pltpu.VMEM((2, GROUP, 512, C), jnp.bfloat16),
                pltpu.SemaphoreType.DMA((2, GROUP)),
            ],
        ),
        out_shape=jax.ShapeDtypeStruct((32, 512, C), jnp.bfloat16),
        compiler_params=pltpu.CompilerParams(vmem_limit_bytes=24 * MIB),
    )(slots, places, count, conv, centre, face, sums, gain, bias)


def pick_kernel(index_ref, in_ref, out_ref, buffer, sems):
    reads = [
        pltpu.make_async_copy(in_ref.at[index_ref[i]], buffer.at[i], sems.at[0, i])
        for i in range(O)
    ]
    writes = [
        pltpu.make_async_copy(buffer.at[i], out_ref.at[i], sems.at[1, i]) for i in range(O)
    ]
    for read in reads:
        read.start()
    for read, write in zip(reads, writes):
        read.wait()
        write.start()
    for write in writes:
        write.wait()


def pick(index, received):
    return pl.pallas_call(
        pick_kernel,
        in_specs=[pl.BlockSpec(memory_space=pltpu.SMEM), pl.BlockSpec(memory_space=pl.ANY)],
        out_specs=pl.BlockSpec(memory_space=pl.ANY),
        scratch_shapes=[
            pltpu.VMEM((O, 512, C), jnp.bfloat16),
            pltpu.SemaphoreType.DMA((2, O)),
        ],
        out_shape=jax.ShapeDtypeStruct((O, 512, C), jnp.bfloat16),
    )(index, received)


def swap(spread, axis):
    return lax.all_to_all(spread, axis, 0, 0, tiled=True)


def neighbours(low_block, high_block, axis):
    count = lax.axis_size(axis)
    up = [(i, i + 1) for i in range(count - 1)]
    down = [(j, i) for i, j in up]
    return lax.ppermute(high_block, axis, up), lax.ppermute(low_block, axis, down)


def routes(owner_map):
    flat = owner_map.reshape(-1)
    index = jnp.arange(flat.shape[0], dtype=jnp.int32)
    active = flat >= 0
    owner = jnp.where(active, flat // O, -1)
    earlier = (index[None, :] < index[:, None]) & active[None, :]
    rank = jnp.sum(earlier.astype(jnp.int32), axis=1)
    pair_rank = jnp.sum((earlier & (owner[None, :] == owner[:, None])).astype(jnp.int32), axis=1)
    slot = jnp.where(active, owner * 2 + pair_rank, -1)
    slots = jnp.arange(32, dtype=jnp.int32)
    here = slot[None, :] == slots[:, None]
    sent = jnp.sum(jnp.where(here, (flat % O)[None, :] + 1, 0), axis=1) - 1
    order = jnp.arange(48, dtype=jnp.int32)
    ordered = active[None, :] & (rank[None, :] == order[:, None])
    places = jnp.sum(jnp.where(ordered, index[None, :], 0), axis=1)
    slot_of = jnp.sum(jnp.where(ordered, slot[None, :], 0), axis=1)
    count = jnp.sum(active.astype(jnp.int32))
    early = jnp.sum(active[:32].astype(jnp.int32))
    counts = jnp.stack([count, early, (count + 2 * GROUP - 1) // (2 * GROUP)])
    return places, slot_of, counts, sent


def pair_weights(taps):
    blank = jnp.zeros((1,) + taps.shape[1:], taps.dtype)
    return jnp.concatenate(
        [jnp.concatenate([taps, blank]), jnp.concatenate([blank, taps])], axis=-1
    )


def on_device(features, occupancy, owner_map, kernel, norm_gain, norm_bias):
    active = (owner_map >= 0).astype(jnp.int32)
    occupied_grid = (
        occupancy.reshape(2, E, 2, E, 16, E) * active[:, None, :, None, :, None]
    ).reshape(occupancy.shape)
    occupied = occupied_grid.astype(jnp.bfloat16)

    def face(x, y):
        return features[x, y] * occupied[x, y][..., None]

    every, first, last = slice(None), slice(0, 1), slice(15, 16)
    y_low, y_high = neighbours(face(every, first), face(every, last), "gy")
    masked = features.astype(jnp.float32) * occupied_grid.astype(jnp.float32)[..., None]
    places, slot_of, counts, sent = routes(owner_map)
    received_slots = lax.all_to_all(
        sent.reshape(16, 1, 2), "gx", split_axis=0, concat_axis=0, tiled=True
    ).reshape(32)
    owned = jnp.arange(O, dtype=jnp.int32)
    source = jnp.sum(
        jnp.where(
            received_slots[None, :] == owned[:, None], jnp.arange(32, dtype=jnp.int32)[None, :], 0
        ),
        axis=1,
    )
    taps = kernel.reshape(3, 3, 3, C, C)
    weight = pair_weights(taps).transpose(1, 2, 0, 3, 4).reshape(3, 12 * C, 2 * C)
    face_weight = jnp.stack(
        [pair_weights(taps[a]).transpose(1, 0, 2, 3).reshape(12 * C, 2 * C) for a in (0, 2)]
    )
    lines = occupied_grid.astype(jnp.float32).reshape(256, 128)
    x_low, x_high = neighbours(
        jnp.concatenate([y_low[0:1], face(first, every), y_high[0:1]], axis=1),
        jnp.concatenate([y_low[15:16], face(last, every), y_high[15:16]], axis=1),
        "gx",
    )
    places, source = lax.optimization_barrier((places, source))
    conv, centre, partial, sums = convolve(places, counts, masked, y_low, y_high, lines, weight)
    face_conv, spread = correct_faces(
        places, counts, x_low, x_high, partial, sums, lines, face_weight
    )
    partly = jnp.sum(swap(spread, "gx"), axis=0)
    totals = swap(jnp.broadcast_to(partly[None], (8, E, C)), "gy")
    result = finish(
        slot_of,
        places,
        counts,
        conv,
        centre,
        face_conv,
        totals,
        norm_gain.reshape(1, C),
        norm_bias.reshape(1, C),
    )
    received = swap(result.reshape(16, 2, 512, C), "gx").reshape(32, 512, C)
    return pick(source, received).reshape(O, 1, 512, C)


def solution(mesh):
    in_specs = (P("gx", "gy", None, None), P("gx", "gy", None), P("gx", "gy", None), P(), P(), P())
    out_specs = P("gx", "gy", None, None)
    return jax.shard_map(
        on_device, mesh=mesh, in_specs=in_specs, out_specs=out_specs, check_vma=False
    )
```

time: 235 us -> 189 us (0.80)
  blocking collectives: 17.5 us -> 110 us
  waiting for transfers between devices: 73.6 us -> 0.01 us
  Pallas kernels: 73.8 us -> 25.2 us
  starting transfers between devices: 34.6 us -> 16.7 us
  local copies, waits for them, and re-layouts: 3.36 us -> 12.1 us
  other arithmetic: 30.4 us -> 22.9 us
    all_to_all x1 -> x3, blocking collectives: 17.5 us -> 110 us  [swap(): return lax.all_to_all(spread, axis, 0, 0, tiled=True)]
    all_to_all x2 -> x0, waiting for transfers between devices: 65.2 us -> none  [the longest x1 60.4 us: on_device(): lax.all_to_all(result.reshape(16, 2, 512, C), 'gx', split_axis=0, concat_...]
    pallas_call x1, Pallas kernels: 42.9 us -> 17.3 us  [convolve(): pl.pallas_call(conv_kernel, grid_spec=pltpu.PrefetchScalarGridSpec(num_sc...]
    pallas_call x1, Pallas kernels: 20.8 us -> 1.61 us  [finish(): pl.pallas_call(finish_kernel, grid_spec=pltpu.PrefetchScalarGridSpec(num_...]
    all_to_all x2 -> x0, starting transfers between devices: 12.4 us -> none  [the longest x1 7.2 us: on_device(): lax.all_to_all(result.reshape(16, 2, 512, C), 'gx', split_axis=0, concat_...]
    ppermute x8 -> x4, starting transfers between devices: 18.9 us -> 8.76 us  [the longest x2 6 us: neighbours(): lax.ppermute(high_block, axis, up)]
    ppermute x8 -> x4, waiting for transfers between devices: 8.45 us -> 0.01 us  [the longest x2 0.01 us: neighbours(): lax.ppermute(high_block, axis, up)]
    unnamed x17 -> x27, local copies, waits for them, and re-layouts: 0.03 us -> 7.04 us
  transfers between devices with their start and end apart: 11 -> 5, of which waited for: 3 -> 0; matrix products, arithmetic and copies ran while one was open for 11% -> 13% of each run, Pallas kernels for 9% -> 9%
where the time goes in v2:
time: 189 us; the launch traced here: 188 us
  blocking collectives  110 us (58%)
  Pallas kernels  25.2 us (13%)
  other arithmetic  22.9 us (12%)
  starting transfers between devices  16.7 us (9%)
  local copies, waits for them, and re-layouts  12.1 us (6%)
    all_to_all x3, blocking collectives, swap(): return lax.all_to_all(spread, axis, 0, 0, tiled=True)  110 us
    pallas_call x1, Pallas kernels, convolve(): pl.pallas_call(conv_kernel, grid_spec=pltpu.PrefetchScalarGridSpec(num_sc...  17.3 us
    mul x1, other arithmetic, on_device(): features.astype(jnp.float32) * occupied_grid.astype(jnp.float32)[..., None]  10.2 us
    all_to_all x1, starting transfers between devices, on_device(): lax.all_to_all(sent.reshape(16, 1, 2), 'gx', split_axis=0, concat_axis=0,...  7.96 us
    unnamed x27, local copies, waits for them, and re-layouts  7.04 us
    ppermute x2, starting transfers between devices, neighbours(): lax.ppermute(high_block, axis, up)  6 us
    mul x2, other arithmetic, face(): return features[x, y] * occupied[x, y][..., None]  4.18 us
  transfers between devices with their start and end apart: 5, of which 0 were waited for; matrix products, arithmetic and copies ran while one was open for 13% of the time, Pallas kernels for 9%

profile of v2, /device:TPU:0, one launch (start us, length us, event | category | flops | bytes accessed | tf_op | source)
XLA Modules:
  0.0 188.2 jit_solution(771419895267923174)
XLA Ops:
  0.0 0.8 reshape.172
  1.2 0.7 sub.21
  1.8 8.0 %all-to-all-start = ((s32[16,1,2]{2,1,0:T(1,128)}), s32[16,1,2]{2,1,0:T(1,128)S(1)}, u32[]{:S(2)}, u32[]{:S(2)}) async-start(s32[16,1,2]{2,1,0:T(1,128)} %bitcast), calls=%async_computation | async-start | bytes 16384 | tf_op jit(solution)/shard_map/all_to_all | solution.py:483
  9.8 0.7 compare_convert_fusion
  10.8 1.0 mul.72
  11.9 2.4 %slice_multiply_fusion.2 = (bf16[16,1,128,128]{3,2,1,0:T(8,128)(2,1)}, bf16[16,1,128,128]{3,2,1,0:T(8,128)(2,1)S(1)}) fusion(bf16[16,16,128,128]{3,2,1,0:T(8,128)(2,1)} %param.6, bf16[16,128]{1,0:T(8,128)(2,1)S(1)} %get-tuple-element.43, bf16[16,128]{1,0:T(8,128)(2,1)S(1)} %get-tuple-element.44), kind=kLoop, calls=%fused_computation.19 | loop fusion | flops 524288 | bytes 2105344 | tf_op jit(solution)/shard_map/mul | solution.py:477
  14.3 2.3 %collective-permute-start = (bf16[16,1,128,128]{3,2,1,0:T(8,128)(2,1)S(1)}, bf16[16,1,128,128]{3,2,1,0:T(8,128)(2,1)}, u32[]{:S(2)}, u32[]{:S(2)}) collective-permute-start(bf16[16,1,128,128]{3,2,1,0:T(8,128)(2,1)S(1)} %get-tuple-element.28), channel_id=1, source_target_pairs={{0,1},{1,2},{2,3},{3,4},{4,5},{5,6},{6,7},{8,9},{9,10},{10,11},{11... | collective-permute-start | bytes 1572872 | tf_op jit(solution)/shard_map/ppermute | solution.py:437
  16.6 1.3 collective-permute-start.1
  17.9 10.2 %convert_multiply_fusion.masked_ref = f32[16,16,128,128]{3,2,1,0:T(8,128)} fusion(bf16[16,16,128,128]{3,2,1,0:T(8,128)(2,1)} %param.6, f32[16,16,128]{2,1,0:T(8,128)S(1)} %get-tuple-element.36), kind=kLoop, calls=%fused_computation | loop fusion | flops 8388608 | bytes 25296896 | tf_op jit(solution)/shard_map/mul | solution.py:481
  28.2 1.8 fusion.2
  30.1 1.7 slice_multiply_fusion
  32.0 0.7 fusion.15
  33.3 0.7 select_reduce_fusion
  34.0 0.7 fusion.13
  34.7 1.9 pad_add_fusion.count_ref
  37.1 0.6 reduce.4
  37.9 0.7 select_reduce_fusion.3.index_ref
  38.6 0.8 fusion.18
  39.4 0.8 fusion.17
  40.2 3.7 %collective-permute-start.2 = (bf16[1,18,128,128]{3,2,1,0:T(8,128)(2,1)S(1)}, bf16[1,18,128,128]{3,2,1,0:T(8,128)(2,1)S(1)}, u32[]{:S(2)}, u32[]{:S(2)}) collective-permute-start(bf16[1,18,128,128]{3,2,1,0:T(8,128)(2,1)S(1)} %pad_maximum_fusion.1), channel_id=1, source_target_pairs={{0,8},{8,16},{16,24},{24,32},{32,40},{40,48},{48,56},{56,64},{64,7... | collective-permute-start | bytes 1769480 | tf_op jit(solution)/shard_map/ppermute | solution.py:437
  44.0 1.5 collective-permute-start.3
  45.5 17.3 %shard_map.64 = (bf16[40,512,128]{2,1,0:T(8,128)(2,1)}, bf16[40,512,128]{2,1,0:T(8,128)(2,1)}, f32[40,64,128]{2,1,0:T(8,128)}, f32[3,8,128]{2,1,0:T(8,128)}) custom-call(s32[48]{0:T(128)} %get-tuple-element.14.place_ref, s32[3]{0:T(128)} %pad_add_fusion.count_ref, f32[16,16,128,128]{3,2,1,0:T(8,128)} %convert_multiply_fusion.masked_ref, ...), custom_call_target="tpu_custom_call" | custom-call | flops 19327352832 | bytes 31457280 | tf_op jit(solution)/shard_map/pallas_call | solution.py:177
  62.9 1.3 copy-done.2
  64.2 0.7 copy-done.5
  64.9 3.1 %shard_map.65 = (bf16[32,64,128]{2,1,0:T(8,128)(2,1)S(1)}, f32[16,8,128]{2,1,0:T(8,128)S(1)}) custom-call(s32[48]{0:T(128)S(1)} %copy-done.6, s32[3]{0:T(128)S(1)} %copy-done.7, bf16[1,18,128,128]{3,2,1,0:T(8,128)(2,1)S(1)} %collective-permute-done.2.x_low_ref, bf16[1,18,128,128]{3,2,1,0:T(8,128)(2,1)S(1)} %collective-permute-done.3.x_high_ref, ...), custom_call_target="tpu_custom_call" | custom-call | tf_op jit(solution)/shard_map/pallas_call | solution.py:281
  68.0 36.1 %all_to_all.20 = f32[16,8,128]{2,1,0:T(8,128)S(1)} all-to-all(f32[16,8,128]{2,1,0:T(8,128)S(1)} %get-tuple-element.20), channel_id=1, replica_groups=mesh['gx'=16,'gy'=8] {'gx'}, dimensions={0} | all-to-all | bytes 131072 | tf_op jit(solution)/shard_map/all_to_all | solution.py:430
  104.1 11.5 %all_to_all.21.sums_ref = f32[8,8,128]{2,1,0:T(8,128)S(1)} all-to-all(f32[8,8,128]{2,1,0:T(8,128)S(1)} %broadcast_in_dim.80), channel_id=1, replica_groups=mesh['gx'=16,'gy'=8] {'gy'}, dimensions={0} | all-to-all | bytes 65536 | tf_op jit(solution)/shard_map/all_to_all | solution.py:430
  115.7 2.5 %copy-done = bf16[40,512,128]{2,1,0:T(8,128)(2,1)S(1)} copy-done((bf16[40,512,128]{2,1,0:T(8,128)(2,1)S(1)}, bf16[40,512,128]{2,1,0:T(8,128)(2,1)}, u32[]{:S(2)}) %copy-start) | copy-done | bytes 5242904
  118.2 2.5 %copy-done.1 = bf16[40,512,128]{2,1,0:T(8,128)(2,1)S(1)} copy-done((bf16[40,512,128]{2,1,0:T(8,128)(2,1)S(1)}, bf16[40,512,128]{2,1,0:T(8,128)(2,1)}, u32[]{:S(2)}) %copy-start.1) | copy-done | bytes 5242904
  120.7 1.6 shard_map.66
  122.3 62.5 %all_to_all.22 = bf16[16,2,512,128]{3,2,1,0:T(8,128)(2,1)} all-to-all(bf16[16,2,512,128]{3,2,1,0:T(8,128)(2,1)S(1)} %bitcast.34), channel_id=1, replica_groups=mesh['gx'=16,'gy'=8] {'gx'}, dimensions={0} | all-to-all | bytes 8388608 | tf_op jit(solution)/shard_map/all_to_all | solution.py:430
  184.8 3.2 %shard_map.67 = bf16[16,512,128]{2,1,0:T(8,128)(2,1)} custom-call(s32[16]{0:T(128)} %select_reduce_fusion.3.index_ref, bf16[32,512,128]{2,1,0:T(8,128)(2,1)} %bitcast.39), custom_call_target="tpu_custom_call" | custom-call | tf_op jit(solution)/shard_map/pallas_call | solution.py:417
  (48 shorter events, 1.8 us)
Async XLA Ops:
  0.0 11.8 %copy-start.11 = (s32[16,16,128]{2,1,0:T(8,128)S(1)}, s32[16,16,128]{2,1,0:T(8,128)}, u32[]{:S(2)}) copy-start(s32[16,16,128]{2,1,0:T(8,128)} %param.7) | copy-start | bytes 393220
  1.8 34.8 %all-to-all-start = ((s32[16,1,2]{2,1,0:T(1,128)}), s32[16,1,2]{2,1,0:T(1,128)S(1)}, u32[]{:S(2)}, u32[]{:S(2)}) async-start(s32[16,1,2]{2,1,0:T(1,128)} %bitcast), calls=%async_computation | async-start | bytes 16384 | tf_op jit(solution)/shard_map/all_to_all | solution.py:483
  11.8 16.3 %copy-start.3 = (f32[16,16,128]{2,1,0:T(8,128)}, f32[16,16,128]{2,1,0:T(8,128)S(1)}, u32[]{:S(2)}) copy-start(f32[16,16,128]{2,1,0:T(8,128)S(1)} %get-tuple-element.36) | copy-start | bytes 393220
  14.3 25.0 %collective-permute-start = (bf16[16,1,128,128]{3,2,1,0:T(8,128)(2,1)S(1)}, bf16[16,1,128,128]{3,2,1,0:T(8,128)(2,1)}, u32[]{:S(2)}, u32[]{:S(2)}) collective-permute-start(bf16[16,1,128,128]{3,2,1,0:T(8,128)(2,1)S(1)} %get-tuple-element.28), channel_id=1, source_target_pairs={{0,1},{1,2},{2,3},{3,4},{4,5},{5,6},{6,7},{8,9},{9,10},{10,11},{11... | collective-permute-start | bytes 1572872 | tf_op jit(solution)/shard_map/ppermute | solution.py:437
  16.6 21.9 %collective-permute-start.1 = (bf16[16,1,128,128]{3,2,1,0:T(8,128)(2,1)}, bf16[16,1,128,128]{3,2,1,0:T(8,128)(2,1)}, u32[]{:S(2)}, u32[]{:S(2)}) collective-permute-start(bf16[16,1,128,128]{3,2,1,0:T(8,128)(2,1)} %get-tuple-element.27), channel_id=1, source_target_pairs={{1,0},{2,1},{3,2},{4,3},{5,4},{6,5},{7,6},{9,8},{10,9},{11,10},{12... | collective-permute-start | bytes 1572872 | tf_op jit(solution)/shard_map/ppermute | solution.py:437
  17.9 10.2 %copy-start.10 = (bf16[27,128,128]{2,1,0:T(8,128)(2,1)S(1)}, bf16[27,128,128]{2,1,0:T(8,128)(2,1)}, u32[]{:S(2)}) copy-start(bf16[27,128,128]{2,1,0:T(8,128)(2,1)} %param.9) | copy-start | bytes 2654212
  30.1 1.9 %copy-start.12 = (s32[2,2,16]{2,1,0:T(2,128)S(1)}, s32[2,2,16]{2,1,0:T(2,128)}, u32[]{:S(2)}) copy-start(s32[2,2,16]{2,1,0:T(2,128)} %param.8) | copy-start | bytes 772
  40.2 22.6 %collective-permute-start.2 = (bf16[1,18,128,128]{3,2,1,0:T(8,128)(2,1)S(1)}, bf16[1,18,128,128]{3,2,1,0:T(8,128)(2,1)S(1)}, u32[]{:S(2)}, u32[]{:S(2)}) collective-permute-start(bf16[1,18,128,128]{3,2,1,0:T(8,128)(2,1)S(1)} %pad_maximum_fusion.1), channel_id=1, source_target_pairs={{0,8},{8,16},{16,24},{24,32},{32,40},{40,48},{48,56},{56,64},{64,7... | collective-permute-start | bytes 1769480 | tf_op jit(solution)/shard_map/ppermute | solution.py:437
  44.0 18.9 %collective-permute-start.3 = (bf16[1,18,128,128]{3,2,1,0:T(8,128)(2,1)S(1)}, bf16[1,18,128,128]{3,2,1,0:T(8,128)(2,1)S(1)}, u32[]{:S(2)}, u32[]{:S(2)}) collective-permute-start(bf16[1,18,128,128]{3,2,1,0:T(8,128)(2,1)S(1)} %pad_maximum_fusion.2), channel_id=1, source_target_pairs={{8,0},{16,8},{24,16},{32,24},{40,32},{48,40},{56,48},{64,56},{72,6... | collective-permute-start | bytes 1769480 | tf_op jit(solution)/shard_map/ppermute | solution.py:437
  45.5 17.4 %copy-start.4 = (f32[16,16,128]{2,1,0:T(8,128)S(1)}, f32[16,16,128]{2,1,0:T(8,128)}, u32[]{:S(2)}) copy-start(f32[16,16,128]{2,1,0:T(8,128)} %copy-done.3) | copy-start | bytes 393220
  45.5 17.4 %copy-start.6 = (s32[48]{0:T(128)S(1)}, s32[48]{0:T(128)}, u32[]{:S(2)}) copy-start(s32[48]{0:T(128)} %get-tuple-element.14.place_ref) | copy-start | bytes 580
  45.5 17.4 %copy-start.7 = (s32[3]{0:T(128)S(1)}, s32[3]{0:T(128)}, u32[]{:S(2)}) copy-start(s32[3]{0:T(128)} %pad_add_fusion.count_ref) | copy-start | bytes 40
  62.8 52.9 %copy-start.8 = (f32[128]{0:T(128)S(1)}, f32[128]{0:T(128)}, u32[]{:S(2)}) copy-start(f32[128]{0:T(128)} %param.10) | copy-start | bytes 1540
  62.8 52.9 %copy-start.9 = (f32[128]{0:T(128)S(1)}, f32[128]{0:T(128)}, u32[]{:S(2)}) copy-start(f32[128]{0:T(128)} %param.11) | copy-start | bytes 1540
  62.9 1.3 copy-start.2
  64.2 0.7 copy-start.5
  115.7 2.5 %copy-start = (bf16[40,512,128]{2,1,0:T(8,128)(2,1)S(1)}, bf16[40,512,128]{2,1,0:T(8,128)(2,1)}, u32[]{:S(2)}) copy-start(bf16[40,512,128]{2,1,0:T(8,128)(2,1)} %get-tuple-element.15.conv_ref) | copy-start | bytes 15728644
  118.2 2.5 %copy-start.1 = (bf16[40,512,128]{2,1,0:T(8,128)(2,1)S(1)}, bf16[40,512,128]{2,1,0:T(8,128)(2,1)}, u32[]{:S(2)}) copy-start(bf16[40,512,128]{2,1,0:T(8,128)(2,1)} %get-tuple-element.16.centre_ref) | copy-start | bytes 15728644

commit v3 on v2

--- a/solution.py
+++ b/solution.py
@@ -16,6 +16,20 @@
 MIB = 1 << 20
 
 
+def pair_taps(weight_ref, taps_ref, index):
+    blank = jnp.zeros((C, C), jnp.bfloat16)
+    for a in range(weight_ref.shape[0]):
+        for dz in range(3):
+            for j in range(4):
+                at = (dz * 4 + j) * C
+                weight_ref[a, at : at + C, 0:C] = (
+                    taps_ref[index(a, dz, j)] if j < 3 else blank
+                )
+                weight_ref[a, at : at + C, C : 2 * C] = (
+                    taps_ref[index(a, dz, j - 1)] if j > 0 else blank
+                )
+
+
 def shifted_scratch():
     return pltpu.VMEM((2, 3, 2, GROUP, 5, 5, 16, C), jnp.bfloat16)
 
@@ -23,16 +37,20 @@
 def conv_kernel(
     place_ref,
     count_ref,
-    masked_ref,
+    features_ref,
     y_low_ref,
     y_high_ref,
+    taps_hbm,
     occupied_ref,
-    weight_ref,
     conv_ref,
     centre_ref,
     face_ref,
     sums_ref,
     padded,
+    raw,
+    margins,
+    taps_ref,
+    weight_ref,
     shifted_a,
     shifted_b,
     total_a,
@@ -40,12 +58,12 @@
     sems,
 ):
     step = pl.program_id(0)
-    count, early, steps = count_ref[0], count_ref[1], count_ref[2]
-    halves = [
+    count, steps = count_ref[0], count_ref[1]
+    chunks = [
         pltpu.make_async_copy(
-            masked_ref.at[lo:hi], padded.at[1 + lo : 1 + hi, 1:17, 8:136, :], sems.at[i]
+            features_ref.at[4 * i : 4 * i + 4], raw.at[i % 2], sems.at[i]
         )
-        for i, (lo, hi) in enumerate(((0, 9), (9, 16)))
+        for i in range(4)
     ]
     row = lax.broadcasted_iota(jnp.int32, (E, C), 0)
     lane = lax.broadcasted_iota(jnp.int32, (E, C), 1)
@@ -132,22 +150,43 @@
 
     @pl.when(step == 0)
     def _():
-        for half in halves:
-            half.start()
+        extra = [
+            pltpu.make_async_copy(y_low_ref, margins.at[0], sems.at[4]),
+            pltpu.make_async_copy(y_high_ref, margins.at[1], sems.at[5]),
+            pltpu.make_async_copy(taps_hbm, taps_ref, sems.at[6]),
+        ]
+        for copy in [chunks[0], chunks[1]] + extra:
+            copy.start()
         edge = jnp.zeros((18, 18, E, C), jnp.float32)
         padded[:, :, 0:8, :] = edge
         padded[:, :, 136:144, :] = edge
         side = jnp.zeros((18, 128, C), jnp.float32)
         padded[0, :, 8:136, :] = side
         padded[17, :, 8:136, :] = side
-        padded[1:17, 0, 8:136, :] = y_low_ref[...].reshape(16, 128, C).astype(jnp.float32)
-        padded[1:17, 17, 8:136, :] = y_high_ref[...].reshape(16, 128, C).astype(jnp.float32)
         sums_ref[...] = jnp.zeros_like(sums_ref)
-        halves[0].wait()
-
-    @pl.when(((step == 0) & (early < 3 * GROUP)) | ((step == 1) & (early >= 3 * GROUP)))
-    def _():
-        halves[1].wait()
+        for i in range(4):
+            chunks[i].wait()
+            columns = jnp.transpose(occupied_ref[i // 2 * 128 : i // 2 * 128 + 128, :])
+
+            def mask_plane(j, carry, i=i, columns=columns):
+                near = pltpu.roll(columns, 128 - 64 * (i % 2) - 16 * j, axis=1)
+                for y in range(16):
+                    live = jnp.broadcast_to(near[:, y : y + 1], (128, C))
+                    padded[1 + 4 * i + j, 1 + y, 8:136, :] = (
+                        raw[i % 2, j, y].astype(jnp.float32) * live
+                    )
+                return carry
+
+            lax.fori_loop(0, 4, mask_plane, 0)
+            if i < 2:
+                chunks[i + 2].start()
+        for copy in extra:
+            copy.wait()
+        for side in range(2):
+            padded[1:17, 17 * side, 8:136, :] = (
+                margins[side].reshape(16, 128, C).astype(jnp.float32)
+            )
+        pair_taps(weight_ref, taps_ref, lambda dy, dz, dx: 9 * dx + 3 * dy + dz)
 
     @pl.when((step == 0) & (steps > 0))
     def _():
@@ -166,12 +205,12 @@
         prepare(2 * step + 2, shifted_a)
 
 
-def convolve(places, count, masked, y_low, y_high, occupied, weight):
+def convolve(places, count, features, y_low, y_high, occupied, taps):
     any_spec = pl.BlockSpec(memory_space=pl.ANY)
     whole = pl.BlockSpec(memory_space=pltpu.VMEM)
 
     def block(i, places, count):
-        return (jnp.minimum(i, count[2]), 0, 0)
+        return (jnp.minimum(i, count[1]), 0, 0)
 
     rows = 2 * GROUP * (16 // GROUP + 1)
     return pl.pallas_call(
@@ -179,7 +218,7 @@
         grid_spec=pltpu.PrefetchScalarGridSpec(
             num_scalar_prefetch=2,
             grid=(16 // GROUP + 1,),
-            in_specs=[any_spec, whole, whole, whole, whole],
+            in_specs=[any_spec, any_spec, any_spec, any_spec, whole],
             out_specs=[
                 pl.BlockSpec((2 * GROUP, 512, C), block),
                 pl.BlockSpec((2 * GROUP, 512, C), block),
@@ -188,11 +227,15 @@
             ],
             scratch_shapes=[
                 pltpu.VMEM((18, 18, 144, C), jnp.float32),
+                pltpu.VMEM((2, 4, 16, 128, C), jnp.bfloat16),
+                pltpu.VMEM((2, 16, 1, 128, C), jnp.bfloat16),
+                pltpu.VMEM((27, C, C), jnp.bfloat16),
+                pltpu.VMEM((3, 12 * C, 2 * C), jnp.bfloat16),
                 shifted_scratch(),
                 shifted_scratch(),
                 pltpu.VMEM((GROUP * 256, 2 * C), jnp.float32),
                 pltpu.VMEM((GROUP * 256, 2 * C), jnp.float32),
-                pltpu.SemaphoreType.DMA((2,)),
+                pltpu.SemaphoreType.DMA((7,)),
             ],
         ),
         out_shape=[
@@ -205,7 +248,7 @@
         cost_estimate=pl.CostEstimate(
             flops=2 * 32 * 256 * 4608 * 256, bytes_accessed=30 * MIB, transcendentals=0
         ),
-    )(places, count, masked, y_low, y_high, occupied, weight)
+    )(places, count, features, y_low, y_high, taps, occupied)
 
 
 def face_kernel(
@@ -216,14 +259,17 @@
     partial_ref,
     sums_ref,
     occupied_ref,
-    weight_ref,
+    taps_ref,
+    slots_ref,
     out_ref,
     norm_ref,
     padded,
     shifted,
     added,
+    weight_ref,
 ):
     count = count_ref[0]
+    pair_taps(weight_ref, taps_ref, lambda side, dz, dy: 18 * side + 3 * dy + dz)
     row = lax.broadcasted_iota(jnp.int32, (E, C), 0)
     lane = lax.broadcasted_iota(jnp.int32, (E, C), 1)
     ones = jnp.ones((C, C), jnp.bfloat16)
@@ -273,14 +319,18 @@
         axis=0,
     )
     norm_ref[...] = jnp.broadcast_to(table[None], norm_ref.shape)
-
-
-def correct_faces(places, count, x_low, x_high, partial, sums, occupied, weight):
+    wide_lane = lax.broadcasted_iota(jnp.int32, (1, C), 1)
+    for i in range(16):
+        pair = jnp.where(wide_lane == 0, slots_ref[2 * i], slots_ref[2 * i + 1])
+        norm_ref[i, 3:4, :] = pair.astype(jnp.float32)
+
+
+def correct_faces(places, count, x_low, x_high, partial, sums, occupied, taps, sent):
     whole = pl.BlockSpec(memory_space=pltpu.VMEM)
     scalars = pl.BlockSpec(memory_space=pltpu.SMEM)
     return pl.pallas_call(
         face_kernel,
-        in_specs=[scalars, scalars] + [whole] * 6,
+        in_specs=[scalars, scalars] + [whole] * 6 + [scalars],
         out_specs=[whole, whole],
         out_shape=[
             jax.ShapeDtypeStruct((32, 64, C), jnp.bfloat16),
@@ -290,9 +340,10 @@
             pltpu.VMEM((18, 144, C), jnp.float32),
             pltpu.VMEM((3, 9, 2, 128, C), jnp.bfloat16),
             pltpu.VMEM((2, 1024, 2 * C), jnp.float32),
+            pltpu.VMEM((2, 12 * C, 2 * C), jnp.bfloat16),
         ],
         compiler_params=pltpu.CompilerParams(vmem_limit_bytes=32 * MIB),
-    )(places, count, x_low, x_high, partial, sums, occupied, weight)
+    )(places, count, x_low, x_high, partial, sums, occupied, taps, sent)
 
 
 def finish_kernel(
@@ -392,7 +443,7 @@
             ],
         ),
         out_shape=jax.ShapeDtypeStruct((32, 512, C), jnp.bfloat16),
-        compiler_params=pltpu.CompilerParams(vmem_limit_bytes=24 * MIB),
+        compiler_params=pltpu.CompilerParams(vmem_limit_bytes=56 * MIB),
     )(slots, places, count, conv, centre, face, sums, gain, bias)
 
 
@@ -437,77 +488,153 @@
     return lax.ppermute(high_block, axis, up), lax.ppermute(low_block, axis, down)
 
 
-def routes(owner_map):
-    flat = owner_map.reshape(-1)
-    index = jnp.arange(flat.shape[0], dtype=jnp.int32)
-    active = flat >= 0
-    owner = jnp.where(active, flat // O, -1)
-    earlier = (index[None, :] < index[:, None]) & active[None, :]
-    rank = jnp.sum(earlier.astype(jnp.int32), axis=1)
-    pair_rank = jnp.sum((earlier & (owner[None, :] == owner[:, None])).astype(jnp.int32), axis=1)
-    slot = jnp.where(active, owner * 2 + pair_rank, -1)
-    slots = jnp.arange(32, dtype=jnp.int32)
-    here = slot[None, :] == slots[:, None]
-    sent = jnp.sum(jnp.where(here, (flat % O)[None, :] + 1, 0), axis=1) - 1
-    order = jnp.arange(48, dtype=jnp.int32)
-    ordered = active[None, :] & (rank[None, :] == order[:, None])
-    places = jnp.sum(jnp.where(ordered, index[None, :], 0), axis=1)
-    slot_of = jnp.sum(jnp.where(ordered, slot[None, :], 0), axis=1)
-    count = jnp.sum(active.astype(jnp.int32))
-    early = jnp.sum(active[:32].astype(jnp.int32))
-    counts = jnp.stack([count, early, (count + 2 * GROUP - 1) // (2 * GROUP)])
-    return places, slot_of, counts, sent
-
-
-def pair_weights(taps):
-    blank = jnp.zeros((1,) + taps.shape[1:], taps.dtype)
-    return jnp.concatenate(
-        [jnp.concatenate([taps, blank]), jnp.concatenate([blank, taps])], axis=-1
+def edges_kernel(
+    owner_ref,
+    active_ref,
+    occupancy_ref,
+    features_ref,
+    lines_ref,
+    x_first_ref,
+    x_last_ref,
+    y_first_ref,
+    y_last_ref,
+    ends_first_ref,
+    ends_last_ref,
+    place_ref,
+    slot_ref,
+    count_ref,
+    sent_ref,
+    raw,
+    met,
+    sems,
+):
+    copies = [
+        pltpu.make_async_copy(features_ref.at[0], raw.at[0], sems.at[0]),
+        pltpu.make_async_copy(features_ref.at[15], raw.at[1], sems.at[1]),
+        pltpu.make_async_copy(features_ref.at[:, 0], raw.at[2], sems.at[2]),
+        pltpu.make_async_copy(features_ref.at[:, 15], raw.at[3], sems.at[3]),
+    ]
+    for copy in copies:
+        copy.start()
+
+    for i in range(17):
+        met[i] = 0
+    for i in range(32):
+        sent_ref[i] = -1
+    for i in range(48):
+        place_ref[i] = 0
+        slot_ref[i] = 0
+
+    def route(i, carry):
+        owned = owner_ref[i // 32, i // 16 % 2, i % 16]
+
+        @pl.when(owned >= 0)
+        def _():
+            owner = owned // 16
+            slot = 2 * owner + met[owner]
+            rank = met[16]
+            met[owner] = met[owner] + 1
+            met[16] = rank + 1
+            place_ref[rank] = i
+            slot_ref[rank] = slot
+            sent_ref[slot] = owned % 16
+
+        return carry
+
+    lax.fori_loop(0, 64, route, 0)
+    count_ref[0] = met[16]
+    count_ref[1] = (met[16] + 2 * GROUP - 1) // (2 * GROUP)
+
+    repeat = jnp.where(
+        lax.broadcasted_iota(jnp.int32, (16, C), 1) // E
+        == lax.broadcasted_iota(jnp.int32, (16, C), 0),
+        1.0,
+        0.0,
+    ).astype(jnp.bfloat16)
+    for bx in range(2):
+        spread = jnp.dot(
+            jnp.where(active_ref[bx] >= 0, 1.0, 0.0).astype(jnp.bfloat16),
+            repeat,
+            preferred_element_type=jnp.float32,
+        )
+        for x in range(bx * E, bx * E + E):
+            for by in range(2):
+                at = x * 16 + by * E
+                lines_ref[at : at + E, :] = (
+                    occupancy_ref[at : at + E, :].astype(jnp.float32) * spread[by : by + 1, :]
+                )
+    columns = [jnp.transpose(lines_ref[128 * i : 128 * i + 128, :]) for i in range(2)]
+
+    def masked(source, at, x, y):
+        column = x % E * 16 + y
+        live = jnp.broadcast_to(columns[x // E][:, column : column + 1], (128, C))
+        return (raw[source, at].astype(jnp.float32) * live).astype(jnp.bfloat16)
+
+    for source, ref, ends, y in ((2, y_first_ref, ends_first_ref, 0), (3, y_last_ref, ends_last_ref, 15)):
+        copies[source].wait()
+        for x in range(16):
+            line = masked(source, x, x, y)
+            ref[x, 0] = line
+            if x in (0, 15):
+                ends[x // 15, 0] = line
+    for source, ref, x in ((0, x_first_ref, 0), (1, x_last_ref, 15)):
+        copies[source].wait()
+        for y in range(16):
+            ref[0, y] = masked(source, y, x, y)
+
+
+def find_edges(owner_map, occupancy, features):
+    whole = pl.BlockSpec(memory_space=pltpu.VMEM)
+    scalars = pl.BlockSpec(memory_space=pltpu.SMEM)
+    blocks = [(1, 16), (1, 16), (16, 1), (16, 1), (2, 1), (2, 1)]
+    return pl.pallas_call(
+        edges_kernel,
+        in_specs=[scalars, whole, whole, pl.BlockSpec(memory_space=pl.ANY)],
+        out_specs=[whole] * 7 + [scalars] * 4,
+        out_shape=[jax.ShapeDtypeStruct((256, 128), jnp.float32)]
+        + [jax.ShapeDtypeStruct(block + (128, C), jnp.bfloat16) for block in blocks]
+        + [jax.ShapeDtypeStruct((n,), jnp.int32) for n in (48, 48, 2, 32)],
+        scratch_shapes=[
+            pltpu.VMEM((4, 16, 128, C), jnp.bfloat16),
+            pltpu.SMEM((17,), jnp.int32),
+            pltpu.SemaphoreType.DMA((4,)),
+        ],
+        compiler_params=pltpu.CompilerParams(vmem_limit_bytes=56 * MIB),
+    )(owner_map, owner_map, occupancy, features)
+
+
+def widen_kernel(first_ref, last_ref, low_ref, high_ref, first_out, last_out):
+    for i, (ref, out) in enumerate(((first_ref, first_out), (last_ref, last_out))):
+        out[0, 0:1] = low_ref[i]
+        out[0, 1:17] = ref[0]
+        out[0, 17:18] = high_ref[i]
+
+
+def widen(first, last, low, high):
+    whole = pl.BlockSpec(memory_space=pltpu.VMEM)
+    return pl.pallas_call(
+        widen_kernel,
+        in_specs=[whole] * 4,
+        out_specs=[whole] * 2,
+        out_shape=[jax.ShapeDtypeStruct((1, 18, 128, C), jnp.bfloat16)] * 2,
+        compiler_params=pltpu.CompilerParams(vmem_limit_bytes=16 * MIB),
+    )(first, last, low, high)
+
+
+def on_device(features, occupancy, owner_map, kernel, norm_gain, norm_bias):
+    lines, x_first, x_last, y_first, y_last, ends_first, ends_last, *routes = find_edges(
+        owner_map, occupancy.reshape(256, 128), features
     )
-
-
-def on_device(features, occupancy, owner_map, kernel, norm_gain, norm_bias):
-    active = (owner_map >= 0).astype(jnp.int32)
-    occupied_grid = (
-        occupancy.reshape(2, E, 2, E, 16, E) * active[:, None, :, None, :, None]
-    ).reshape(occupancy.shape)
-    occupied = occupied_grid.astype(jnp.bfloat16)
-
-    def face(x, y):
-        return features[x, y] * occupied[x, y][..., None]
-
-    every, first, last = slice(None), slice(0, 1), slice(15, 16)
-    y_low, y_high = neighbours(face(every, first), face(every, last), "gy")
-    masked = features.astype(jnp.float32) * occupied_grid.astype(jnp.float32)[..., None]
-    places, slot_of, counts, sent = routes(owner_map)
-    received_slots = lax.all_to_all(
-        sent.reshape(16, 1, 2), "gx", split_axis=0, concat_axis=0, tiled=True
-    ).reshape(32)
-    owned = jnp.arange(O, dtype=jnp.int32)
-    source = jnp.sum(
-        jnp.where(
-            received_slots[None, :] == owned[:, None], jnp.arange(32, dtype=jnp.int32)[None, :], 0
-        ),
-        axis=1,
+    places, slot_of, counts, sent = routes
+    line_low, line_high = neighbours(ends_first, ends_last, "gy")
+    y_low, y_high = neighbours(y_first, y_last, "gy")
+    x_low, x_high = neighbours(*widen(x_first, x_last, line_low, line_high), "gx")
+    conv, centre, partial, sums = convolve(places, counts, features, y_low, y_high, lines, kernel)
+    face_conv, spread = correct_faces(
+        places, counts, x_low, x_high, partial, sums, lines, kernel, sent
     )
-    taps = kernel.reshape(3, 3, 3, C, C)
-    weight = pair_weights(taps).transpose(1, 2, 0, 3, 4).reshape(3, 12 * C, 2 * C)
-    face_weight = jnp.stack(
-        [pair_weights(taps[a]).transpose(1, 0, 2, 3).reshape(12 * C, 2 * C) for a in (0, 2)]
-    )
-    lines = occupied_grid.astype(jnp.float32).reshape(256, 128)
-    x_low, x_high = neighbours(
-        jnp.concatenate([y_low[0:1], face(first, every), y_high[0:1]], axis=1),
-        jnp.concatenate([y_low[15:16], face(last, every), y_high[15:16]], axis=1),
-        "gx",
-    )
-    places, source = lax.optimization_barrier((places, source))
-    conv, centre, partial, sums = convolve(places, counts, masked, y_low, y_high, lines, weight)
-    face_conv, spread = correct_faces(
-        places, counts, x_low, x_high, partial, sums, lines, face_weight
-    )
-    partly = jnp.sum(swap(spread, "gx"), axis=0)
-    totals = swap(jnp.broadcast_to(partly[None], (8, E, C)), "gy")
+    arrived = swap(spread, "gx")
+    totals = swap(jnp.broadcast_to(jnp.sum(arrived, axis=0)[None], (8, E, C)), "gy")
     result = finish(
         slot_of,
         places,
@@ -520,6 +647,12 @@
         norm_bias.reshape(1, C),
     )
     received = swap(result.reshape(16, 2, 512, C), "gx").reshape(32, 512, C)
+    named = arrived[:, 3, 0:2].reshape(32).astype(jnp.int32)
+    owned = jnp.arange(O, dtype=jnp.int32)
+    source = jnp.sum(
+        jnp.where(named[None, :] == owned[:, None], jnp.arange(32, dtype=jnp.int32)[None, :], 0),
+        axis=1,
+    )
     return pick(source, received).reshape(O, 1, 512, C)
 
 

time: 189 us -> 182 us (0.963)
  blocking collectives: 110 us -> 27.4 us
  waiting for transfers between devices: 0.01 us -> 62.5 us
  Pallas kernels: 25.2 us -> 64.6 us
  other arithmetic: 22.9 us -> 0.69 us
  local copies, waits for them, and re-layouts: 12.1 us -> 5.95 us
    all_to_all x3 -> x2, blocking collectives: 110 us -> 27.4 us  [swap(): return lax.all_to_all(spread, axis, 0, 0, tiled=True)]
    all_to_all x1, waiting for transfers between devices: 0.01 us -> 59.2 us  [swap(): return lax.all_to_all(spread, axis, 0, 0, tiled=True)]
    pallas_call x1, Pallas kernels: 17.3 us -> 38.2 us  [convolve(): pl.pallas_call(conv_kernel, grid_spec=pltpu.PrefetchScalarGridSpec(num_sc...]
    mul x3 -> x0, other arithmetic: 14.4 us -> none  [the longest x1 10.2 us: on_device(): features.astype(jnp.float32) * occupied_grid.astype(jnp.float32)[..., None]]
    pallas_call x1 -> x3, Pallas kernels: 3.1 us -> 13.6 us  [the longest x1 7.86 us: correct_faces(): pl.pallas_call(face_kernel, in_specs=[scalars, scalars] + [whole] * 6 + [...]
    pallas_call x1, Pallas kernels: 1.61 us -> 9.57 us  [finish(): pl.pallas_call(finish_kernel, grid_spec=pltpu.PrefetchScalarGridSpec(num_...]
    ppermute x2 -> x3, starting transfers between devices: 6 us -> 9.65 us  [neighbours(): lax.ppermute(high_block, axis, up)]
    all_to_all x1, starting transfers between devices: 7.96 us -> 4.55 us  [swap(): return lax.all_to_all(spread, axis, 0, 0, tiled=True)]
  transfers between devices with their start and end apart: 5 -> 7, of which waited for: 0 -> 2; matrix products, arithmetic and copies ran while one was open for 13% -> 0% of each run, Pallas kernels for 9% -> 21%
where the time goes in v3:
time: 182 us; the launch traced here: 179 us
  Pallas kernels  64.6 us (35%)
  waiting for transfers between devices  62.5 us (34%)
  blocking collectives  27.4 us (15%)
  starting transfers between devices  18.1 us (10%)
  local copies, waits for them, and re-layouts  5.95 us (3%)
    all_to_all x1, waiting for transfers between devices, swap(): return lax.all_to_all(spread, axis, 0, 0, tiled=True)  59.2 us
    pallas_call x1, Pallas kernels, convolve(): pl.pallas_call(conv_kernel, grid_spec=pltpu.PrefetchScalarGridSpec(num_sc...  38.2 us
    all_to_all x2, blocking collectives, swap(): return lax.all_to_all(spread, axis, 0, 0, tiled=True)  27.4 us
    ppermute x3, starting transfers between devices, neighbours(): lax.ppermute(high_block, axis, up)  9.65 us
    pallas_call x1, Pallas kernels, finish(): pl.pallas_call(finish_kernel, grid_spec=pltpu.PrefetchScalarGridSpec(num_...  9.57 us
    pallas_call x1, Pallas kernels, correct_faces(): pl.pallas_call(face_kernel, in_specs=[scalars, scalars] + [whole] * 6 + [...  7.86 us
    unnamed x24, local copies, waits for them, and re-layouts  5.86 us
    pallas_call x1, Pallas kernels, find_edges(): pl.pallas_call(edges_kernel, in_specs=[scalars, whole, whole, pl.BlockSpe...  5.69 us
  transfers between devices with their start and end apart: 7, of which 2 were waited for; matrix products, arithmetic and copies ran while one was open for 0% of the time, Pallas kernels for 21%

profile of v3, /device:TPU:0, one launch (start us, length us, event | category | flops | bytes accessed | tf_op | source)
XLA Modules:
  0.0 179.5 jit_solution(15819210743510115229)
XLA Ops:
  0.0 5.7 %shard_map.64 = (f32[256,128]{1,0:T(8,128)}, bf16[1,16,128,128]{3,2,1,0:T(8,128)(2,1)}, bf16[1,16,128,128]{3,2,1,0:T(8,128)(2,1)}, bf16[16,1,128,128]{3,2,1,0:T(...) custom-call(s32[2,2,16]{2,1,0:T(2,128)} %active_ref.1, ...), custom_call_target="tpu_custom_call" | custom-call | tf_op jit(solution)/shard_map/pallas_call | solution.py:590
  5.7 1.3 collective-permute-start.4
  7.0 1.3 collective-permute-start.5
  8.3 4.9 %collective-permute-start = (bf16[2,1,128,128]{3,2,1,0:T(8,128)(2,1)}, bf16[2,1,128,128]{3,2,1,0:T(8,128)(2,1)S(1)}, u32[]{:S(2)}, u32[]{:S(2)}) collective-permute-start(bf16[2,1,128,128]{3,2,1,0:T(8,128)(2,1)} %get-tuple-element.28), channel_id=1, source_target_pairs={{0,1},{1,2},{2,3},{3,4},{4,5},{5,6},{6,7},{8,9},{9,10},{10,11},{11... | collective-permute-start | bytes 196616 | tf_op jit(solution)/shard_map/ppermute | solution.py:488
  13.2 1.3 collective-permute-start.1
  14.5 0.0 collective-permute-done.low_ref
  14.5 3.3 %collective-permute-done.1.high_ref = bf16[2,1,128,128]{3,2,1,0:T(8,128)(2,1)S(1)} collective-permute-done((bf16[2,1,128,128]{3,2,1,0:T(8,128)(2,1)}, bf16[2,1,128,128]{3,2,1,0:T(8,128)(2,1)S(1)}, u32[]{:S(2)}, u32[]{:S(2)}) %collective-permute-start.1) | collective-permute-done | bytes 65568 | tf_op jit(solution)/shard_map/ppermute | solution.py:488
  17.8 1.0 copy-done.3
  18.9 1.0 copy-done.4
  19.9 0.1 shard_map.65
  20.0 3.4 %collective-permute-start.2 = (bf16[1,18,128,128]{3,2,1,0:T(8,128)(2,1)S(1)}, bf16[1,18,128,128]{3,2,1,0:T(8,128)(2,1)S(1)}, u32[]{:S(2)}, u32[]{:S(2)}) collective-permute-start(bf16[1,18,128,128]{3,2,1,0:T(8,128)(2,1)S(1)} %get-tuple-element.30), channel_id=1, source_target_pairs={{0,8},{8,16},{16,24},{24,32},{32,40},{40,48},{48,56},{56,64},{64,7... | collective-permute-start | bytes 1769480 | tf_op jit(solution)/shard_map/ppermute | solution.py:488
  23.4 1.3 collective-permute-start.3
  24.7 0.0 collective-permute-done.4.y_low_ref
  24.8 0.0 collective-permute-done.5.y_high_ref
  24.8 0.8 copy-done.10
  25.5 0.2 copy-done.11
  25.7 38.2 %shard_map.66 = (bf16[40,512,128]{2,1,0:T(8,128)(2,1)}, bf16[40,512,128]{2,1,0:T(8,128)(2,1)}, f32[40,64,128]{2,1,0:T(8,128)}, f32[3,8,128]{2,1,0:T(8,128)}) custom-call(s32[48]{0:T(128)} %get-tuple-element.24.place_ref, s32[2]{0:T(128)} %get-tuple-element.25.count_ref, bf16[16,16,128,128]{3,2,1,0:T(8,128)(2,1)} %features_ref.3, ...), custom_call_target="tpu_custom_call" | custom-call | flops 19327352832 | bytes 31457280 | tf_op jit(solution)/shard_map/pallas_call | solution.py:216
  63.9 0.0 collective-permute-done.3.x_high_ref
  64.0 0.0 copy-start
  64.0 1.3 copy-done
  65.3 0.7 copy-done.6
  66.0 7.9 %shard_map.67 = (bf16[32,64,128]{2,1,0:T(8,128)(2,1)S(1)}, f32[16,8,128]{2,1,0:T(8,128)S(1)}) custom-call(s32[48]{0:T(128)S(1)} %copy-done.7, s32[2]{0:T(128)S(1)} %copy-done.8, bf16[1,18,128,128]{3,2,1,0:T(8,128)(2,1)S(1)} %collective-permute-done.2.x_low_ref, bf16[1,18,128,128]{3,2,1,0:T(8,128)(2,1)S(1)} %collective-permute-done.3.x_high_ref, ...), custom_call_target="tpu_custom_call" | custom-call | tf_op jit(solution)/shard_map/pallas_call | solution.py:331
  73.9 0.0 copy-start.2
  73.9 0.8 copy-done.2
  74.7 15.6 %all_to_all.15 = f32[16,8,128]{2,1,0:T(8,128)S(1)} all-to-all(f32[16,8,128]{2,1,0:T(8,128)S(1)} %get-tuple-element.38), channel_id=1, replica_groups=mesh['gx'=16,'gy'=8] {'gx'}, dimensions={0} | all-to-all | bytes 131072 | tf_op jit(solution)/shard_map/all_to_all | solution.py:481
  90.3 11.8 %all_to_all.16.sums_ref = f32[8,8,128]{2,1,0:T(8,128)} all-to-all(f32[8,8,128]{2,1,0:T(8,128)S(1)} %broadcast_in_dim.23), channel_id=1, replica_groups=mesh['gx'=16,'gy'=8] {'gy'}, dimensions={0} | all-to-all | bytes 65536 | tf_op jit(solution)/shard_map/all_to_all | solution.py:481
  102.1 9.6 %shard_map.68 = bf16[32,512,128]{2,1,0:T(8,128)(2,1)} custom-call(s32[48]{0:T(128)} %get-tuple-element.39.slot_ref, s32[48]{0:T(128)} %get-tuple-element.24.place_ref, s32[2]{0:T(128)} %get-tuple-element.25.count_ref, bf16[40,512,128]{2,1,0:T(8,128)(2,1)} %get-tuple-element.40.conv_ref, bf16[40,512,128]{2,1,0:T(8,128)(2,1)} %get-tuple-element.41.centre_ref, ...), custom_call_target="tpu_custom_call" | custom-call | tf_op jit(solution)/shard_map/pallas_call | solution.py:426
  111.7 4.6 %all-to-all-start.2 = ((bf16[16,2,512,128]{3,2,1,0:T(8,128)(2,1)}), bf16[16,2,512,128]{3,2,1,0:T(8,128)(2,1)}, u32[]{:S(2)}, u32[]{:S(2)}) async-start(bf16[16,2,512,128]{3,2,1,0:T(8,128)(2,1)} %bitcast.8), calls=%async_computation.2 | async-start | bytes 8388608 | tf_op jit(solution)/shard_map/all_to_all | solution.py:481
  116.3 0.1 convert_element_type.11
  116.3 0.6 select_reduce_fusion.index_ref
  117.0 59.2 %all-to-all-done.2 = bf16[16,2,512,128]{3,2,1,0:T(8,128)(2,1)} async-done(((bf16[16,2,512,128]{3,2,1,0:T(8,128)(2,1)}), bf16[16,2,512,128]{3,2,1,0:T(8,128)(2,1)}, u32[]{:S(2)}, u32[]{:S(2)}) %all-to-all-start.2) | async-done | bytes 4194336 | tf_op jit(solution)/shard_map/all_to_all | solution.py:481
  176.2 3.2 %shard_map.69 = bf16[16,512,128]{2,1,0:T(8,128)(2,1)} custom-call(s32[16]{0:T(128)} %select_reduce_fusion.index_ref, bf16[32,512,128]{2,1,0:T(8,128)(2,1)} %bitcast.4.in_ref), custom_call_target="tpu_custom_call" | custom-call | tf_op jit(solution)/shard_map/pallas_call | solution.py:468
  (19 shorter events, 0.1 us)
Async XLA Ops:
  5.7 19.0 %collective-permute-start.4 = (bf16[16,1,128,128]{3,2,1,0:T(8,128)(2,1)}, bf16[16,1,128,128]{3,2,1,0:T(8,128)(2,1)S(1)}, u32[]{:S(2)}, u32[]{:S(2)}) collective-permute-start(bf16[16,1,128,128]{3,2,1,0:T(8,128)(2,1)} %get-tuple-element.32), channel_id=1, source_target_pairs={{0,1},{1,2},{2,3},{3,4},{4,5},{5,6},{6,7},{8,9},{9,10},{10,11},{11... | collective-permute-start | bytes 1572872 | tf_op jit(solution)/shard_map/ppermute | solution.py:488
  7.0 17.7 %collective-permute-start.5 = (bf16[16,1,128,128]{3,2,1,0:T(8,128)(2,1)}, bf16[16,1,128,128]{3,2,1,0:T(8,128)(2,1)S(1)}, u32[]{:S(2)}, u32[]{:S(2)}) collective-permute-start(bf16[16,1,128,128]{3,2,1,0:T(8,128)(2,1)} %get-tuple-element.33), channel_id=1, source_target_pairs={{1,0},{2,1},{3,2},{4,3},{5,4},{6,5},{7,6},{9,8},{10,9},{11,10},{12... | collective-permute-start | bytes 1572872 | tf_op jit(solution)/shard_map/ppermute | solution.py:488
  8.3 6.2 %collective-permute-start = (bf16[2,1,128,128]{3,2,1,0:T(8,128)(2,1)}, bf16[2,1,128,128]{3,2,1,0:T(8,128)(2,1)S(1)}, u32[]{:S(2)}, u32[]{:S(2)}) collective-permute-start(bf16[2,1,128,128]{3,2,1,0:T(8,128)(2,1)} %get-tuple-element.28), channel_id=1, source_target_pairs={{0,1},{1,2},{2,3},{3,4},{4,5},{5,6},{6,7},{8,9},{9,10},{10,11},{11... | collective-permute-start | bytes 196616 | tf_op jit(solution)/shard_map/ppermute | solution.py:488
  13.2 4.6 %collective-permute-start.1 = (bf16[2,1,128,128]{3,2,1,0:T(8,128)(2,1)}, bf16[2,1,128,128]{3,2,1,0:T(8,128)(2,1)S(1)}, u32[]{:S(2)}, u32[]{:S(2)}) collective-permute-start(bf16[2,1,128,128]{3,2,1,0:T(8,128)(2,1)} %get-tuple-element.29), channel_id=1, source_target_pairs={{1,0},{2,1},{3,2},{4,3},{5,4},{6,5},{7,6},{9,8},{10,9},{11,10},{12... | collective-permute-start | bytes 196616 | tf_op jit(solution)/shard_map/ppermute | solution.py:488
  17.8 1.0 copy-start.3
  18.9 1.0 copy-start.4
  20.0 43.9 %collective-permute-start.2 = (bf16[1,18,128,128]{3,2,1,0:T(8,128)(2,1)S(1)}, bf16[1,18,128,128]{3,2,1,0:T(8,128)(2,1)S(1)}, u32[]{:S(2)}, u32[]{:S(2)}) collective-permute-start(bf16[1,18,128,128]{3,2,1,0:T(8,128)(2,1)S(1)} %get-tuple-element.30), channel_id=1, source_target_pairs={{0,8},{8,16},{16,24},{24,32},{32,40},{40,48},{48,56},{56,64},{64,7... | collective-permute-start | bytes 1769480 | tf_op jit(solution)/shard_map/ppermute | solution.py:488
  23.4 40.5 %collective-permute-start.3 = (bf16[1,18,128,128]{3,2,1,0:T(8,128)(2,1)S(1)}, bf16[1,18,128,128]{3,2,1,0:T(8,128)(2,1)S(1)}, u32[]{:S(2)}, u32[]{:S(2)}) collective-permute-start(bf16[1,18,128,128]{3,2,1,0:T(8,128)(2,1)S(1)} %get-tuple-element.31), channel_id=1, source_target_pairs={{8,0},{16,8},{24,16},{32,24},{40,32},{48,40},{56,48},{64,56},{72,6... | collective-permute-start | bytes 1769480 | tf_op jit(solution)/shard_map/ppermute | solution.py:488
  24.7 0.8 copy-start.10
  24.8 1.0 copy-start.11
  25.7 38.2 %copy-start.1 = (bf16[27,128,128]{2,1,0:T(8,128)(2,1)S(1)}, bf16[27,128,128]{2,1,0:T(8,128)(2,1)}, u32[]{:S(2)}) copy-start(bf16[27,128,128]{2,1,0:T(8,128)(2,1)} %taps_ref.1) | copy-start | bytes 2654212
  25.7 38.2 %copy-start.5 = (f32[256,128]{1,0:T(8,128)S(1)}, f32[256,128]{1,0:T(8,128)}, u32[]{:S(2)}) copy-start(f32[256,128]{1,0:T(8,128)} %get-tuple-element.34.occupied_ref) | copy-start | bytes 393220
  25.7 38.2 %copy-start.7 = (s32[48]{0:T(128)S(1)}, s32[48]{0:T(128)}, u32[]{:S(2)}) copy-start(s32[48]{0:T(128)} %get-tuple-element.24.place_ref) | copy-start | bytes 580
  25.7 38.2 %copy-start.8 = (s32[2]{0:T(128)S(1)}, s32[2]{0:T(128)}, u32[]{:S(2)}) copy-start(s32[2]{0:T(128)} %get-tuple-element.25.count_ref) | copy-start | bytes 28
  25.7 38.2 %copy-start.9 = (s32[32]{0:T(128)S(1)}, s32[32]{0:T(128)}, u32[]{:S(2)}) copy-start(s32[32]{0:T(128)} %get-tuple-element.37.slots_ref) | copy-start | bytes 388
  64.0 1.3 copy-start
  65.3 0.7 copy-start.6
  73.9 0.8 copy-start.2
  111.7 64.6 %all-to-all-start.2 = ((bf16[16,2,512,128]{3,2,1,0:T(8,128)(2,1)}), bf16[16,2,512,128]{3,2,1,0:T(8,128)(2,1)}, u32[]{:S(2)}, u32[]{:S(2)}) async-start(bf16[16,2,512,128]{3,2,1,0:T(8,128)(2,1)} %bitcast.8), calls=%async_computation.2 | async-start | bytes 8388608 | tf_op jit(solution)/shard_map/all_to_all | solution.py:481

commit v4 on v3

v4 whole, which is shorter than its diff:
```python
import functools

import jax
import jax.numpy as jnp
from jax import lax
from jax.experimental import pallas as pl
from jax.experimental.pallas import tpu as pltpu
from jax.sharding import PartitionSpec as P

O = 16
E = 8
C = 128
GROUP = 4
ABSENT = -1e30
EPSILON = 1e-05
MIB = 1 << 20


def pair_taps(weight_ref, taps_ref, index):
    blank = jnp.zeros((C, C), jnp.bfloat16)
    for a in range(weight_ref.shape[0]):
        for dz in range(3):
            for j in range(4):
                at = (dz * 4 + j) * C
                weight_ref[a, at : at + C, 0:C] = (
                    taps_ref[index(a, dz, j)] if j < 3 else blank
                )
                weight_ref[a, at : at + C, C : 2 * C] = (
                    taps_ref[index(a, dz, j - 1)] if j > 0 else blank
                )


def shifted_scratch():
    return pltpu.VMEM((2, 3, 2, GROUP, 5, 5, 16, C), jnp.bfloat16)


def conv_kernel(
    place_ref,
    count_ref,
    features_ref,
    y_low_ref,
    y_high_ref,
    taps_hbm,
    occupied_ref,
    conv_ref,
    centre_ref,
    face_ref,
    sums_ref,
    stage,
    out_sems,
    padded,
    raw,
    margins,
    columns_ref,
    taps_ref,
    weight_ref,
    shifted_a,
    shifted_b,
    total_a,
    total_b,
    sems,
):
    count, steps = count_ref[0], count_ref[1]
    chunks = [
        pltpu.make_async_copy(
            features_ref.at[4 * i : 4 * i + 4], raw.at[i % 2], sems.at[i]
        )
        for i in range(4)
    ]
    lane = lax.broadcasted_iota(jnp.int32, (E, C), 1)

    def place_of(k):
        place = place_ref[k]
        return place // 32, place // 16 % 2, place % 16

    def prepare(group, shifted):
        for b in range(GROUP):
            bx, by, bz = place_of(group * GROUP + b)
            for dz in range(3):
                for xx in range(10):
                    lines = [
                        padded[bx * E + xx, by * E + yy, pl.ds(bz * E + 7 + dz, E), :]
                        for yy in range(10)
                    ]
                    for parity in range(2):
                        for yp in range(5 - parity):
                            pair = jnp.concatenate(
                                [lines[2 * yp + parity], lines[2 * yp + parity + 1]], axis=0
                            )
                            shifted[parity, dz, xx % 2, b, xx // 2, yp] = pair.astype(jnp.bfloat16)

    def multiply(shifted, total):
        for dy in range(3):
            parity, first = dy % 2, dy // 2
            parts = []
            for dz in range(3):
                for j in range(4):
                    part = shifted[
                        parity, dz, j % 2, :, j // 2 : j // 2 + 4, first : first + 4, :, :
                    ]
                    parts.append(part.reshape(GROUP * 256, C))
            product = jnp.dot(
                jnp.concatenate(parts, axis=1),
                weight_ref[dy],
                preferred_element_type=jnp.float32,
            )
            if dy == 0:
                total[...] = product
            else:
                total[...] += product

    def emit(group, shifted, total, parity, at):
        summed = jnp.zeros((E, C), jnp.float32)
        squared = jnp.zeros((E, C), jnp.float32)
        counted = jnp.zeros((E, C), jnp.float32)
        for b in range(GROUP):
            k = group * GROUP + b
            bx, by, bz = place_of(k)
            valid = jnp.where(k < count, 1.0, 0.0)
            near = columns_ref[bx, pl.ds(pl.multiple_of(bz * E, E), E), :] * valid
            near = pltpu.roll(near, C - by * E, axis=1)
            counted += jnp.where(lane % 16 < E, near, 0.0)
            for x in range(E):
                live = jnp.concatenate(
                    [
                        jnp.broadcast_to(near[:, x * 16 + y : x * 16 + y + 1], (E, C))
                        for y in range(E)
                    ],
                    axis=0,
                )
                block = total[b * 256 + (x // 2) * 64 : b * 256 + (x // 2) * 64 + 64,
                              (x % 2) * C : (x % 2 + 1) * C]
                wide = (block * live).astype(jnp.bfloat16).astype(jnp.float32)
                kept = wide
                if x == 0:
                    kept = wide * jnp.where(bx == 0, 0.0, 1.0)
                    face_low = block
                if x == E - 1:
                    kept = wide * jnp.where(bx == 0, 1.0, 0.0)
                    face_ref[k] = jnp.where(bx == 0, face_low, block)
                summed += jnp.sum(kept.reshape(E, E, C), axis=0)
                squared += jnp.sum((kept * kept).reshape(E, E, C), axis=0)
                stage[parity, 0, at + b, x * 64 : (x + 1) * 64, :] = jnp.where(
                    live > 0.5, wide, ABSENT
                ).astype(jnp.bfloat16)
                stage[parity, 1, at + b, x * 64 : (x + 1) * 64, :] = shifted[
                    1, 1, (x + 1) % 2, b, (x + 1) // 2, 0:4
                ].reshape(64, C)
        sums_ref[0] += summed
        sums_ref[1] += squared
        sums_ref[2] += counted

    extra = [
        pltpu.make_async_copy(y_low_ref, margins.at[0], sems.at[4]),
        pltpu.make_async_copy(y_high_ref, margins.at[1], sems.at[5]),
        pltpu.make_async_copy(taps_hbm, taps_ref, sems.at[6]),
    ]
    for copy in [chunks[0], chunks[1]] + extra:
        copy.start()
    edge = jnp.zeros((18, 18, E, C), jnp.float32)
    padded[:, :, 0:8, :] = edge
    padded[:, :, 136:144, :] = edge
    side = jnp.zeros((18, 128, C), jnp.float32)
    padded[0, :, 8:136, :] = side
    padded[17, :, 8:136, :] = side
    sums_ref[...] = jnp.zeros_like(sums_ref)
    for i in range(2):
        columns_ref[i] = jnp.transpose(occupied_ref[128 * i : 128 * i + 128, :])
    for i in range(4):
        chunks[i].wait()
        columns = columns_ref[i // 2]

        def mask_plane(j, carry, i=i, columns=columns):
            near = pltpu.roll(columns, 128 - 64 * (i % 2) - 16 * j, axis=1)
            for y in range(16):
                live = jnp.broadcast_to(near[:, y : y + 1], (128, C))
                padded[1 + 4 * i + j, 1 + y, 8:136, :] = (
                    raw[i % 2, j, y].astype(jnp.float32) * live
                )
            return carry

        lax.fori_loop(0, 4, mask_plane, 0)
        if i < 2:
            chunks[i + 2].start()
    for copy in extra:
        copy.wait()
    for side in range(2):
        padded[1:17, 17 * side, 8:136, :] = (
            margins[side].reshape(16, 128, C).astype(jnp.float32)
        )
    pair_taps(weight_ref, taps_ref, lambda dy, dz, dx: 9 * dx + 3 * dy + dz)

    @pl.when(steps > 0)
    def _():
        prepare(0, shifted_a)

    def outgoing(step):
        rows = pl.ds(step * 2 * GROUP, 2 * GROUP)
        return [
            pltpu.make_async_copy(
                stage.at[step % 2, i], ref.at[rows], out_sems.at[step % 2, i]
            )
            for i, ref in enumerate((conv_ref, centre_ref))
        ]

    def drain(step):
        for copy in outgoing(step):
            copy.wait()

    def pair(step, carry):
        @pl.when(step >= 2)
        def _():
            drain(step - 2)

        prepare(2 * step + 1, shifted_b)
        multiply(shifted_a, total_a)
        emit(2 * step, shifted_a, total_a, step % 2, 0)
        multiply(shifted_b, total_b)
        emit(2 * step + 1, shifted_b, total_b, step % 2, GROUP)
        prepare(2 * step + 2, shifted_a)

        for copy in outgoing(step):
            copy.start()
        return carry

    lax.fori_loop(0, steps, pair, 0)

    @pl.when(steps >= 2)
    def _():
        drain(steps - 2)

    @pl.when(steps >= 1)
    def _():
        drain(steps - 1)


def convolve(places, count, features, y_low, y_high, occupied, taps):
    any_spec = pl.BlockSpec(memory_space=pl.ANY)
    whole = pl.BlockSpec(memory_space=pltpu.VMEM)
    scalars = pl.BlockSpec(memory_space=pltpu.SMEM)
    return pl.pallas_call(
        conv_kernel,
        in_specs=[scalars, scalars] + [any_spec] * 4 + [whole],
        out_specs=[any_spec] * 2 + [whole] * 2,
        out_shape=[
            jax.ShapeDtypeStruct((32, 512, C), jnp.bfloat16),
            jax.ShapeDtypeStruct((32, 512, C), jnp.bfloat16),
            jax.ShapeDtypeStruct((32, 64, C), jnp.float32),
            jax.ShapeDtypeStruct((3, E, C), jnp.float32),
        ],
        scratch_shapes=[
            pltpu.VMEM((2, 2, 2 * GROUP, 512, C), jnp.bfloat16),
            pltpu.SemaphoreType.DMA((2, 2)),
            pltpu.VMEM((18, 18, 144, C), jnp.float32),
            pltpu.VMEM((2, 4, 16, 128, C), jnp.bfloat16),
            pltpu.VMEM((2, 16, 1, 128, C), jnp.bfloat16),
            pltpu.VMEM((2, C, C), jnp.float32),
            pltpu.VMEM((27, C, C), jnp.bfloat16),
            pltpu.VMEM((3, 12 * C, 2 * C), jnp.bfloat16),
            shifted_scratch(),
            shifted_scratch(),
            pltpu.VMEM((GROUP * 256, 2 * C), jnp.float32),
            pltpu.VMEM((GROUP * 256, 2 * C), jnp.float32),
            pltpu.SemaphoreType.DMA((7,)),
        ],
        compiler_params=pltpu.CompilerParams(vmem_limit_bytes=52 * MIB),
        cost_estimate=pl.CostEstimate(
            flops=2 * 32 * 256 * 4608 * 256, bytes_accessed=30 * MIB, transcendentals=0
        ),
    )(places, count, features, y_low, y_high, taps, occupied)


def face_kernel(
    place_ref,
    count_ref,
    x_low_ref,
    x_high_ref,
    partial_hbm,
    sums_ref,
    occupied_ref,
    taps_ref,
    slots_ref,
    out_ref,
    norm_ref,
    partial_ref,
    buffer,
    sems,
    columns_ref,
    padded,
    shifted,
    added,
    weight_ref,
):
    count = count_ref[0]
    fetch = pltpu.make_async_copy(partial_hbm, partial_ref, sems.at[8])
    fetch.start()
    pair_taps(weight_ref, taps_ref, lambda side, dz, dy: 18 * side + 3 * dy + dz)
    for i in range(2):
        columns_ref[i] = jnp.transpose(occupied_ref[128 * i : 128 * i + 128, :])
    padded[:, 0:8, :] = jnp.zeros((18, E, C), jnp.float32)
    padded[:, 136:144, :] = jnp.zeros((18, E, C), jnp.float32)
    for side, ref in enumerate((x_low_ref, x_high_ref)):
        padded[:, 8:136, :] = ref[0].astype(jnp.float32)
        for dz in range(3):
            shifted[dz] = padded[:, 7 + dz : 135 + dz, :].astype(jnp.bfloat16).reshape(
                9, 2, 128, C
            )
        parts = []
        for dz in range(3):
            for j in range(4):
                parts.append(shifted[dz, j // 2 : j // 2 + 8, j % 2].reshape(1024, C))
        added[side] = jnp.dot(
            jnp.concatenate(parts, axis=1), weight_ref[side], preferred_element_type=jnp.float32
        )

    fetch.wait()

    def outgoing(i):
        rows = pl.ds(i * GROUP, GROUP)
        return pltpu.make_async_copy(buffer.at[rows], out_ref.at[rows], sems.at[i])

    def several(i, carry):
        summed, squared = carry
        for b in range(GROUP):
            k = i * GROUP + b
            place = place_ref[k]
            bx, by, bz = place // 32, place // 16 % 2, place % 16
            valid = jnp.where(k < count, 1.0, 0.0)
            near = columns_ref[bx, pl.ds(pl.multiple_of(bz * E, E), E), :] * valid
            near = pltpu.roll(near, C - bx * 112 - by * E, axis=1)
            live = jnp.concatenate(
                [jnp.broadcast_to(near[:, y : y + 1], (E, C)) for y in range(E)], axis=0
            )
            pieces = []
            for y in range(E):
                start = pl.multiple_of((by * 4 + y // 2) * 128 + bz * E, E)
                pieces.append(added[bx, pl.ds(start, E), (y % 2) * C : (y % 2 + 1) * C])
            block = partial_ref[k] + jnp.concatenate(pieces, axis=0)
            wide = (block * live).astype(jnp.bfloat16).astype(jnp.float32)
            wide = jnp.where(live > 0.5, wide, 0.0)
            buffer[k] = jnp.where(live > 0.5, wide, ABSENT).astype(jnp.bfloat16)
            summed += jnp.sum(wide.reshape(E, E, C), axis=0)
            squared += jnp.sum((wide * wide).reshape(E, E, C), axis=0)
        outgoing(i).start()
        return summed, squared

    rounds = (count + GROUP - 1) // GROUP
    summed, squared = lax.fori_loop(0, rounds, several, (sums_ref[0], sums_ref[1]))
    table = jnp.concatenate(
        [
            jnp.sum(summed, axis=0, keepdims=True),
            jnp.sum(squared, axis=0, keepdims=True),
            jnp.broadcast_to(jnp.sum(sums_ref[2]), (1, C)),
            jnp.zeros((5, C), jnp.float32),
        ],
        axis=0,
    )
    norm_ref[...] = jnp.broadcast_to(table[None], norm_ref.shape)
    wide_lane = lax.broadcasted_iota(jnp.int32, (1, C), 1)
    for i in range(16):
        pair = jnp.where(wide_lane == 0, slots_ref[2 * i], slots_ref[2 * i + 1])
        norm_ref[i, 3:4, :] = pair.astype(jnp.float32)

    def drain(i, carry):
        outgoing(i).wait()
        return carry

    lax.fori_loop(0, rounds, drain, 0)


def correct_faces(places, count, x_low, x_high, partial, sums, occupied, taps, sent):
    any_spec = pl.BlockSpec(memory_space=pl.ANY)
    whole = pl.BlockSpec(memory_space=pltpu.VMEM)
    scalars = pl.BlockSpec(memory_space=pltpu.SMEM)
    return pl.pallas_call(
        face_kernel,
        in_specs=[scalars, scalars, whole, whole, any_spec] + [whole] * 3 + [scalars],
        out_specs=[any_spec, whole],
        out_shape=[
            jax.ShapeDtypeStruct((32, 64, C), jnp.bfloat16),
            jax.ShapeDtypeStruct((16, E, C), jnp.float32),
        ],
        scratch_shapes=[
            pltpu.VMEM((32, 64, C), jnp.float32),
            pltpu.VMEM((32, 64, C), jnp.bfloat16),
            pltpu.SemaphoreType.DMA((9,)),
            pltpu.VMEM((2, C, C), jnp.float32),
            pltpu.VMEM((18, 144, C), jnp.float32),
            pltpu.VMEM((3, 9, 2, 128, C), jnp.bfloat16),
            pltpu.VMEM((2, 1024, 2 * C), jnp.float32),
            pltpu.VMEM((2, 12 * C, 2 * C), jnp.bfloat16),
        ],
        compiler_params=pltpu.CompilerParams(vmem_limit_bytes=32 * MIB),
    )(places, count, x_low, x_high, partial, sums, occupied, taps, sent)


def finish_kernel(
    slot_ref,
    place_ref,
    count_ref,
    conv_hbm,
    centre_hbm,
    face_ref,
    sums_ref,
    gain_ref,
    bias_ref,
    out_ref,
    conv_ref,
    centre_ref,
    buffer,
    in_sems,
    sems,
):
    count = count_ref[0]

    def incoming(group):
        rows = pl.ds(group * GROUP, GROUP)
        return [
            pltpu.make_async_copy(hbm.at[rows], ref.at[rows], in_sems.at[i, group])
            for i, (hbm, ref) in enumerate(((conv_hbm, conv_ref), (centre_hbm, centre_ref)))
        ]

    for group in range(32 // GROUP):

        @pl.when(group * GROUP < count)
        def _():
            for each in incoming(group):
                each.start()

    sums = jnp.sum(sums_ref[...], axis=0)
    mean = sums[0:1] / sums[2:3]
    variance = sums[1:2] / sums[2:3] - mean * mean
    factor = gain_ref[...] / jnp.sqrt(variance + EPSILON)
    bias = bias_ref[...]

    def copy(k):
        return pltpu.make_async_copy(buffer.at[k], out_ref.at[slot_ref[k]], sems.at[k])

    def one(k, carry):
        @pl.when(k % GROUP == 0)
        def _():
            for each in incoming(k // GROUP):
                each.wait()

        bx = place_ref[k] // 32
        for x in range(E):
            conv = conv_ref[k, x * 64 : (x + 1) * 64, :].astype(jnp.float32)
            if x in (0, E - 1):
                own = face_ref[k].astype(jnp.float32)
                conv = jnp.where(bx == (0 if x == 0 else 1), own, conv)
            scaled = factor * (conv - mean) + bias
            silu = scaled * (0.5 + 0.5 * jnp.tanh(0.5 * scaled))
            silu = jnp.where(conv > 0.5 * ABSENT, silu, 0.0)
            centre = centre_ref[k, x * 64 : (x + 1) * 64, :].astype(jnp.float32)
            buffer[k, x * 64 : (x + 1) * 64, :] = (centre + silu).astype(jnp.bfloat16)
        copy(k).start()
        return carry

    def drain(k, carry):
        copy(k).wait()
        return carry

    lax.fori_loop(0, count, one, 0)
    lax.fori_loop(0, count, drain, 0)


def finish(slots, places, count, conv, centre, face, sums, gain, bias):
    whole = pl.BlockSpec(memory_space=pltpu.VMEM)
    scalars = pl.BlockSpec(memory_space=pltpu.SMEM)
    return pl.pallas_call(
        finish_kernel,
        in_specs=[scalars] * 3 + [pl.BlockSpec(memory_space=pl.ANY)] * 2 + [whole] * 4,
        out_specs=pl.BlockSpec(memory_space=pl.ANY),
        scratch_shapes=[
            pltpu.VMEM((32, 512, C), jnp.bfloat16),
            pltpu.VMEM((32, 512, C), jnp.bfloat16),
            pltpu.VMEM((32, 512, C), jnp.bfloat16),
            pltpu.SemaphoreType.DMA((2, 32 // GROUP)),
            pltpu.SemaphoreType.DMA((32,)),
        ],
        out_shape=jax.ShapeDtypeStruct((32, 512, C), jnp.bfloat16),
        compiler_params=pltpu.CompilerParams(vmem_limit_bytes=56 * MIB),
    )(slots, places, count, conv, centre, face, sums, gain, bias)


def pick_kernel(named_ref, in_ref, out_ref, buffer, sems):
    named = named_ref[:, 3, :]
    lane = lax.broadcasted_iota(jnp.int32, (16, C), 1)
    source = 2 * lax.broadcasted_iota(jnp.int32, (16, C), 0) + lane
    reads, writes = [], []
    for i in range(O):
        hit = (named == float(i)) & (lane < 2)
        index = jnp.sum(jnp.where(hit, source, 0))
        reads.append(pltpu.make_async_copy(in_ref.at[index], buffer.at[i], sems.at[0, i]))
        writes.append(pltpu.make_async_copy(buffer.at[i], out_ref.at[i], sems.at[1, i]))
    for read in reads:
        read.start()
    for read, write in zip(reads, writes):
        read.wait()
        write.start()
    for write in writes:
        write.wait()


def pick(named, received):
    return pl.pallas_call(
        pick_kernel,
        in_specs=[pl.BlockSpec(memory_space=pltpu.VMEM), pl.BlockSpec(memory_space=pl.ANY)],
        out_specs=pl.BlockSpec(memory_space=pl.ANY),
        scratch_shapes=[
            pltpu.VMEM((O, 512, C), jnp.bfloat16),
            pltpu.SemaphoreType.DMA((2, O)),
        ],
        out_shape=jax.ShapeDtypeStruct((O, 512, C), jnp.bfloat16),
    )(named, received)


def swap(spread, axis):
    return lax.all_to_all(spread, axis, 0, 0, tiled=True)


def neighbours(low_block, high_block, axis):
    count = lax.axis_size(axis)
    up = [(i, i + 1) for i in range(count - 1)]
    down = [(j, i) for i, j in up]
    return lax.ppermute(high_block, axis, up), lax.ppermute(low_block, axis, down)


def masked_line(line, columns, x, y):
    column = x % E * 16 + y
    live = jnp.broadcast_to(columns[x // E][:, column : column + 1], (128, C))
    return (line.astype(jnp.float32) * live).astype(jnp.bfloat16)


def line_columns(lines_ref):
    return [jnp.transpose(lines_ref[128 * i : 128 * i + 128, :]) for i in range(2)]


def y_edges_kernel(
    active_ref,
    occupancy_ref,
    features_ref,
    lines_ref,
    first_ref,
    last_ref,
    ends_first_ref,
    ends_last_ref,
    raw,
    sems,
):
    copies = [
        pltpu.make_async_copy(features_ref.at[:, 15 * i], raw.at[i], sems.at[i]) for i in range(2)
    ]
    for copy in copies:
        copy.start()
    repeat = jnp.where(
        lax.broadcasted_iota(jnp.int32, (16, C), 1) // E
        == lax.broadcasted_iota(jnp.int32, (16, C), 0),
        1.0,
        0.0,
    ).astype(jnp.bfloat16)
    for bx in range(2):
        spread = jnp.dot(
            jnp.where(active_ref[bx] >= 0, 1.0, 0.0).astype(jnp.bfloat16),
            repeat,
            preferred_element_type=jnp.float32,
        )
        for x in range(bx * E, bx * E + E):
            for by in range(2):
                at = x * 16 + by * E
                lines_ref[at : at + E, :] = (
                    occupancy_ref[at : at + E, :].astype(jnp.float32) * spread[by : by + 1, :]
                )
    columns = line_columns(lines_ref)
    for i, (ref, ends) in enumerate(((first_ref, ends_first_ref), (last_ref, ends_last_ref))):
        copies[i].wait()
        for x in range(16):
            line = masked_line(raw[i, x], columns, x, 15 * i)
            ref[x, 0] = line
            if x in (0, 15):
                ends[x // 15, 0] = line


def x_edges_kernel(
    owner_ref,
    lines_ref,
    features_ref,
    first_ref,
    last_ref,
    place_ref,
    slot_ref,
    count_ref,
    sent_ref,
    raw,
    met,
    sems,
):
    copies = [
        pltpu.make_async_copy(features_ref.at[15 * i], raw.at[i], sems.at[i]) for i in range(2)
    ]
    for copy in copies:
        copy.start()

    for i in range(17):
        met[i] = 0
    for i in range(32):
        sent_ref[i] = -1
    for i in range(48):
        place_ref[i] = 0
        slot_ref[i] = 0

    def route(i, carry):
        owned = owner_ref[i // 32, i // 16 % 2, i % 16]

        @pl.when(owned >= 0)
        def _():
            owner = owned // 16
            slot = 2 * owner + met[owner]
            rank = met[16]
            met[owner] = met[owner] + 1
            met[16] = rank + 1
            place_ref[rank] = i
            slot_ref[rank] = slot
            sent_ref[slot] = owned % 16

        return carry

    lax.fori_loop(0, 64, route, 0)
    count_ref[0] = met[16]
    count_ref[1] = (met[16] + 2 * GROUP - 1) // (2 * GROUP)
    columns = line_columns(lines_ref)
    for i, ref in enumerate((first_ref, last_ref)):
        copies[i].wait()
        for y in range(16):
            ref[0, 1 + y] = masked_line(raw[i, y], columns, 15 * i, y)


def y_edges(owner_map, occupancy, features):
    whole = pl.BlockSpec(memory_space=pltpu.VMEM)
    blocks = [(16, 1), (16, 1), (2, 1), (2, 1)]
    return pl.pallas_call(
        y_edges_kernel,
        in_specs=[whole, whole, pl.BlockSpec(memory_space=pl.ANY)],
        out_specs=[whole] * 5,
        out_shape=[jax.ShapeDtypeStruct((256, 128), jnp.float32)]
        + [jax.ShapeDtypeStruct(block + (128, C), jnp.bfloat16) for block in blocks],
        scratch_shapes=[
            pltpu.VMEM((2, 16, 128, C), jnp.bfloat16),
            pltpu.SemaphoreType.DMA((2,)),
        ],
        compiler_params=pltpu.CompilerParams(vmem_limit_bytes=57 * MIB),
    )(owner_map, occupancy, features)


def x_edges(owner_map, lines, features):
    whole = pl.BlockSpec(memory_space=pltpu.VMEM)
    scalars = pl.BlockSpec(memory_space=pltpu.SMEM)
    return pl.pallas_call(
        x_edges_kernel,
        in_specs=[scalars, whole, pl.BlockSpec(memory_space=pl.ANY)],
        out_specs=[whole] * 2 + [scalars] * 4,
        out_shape=[jax.ShapeDtypeStruct((1, 18, 128, C), jnp.bfloat16)] * 2
        + [jax.ShapeDtypeStruct((n,), jnp.int32) for n in (48, 48, 2, 32)],
        scratch_shapes=[
            pltpu.VMEM((2, 16, 128, C), jnp.bfloat16),
            pltpu.SMEM((17,), jnp.int32),
            pltpu.SemaphoreType.DMA((2,)),
        ],
        compiler_params=pltpu.CompilerParams(vmem_limit_bytes=57 * MIB),
    )(owner_map, lines, features)


def widen_kernel(first_ref, last_ref, low_ref, high_ref, first_out, last_out, sems):
    copies = []
    for i, out in enumerate((first_out, last_out)):
        for j, ref in enumerate((low_ref, high_ref)):
            copies.append(
                pltpu.make_async_copy(ref.at[i], out.at[0, 17 * j : 17 * j + 1], sems.at[i, j])
            )
    for copy in copies:
        copy.start()
    for copy in copies:
        copy.wait()


def widen(first, last, low, high):
    any_spec = pl.BlockSpec(memory_space=pl.ANY)
    return pl.pallas_call(
        widen_kernel,
        in_specs=[any_spec] * 2 + [pl.BlockSpec(memory_space=pltpu.VMEM)] * 2,
        out_specs=[any_spec] * 2,
        out_shape=[jax.ShapeDtypeStruct((1, 18, 128, C), jnp.bfloat16)] * 2,
        scratch_shapes=[pltpu.SemaphoreType.DMA((2, 2))],
        input_output_aliases={0: 0, 1: 1},
    )(first, last, low, high)


def on_device(features, occupancy, owner_map, kernel, norm_gain, norm_bias):
    lines, y_first, y_last, ends_first, ends_last = y_edges(
        owner_map, occupancy.reshape(256, 128), features
    )
    line_low, line_high = neighbours(ends_first, ends_last, "gy")
    y_low, y_high = neighbours(y_first, y_last, "gy")
    x_first, x_last, places, slot_of, counts, sent = x_edges(owner_map, lines, features)
    x_low, x_high = neighbours(*widen(x_first, x_last, line_low, line_high), "gx")
    conv, centre, partial, sums = convolve(places, counts, features, y_low, y_high, lines, kernel)
    face_conv, spread = correct_faces(
        places, counts, x_low, x_high, partial, sums, lines, kernel, sent
    )
    arrived = swap(spread, "gx")
    totals = swap(jnp.broadcast_to(jnp.sum(arrived, axis=0)[None], (8, E, C)), "gy")
    result = finish(
        slot_of,
        places,
        counts,
        conv,
        centre,
        face_conv,
        totals,
        norm_gain.reshape(1, C),
        norm_bias.reshape(1, C),
    )
    received = swap(result.reshape(16, 2, 512, C), "gx").reshape(32, 512, C)
    return pick(arrived, received).reshape(O, 1, 512, C)


def solution(mesh):
    in_specs = (P("gx", "gy", None, None), P("gx", "gy", None), P("gx", "gy", None), P(), P(), P())
    out_specs = P("gx", "gy", None, None)
    return jax.shard_map(
        on_device, mesh=mesh, in_specs=in_specs, out_specs=out_specs, check_vma=False
    )
```

time: 182 us -> 162 us (0.89); the launches traced: 179 us -> 162 us
  blocking collectives: 27.4 us -> 89.9 us
  waiting for transfers between devices: 62.5 us -> 0.02 us
  Pallas kernels: 64.6 us -> 54.1 us
  starting transfers between devices: 18.1 us -> 13.5 us
  local copies, waits for them, and re-layouts: 5.95 us -> 3.9 us
    all_to_all x2 -> x3, blocking collectives: 27.4 us -> 89.9 us  [swap(): return lax.all_to_all(spread, axis, 0, 0, tiled=True)]
    all_to_all x1 -> x0, waiting for transfers between devices: 59.2 us -> none  [swap(): return lax.all_to_all(spread, axis, 0, 0, tiled=True)]
    pallas_call x6 -> x7, Pallas kernels: 64.6 us -> 54.1 us  [the longest x1 29 us: convolve(): pl.pallas_call(conv_kernel, in_specs=[scalars, scalars] + [any_spec] * 4...]
    all_to_all x1 -> x0, starting transfers between devices: 4.55 us -> none  [swap(): return lax.all_to_all(spread, axis, 0, 0, tiled=True)]
    ppermute x3, waiting for transfers between devices: 3.29 us -> 0.01 us  [neighbours(): lax.ppermute(low_block, axis, down)]
    unnamed x24 -> x20, local copies, waits for them, and re-layouts: 5.86 us -> 3.9 us
  transfers between devices with their start and end apart: 7 -> 6, of which waited for: 2 -> 0; matrix products, arithmetic and copies ran while one was open for 0% -> 0% of each run, Pallas kernels for 21% -> 22%
where the time goes in v4:
time: 162 us
  blocking collectives  89.9 us (55%)
  Pallas kernels  54.1 us (33%)
  starting transfers between devices  13.5 us (8%)
  local copies, waits for them, and re-layouts  3.9 us (2%)
    all_to_all x3, blocking collectives, swap(): return lax.all_to_all(spread, axis, 0, 0, tiled=True)  89.9 us
    pallas_call x1, Pallas kernels, convolve(): pl.pallas_call(conv_kernel, in_specs=[scalars, scalars] + [any_spec] * 4...  29 us
    ppermute x3, starting transfers between devices, neighbours(): lax.ppermute(high_block, axis, up)  9.65 us
    pallas_call x1, Pallas kernels, finish(): pl.pallas_call(finish_kernel, in_specs=[scalars] * 3 + [pl.BlockSpec(memo...  6.5 us
    pallas_call x1, Pallas kernels, correct_faces(): pl.pallas_call(face_kernel, in_specs=[scalars, scalars, whole, whole, any...  5.16 us
    pallas_call x1, Pallas kernels, x_edges(): pl.pallas_call(x_edges_kernel, in_specs=[scalars, whole, pl.BlockSpec(mem...  4.67 us
    unnamed x20, local copies, waits for them, and re-layouts  3.9 us
    ppermute x3, starting transfers between devices, neighbours(): lax.ppermute(low_block, axis, down)  3.88 us
  transfers between devices with their start and end apart: 6, of which 0 were waited for; matrix products, arithmetic and copies ran while one was open for 0% of the time, Pallas kernels for 22%

profile of v4, /device:TPU:0, one launch (start us, length us, event | category | flops | bytes accessed | tf_op | source)
XLA Modules:
  0.0 161.7 jit_solution(3161575128880810552)
XLA Ops:
  0.0 3.5 %shard_map.64 = (f32[256,128]{1,0:T(8,128)}, bf16[16,1,128,128]{3,2,1,0:T(8,128)(2,1)}, bf16[16,1,128,128]{3,2,1,0:T(8,128)(2,1)}, bf16[2,1,128,128]{3,2,1,0:T(8,128)(2,1)}, bf16[2,1,128,128]{3,2,1,0:T(8,128)(2,1)}) custom-call(s32[2,2,16]{2,1,0:T(2,128)} %owner_ref.1, s32[256,128]{1,0:T(8,128)} %bitcast.10, bf16[16,16,128,128]{3,2,1,0:T(8,128)(2,1)} %features_ref.5), custom_call_target="tpu_custom_call" | custom-call | tf_op jit(solution)/shard_map/pallas_call | solution.py:641
  3.5 1.3 collective-permute-start.4
  4.9 1.3 collective-permute-start.5
  6.2 4.9 %collective-permute-start = (bf16[2,1,128,128]{3,2,1,0:T(8,128)(2,1)}, bf16[2,1,128,128]{3,2,1,0:T(8,128)(2,1)S(1)}, u32[]{:S(2)}, u32[]{:S(2)}) collective-permute-start(bf16[2,1,128,128]{3,2,1,0:T(8,128)(2,1)} %get-tuple-element.29), channel_id=1, source_target_pairs={{0,1},{1,2},{2,3},{3,4},{4,5},{5,6},{6,7},{8,9},{9,10},{10,11},{11... | collective-permute-start | bytes 196616 | tf_op jit(solution)/shard_map/ppermute | solution.py:526
  11.1 1.3 collective-permute-start.1
  12.4 4.7 %shard_map.65 = (bf16[1,18,128,128]{3,2,1,0:T(8,128)(2,1)}, bf16[1,18,128,128]{3,2,1,0:T(8,128)(2,1)}, s32[48]{0:T(128)}, s32[48]{0:T(128)}, s32[2]{0:T(128)}, /*index=5*/s32[32]{0:T(128)}) custom-call(s32[2,2,16]{2,1,0:T(2,128)} %owner_ref.1, f32[256,128]{1,0:T(8,128)} %get-tuple-element.24.lines_ref.occupied_ref, bf16[16,16,128,128]{3,2,1,0:T(8,128)(2,1)} %features_ref.5), custom_call_target="tpu_custom_call" | custom-call | tf_op jit(solution)/shard_map/pallas_call | solution.py:658
  17.0 0.0 collective-permute-done.low_ref
  17.1 0.0 copy-start.8
  17.1 0.0 collective-permute-done.1.high_ref
  17.1 0.6 copy-done.8
  17.7 0.0 copy-done.9
  17.7 1.6 shard_map.66
  19.3 3.4 %collective-permute-start.2 = (bf16[1,18,128,128]{3,2,1,0:T(8,128)(2,1)}, bf16[1,18,128,128]{3,2,1,0:T(8,128)(2,1)S(1)}, u32[]{:S(2)}, u32[]{:S(2)}) collective-permute-start(bf16[1,18,128,128]{3,2,1,0:T(8,128)(2,1)} %get-tuple-element.31), channel_id=1, source_target_pairs={{0,8},{8,16},{16,24},{24,32},{32,40},{40,48},{48,56},{56,64},{64,7... | collective-permute-start | bytes 1769480 | tf_op jit(solution)/shard_map/ppermute | solution.py:526
  22.7 1.3 collective-permute-start.3
  24.0 0.0 collective-permute-done.4.y_low_ref
  24.0 0.0 collective-permute-done.5.y_high_ref
  24.1 0.6 copy-done.4
  24.7 0.6 copy-done.5
  25.3 29.0 %shard_map.67 = (bf16[32,512,128]{2,1,0:T(8,128)(2,1)}, bf16[32,512,128]{2,1,0:T(8,128)(2,1)}, f32[32,64,128]{2,1,0:T(8,128)}, f32[3,8,128]{2,1,0:T(8,128)S(1)}) custom-call(s32[48]{0:T(128)S(1)} %copy-done.4, s32[2]{0:T(128)S(1)} %copy-done.5, bf16[16,16,128,128]{3,2,1,0:T(8,128)(2,1)} %features_ref.5, ...), custom_call_target="tpu_custom_call" | custom-call | flops 19327352832 | bytes 31457280 | tf_op jit(solution)/shard_map/pallas_call | solution.py:241
  54.4 0.0 collective-permute-done.2.x_low_ref
  54.4 0.0 collective-permute-done.3.x_high_ref
  54.4 0.0 copy-start
  54.4 1.2 copy-done
  55.6 5.2 %shard_map.68 = (bf16[32,64,128]{2,1,0:T(8,128)(2,1)S(1)}, f32[16,8,128]{2,1,0:T(8,128)S(1)}) custom-call(s32[48]{0:T(128)S(1)} %copy-done.4, s32[2]{0:T(128)S(1)} %copy-done.5, bf16[1,18,128,128]{3,2,1,0:T(8,128)(2,1)S(1)} %collective-permute-done.2.x_low_ref, bf16[1,18,128,128]{3,2,1,0:T(8,128)(2,1)S(1)} %collective-permute-done.3.x_high_ref, ...), custom_call_target="tpu_custom_call" | custom-call | tf_op jit(solution)/shard_map/pallas_call | solution.py:375
  60.8 0.0 copy-start.3
  60.8 0.8 copy-done.3
  61.6 22.7 %all_to_all.15.named_ref = f32[16,8,128]{2,1,0:T(8,128)S(1)} all-to-all(f32[16,8,128]{2,1,0:T(8,128)S(1)} %get-tuple-element.38), channel_id=1, replica_groups=mesh['gx'=16,'gy'=8] {'gx'}, dimensions={0} | all-to-all | bytes 131072 | tf_op jit(solution)/shard_map/all_to_all | solution.py:519
  84.4 12.0 %all_to_all.16.sums_ref = f32[8,8,128]{2,1,0:T(8,128)} all-to-all(f32[8,8,128]{2,1,0:T(8,128)S(1)} %broadcast_in_dim.2), channel_id=1, replica_groups=mesh['gx'=16,'gy'=8] {'gy'}, dimensions={0} | all-to-all | bytes 65536 | tf_op jit(solution)/shard_map/all_to_all | solution.py:519
  96.4 6.5 %shard_map.69 = bf16[32,512,128]{2,1,0:T(8,128)(2,1)} custom-call(s32[48]{0:T(128)} %get-tuple-element.39.slot_ref, s32[48]{0:T(128)} %get-tuple-element.25.place_ref, s32[2]{0:T(128)} %get-tuple-element.26.count_ref, bf16[32,512,128]{2,1,0:T(8,128)(2,1)} %get-tuple-element.40.conv_hbm, bf16[32,512,128]{2,1,0:T(8,128)(2,1)} %get-tuple-element.41.centre_hbm, ...), custom_call_target="tpu_custom_call" | custom-call | tf_op jit(solution)/shard_map/pallas_call | solution.py:470
  102.9 0.0 copy-done.7
  102.9 55.2 %all_to_all.17 = bf16[16,2,512,128]{3,2,1,0:T(8,128)(2,1)} all-to-all(bf16[16,2,512,128]{3,2,1,0:T(8,128)(2,1)} %bitcast.9), channel_id=1, replica_groups=mesh['gx'=16,'gy'=8] {'gx'}, dimensions={0} | all-to-all | bytes 8388608 | tf_op jit(solution)/shard_map/all_to_all | solution.py:519
  158.1 3.6 %shard_map.70 = bf16[16,512,128]{2,1,0:T(8,128)(2,1)} custom-call(f32[16,8,128]{2,1,0:T(8,128)} %copy-done.7, bf16[32,512,128]{2,1,0:T(8,128)(2,1)} %bitcast.8), custom_call_target="tpu_custom_call" | custom-call | tf_op jit(solution)/shard_map/pallas_call | solution.py:506
  (12 shorter events, 0.0 us)
Async XLA Ops:
  3.5 20.5 %collective-permute-start.4 = (bf16[16,1,128,128]{3,2,1,0:T(8,128)(2,1)}, bf16[16,1,128,128]{3,2,1,0:T(8,128)(2,1)S(1)}, u32[]{:S(2)}, u32[]{:S(2)}) collective-permute-start(bf16[16,1,128,128]{3,2,1,0:T(8,128)(2,1)} %get-tuple-element.33), channel_id=1, source_target_pairs={{0,1},{1,2},{2,3},{3,4},{4,5},{5,6},{6,7},{8,9},{9,10},{10,11},{11... | collective-permute-start | bytes 1572872 | tf_op jit(solution)/shard_map/ppermute | solution.py:526
  4.9 19.2 %collective-permute-start.5 = (bf16[16,1,128,128]{3,2,1,0:T(8,128)(2,1)}, bf16[16,1,128,128]{3,2,1,0:T(8,128)(2,1)S(1)}, u32[]{:S(2)}, u32[]{:S(2)}) collective-permute-start(bf16[16,1,128,128]{3,2,1,0:T(8,128)(2,1)} %get-tuple-element.34), channel_id=1, source_target_pairs={{1,0},{2,1},{3,2},{4,3},{5,4},{6,5},{7,6},{9,8},{10,9},{11,10},{12... | collective-permute-start | bytes 1572872 | tf_op jit(solution)/shard_map/ppermute | solution.py:526
  6.2 10.9 %collective-permute-start = (bf16[2,1,128,128]{3,2,1,0:T(8,128)(2,1)}, bf16[2,1,128,128]{3,2,1,0:T(8,128)(2,1)S(1)}, u32[]{:S(2)}, u32[]{:S(2)}) collective-permute-start(bf16[2,1,128,128]{3,2,1,0:T(8,128)(2,1)} %get-tuple-element.29), channel_id=1, source_target_pairs={{0,1},{1,2},{2,3},{3,4},{4,5},{5,6},{6,7},{8,9},{9,10},{10,11},{11... | collective-permute-start | bytes 196616 | tf_op jit(solution)/shard_map/ppermute | solution.py:526
  11.1 6.0 %collective-permute-start.1 = (bf16[2,1,128,128]{3,2,1,0:T(8,128)(2,1)}, bf16[2,1,128,128]{3,2,1,0:T(8,128)(2,1)S(1)}, u32[]{:S(2)}, u32[]{:S(2)}) collective-permute-start(bf16[2,1,128,128]{3,2,1,0:T(8,128)(2,1)} %get-tuple-element.30), channel_id=1, source_target_pairs={{1,0},{2,1},{3,2},{4,3},{5,4},{6,5},{7,6},{9,8},{10,9},{11,10},{12... | collective-permute-start | bytes 196616 | tf_op jit(solution)/shard_map/ppermute | solution.py:526
  12.4 11.7 %copy-start.2 = (f32[256,128]{1,0:T(8,128)S(1)}, f32[256,128]{1,0:T(8,128)}, u32[]{:S(2)}) copy-start(f32[256,128]{1,0:T(8,128)} %get-tuple-element.24.lines_ref.occupied_ref) | copy-start | bytes 393220
  17.1 0.6 copy-start.8
  17.1 0.6 copy-start.9
  19.3 35.1 %collective-permute-start.2 = (bf16[1,18,128,128]{3,2,1,0:T(8,128)(2,1)}, bf16[1,18,128,128]{3,2,1,0:T(8,128)(2,1)S(1)}, u32[]{:S(2)}, u32[]{:S(2)}) collective-permute-start(bf16[1,18,128,128]{3,2,1,0:T(8,128)(2,1)} %get-tuple-element.31), channel_id=1, source_target_pairs={{0,8},{8,16},{16,24},{24,32},{32,40},{40,48},{48,56},{56,64},{64,7... | collective-permute-start | bytes 1769480 | tf_op jit(solution)/shard_map/ppermute | solution.py:526
  22.7 31.6 %collective-permute-start.3 = (bf16[1,18,128,128]{3,2,1,0:T(8,128)(2,1)}, bf16[1,18,128,128]{3,2,1,0:T(8,128)(2,1)S(1)}, u32[]{:S(2)}, u32[]{:S(2)}) collective-permute-start(bf16[1,18,128,128]{3,2,1,0:T(8,128)(2,1)} %get-tuple-element.32), channel_id=1, source_target_pairs={{8,0},{16,8},{24,16},{32,24},{40,32},{48,40},{56,48},{64,56},{72,6... | collective-permute-start | bytes 1769480 | tf_op jit(solution)/shard_map/ppermute | solution.py:526
  24.1 0.6 copy-start.4
  24.7 0.6 copy-start.5
  25.3 29.1 %copy-start.1 = (bf16[27,128,128]{2,1,0:T(8,128)(2,1)S(1)}, bf16[27,128,128]{2,1,0:T(8,128)(2,1)}, u32[]{:S(2)}) copy-start(bf16[27,128,128]{2,1,0:T(8,128)(2,1)} %taps_ref.1) | copy-start | bytes 2654212
  25.3 29.1 %copy-start.6 = (s32[32]{0:T(128)S(1)}, s32[32]{0:T(128)}, u32[]{:S(2)}) copy-start(s32[32]{0:T(128)} %get-tuple-element.37.slots_ref) | copy-start | bytes 388
  54.4 1.2 copy-start
  60.8 0.8 copy-start.3
  84.3 18.6 %copy-start.7 = (f32[16,8,128]{2,1,0:T(8,128)}, f32[16,8,128]{2,1,0:T(8,128)S(1)}, u32[]{:S(2)}) copy-start(f32[16,8,128]{2,1,0:T(8,128)S(1)} %all_to_all.15.named_ref) | copy-start | bytes 196612

commit v5 on v4

--- a/solution.py
+++ b/solution.py
@@ -8,6 +8,7 @@
 from jax.sharding import PartitionSpec as P
 
 O = 16
+SLOTS, SENT, COUNT = 48, 96, 128
 E = 8
 C = 128
 GROUP = 4
@@ -35,8 +36,7 @@
 
 
 def conv_kernel(
-    place_ref,
-    count_ref,
+    route_ref,
     features_ref,
     y_low_ref,
     y_high_ref,
@@ -60,7 +60,7 @@
     total_b,
     sems,
 ):
-    count, steps = count_ref[0], count_ref[1]
+    count, steps = route_ref[COUNT], route_ref[COUNT + 1]
     chunks = [
         pltpu.make_async_copy(
             features_ref.at[4 * i : 4 * i + 4], raw.at[i % 2], sems.at[i]
@@ -70,7 +70,7 @@
     lane = lax.broadcasted_iota(jnp.int32, (E, C), 1)
 
     def place_of(k):
-        place = place_ref[k]
+        place = route_ref[k]
         return place // 32, place // 16 % 2, place % 16
 
     def prepare(group, shifted):
@@ -234,13 +234,13 @@
         drain(steps - 1)
 
 
-def convolve(places, count, features, y_low, y_high, occupied, taps):
+def convolve(routes, features, y_low, y_high, occupied, taps):
     any_spec = pl.BlockSpec(memory_space=pl.ANY)
     whole = pl.BlockSpec(memory_space=pltpu.VMEM)
     scalars = pl.BlockSpec(memory_space=pltpu.SMEM)
     return pl.pallas_call(
         conv_kernel,
-        in_specs=[scalars, scalars] + [any_spec] * 4 + [whole],
+        in_specs=[scalars] + [any_spec] * 4 + [whole],
         out_specs=[any_spec] * 2 + [whole] * 2,
         out_shape=[
             jax.ShapeDtypeStruct((32, 512, C), jnp.bfloat16),
@@ -263,23 +263,21 @@
             pltpu.VMEM((GROUP * 256, 2 * C), jnp.float32),
             pltpu.SemaphoreType.DMA((7,)),
         ],
-        compiler_params=pltpu.CompilerParams(vmem_limit_bytes=52 * MIB),
+        compiler_params=pltpu.CompilerParams(vmem_limit_bytes=49 * MIB),
         cost_estimate=pl.CostEstimate(
             flops=2 * 32 * 256 * 4608 * 256, bytes_accessed=30 * MIB, transcendentals=0
         ),
-    )(places, count, features, y_low, y_high, taps, occupied)
+    )(routes, features, y_low, y_high, taps, occupied)
 
 
 def face_kernel(
-    place_ref,
-    count_ref,
+    route_ref,
     x_low_ref,
     x_high_ref,
     partial_hbm,
     sums_ref,
     occupied_ref,
     taps_ref,
-    slots_ref,
     out_ref,
     norm_ref,
     partial_ref,
@@ -291,7 +289,7 @@
     added,
     weight_ref,
 ):
-    count = count_ref[0]
+    count = route_ref[COUNT]
     fetch = pltpu.make_async_copy(partial_hbm, partial_ref, sems.at[8])
     fetch.start()
     pair_taps(weight_ref, taps_ref, lambda side, dz, dy: 18 * side + 3 * dy + dz)
@@ -323,7 +321,7 @@
         summed, squared = carry
         for b in range(GROUP):
             k = i * GROUP + b
-            place = place_ref[k]
+            place = route_ref[k]
             bx, by, bz = place // 32, place // 16 % 2, place % 16
             valid = jnp.where(k < count, 1.0, 0.0)
             near = columns_ref[bx, pl.ds(pl.multiple_of(bz * E, E), E), :] * valid
@@ -346,20 +344,16 @@
 
     rounds = (count + GROUP - 1) // GROUP
     summed, squared = lax.fori_loop(0, rounds, several, (sums_ref[0], sums_ref[1]))
-    table = jnp.concatenate(
-        [
-            jnp.sum(summed, axis=0, keepdims=True),
-            jnp.sum(squared, axis=0, keepdims=True),
-            jnp.broadcast_to(jnp.sum(sums_ref[2]), (1, C)),
-            jnp.zeros((5, C), jnp.float32),
-        ],
-        axis=0,
-    )
-    norm_ref[...] = jnp.broadcast_to(table[None], norm_ref.shape)
-    wide_lane = lax.broadcasted_iota(jnp.int32, (1, C), 1)
+    sums = [
+        jnp.sum(summed, axis=0, keepdims=True),
+        jnp.sum(squared, axis=0, keepdims=True),
+        jnp.broadcast_to(jnp.sum(sums_ref[2]), (1, C)),
+    ]
+    first_lane = lax.broadcasted_iota(jnp.int32, (1, C), 1) == 0
     for i in range(16):
-        pair = jnp.where(wide_lane == 0, slots_ref[2 * i], slots_ref[2 * i + 1])
-        norm_ref[i, 3:4, :] = pair.astype(jnp.float32)
+        pair = jnp.where(first_lane, route_ref[SENT + 2 * i], route_ref[SENT + 2 * i + 1])
+        table = jnp.concatenate(sums + [pair.astype(jnp.float32)], axis=0)
+        norm_ref[8 * i : 8 * i + 8] = jnp.broadcast_to(table[None], (8, 4, C))
 
     def drain(i, carry):
         outgoing(i).wait()
@@ -368,17 +362,17 @@
     lax.fori_loop(0, rounds, drain, 0)
 
 
-def correct_faces(places, count, x_low, x_high, partial, sums, occupied, taps, sent):
+def correct_faces(routes, x_low, x_high, partial, sums, occupied, taps):
     any_spec = pl.BlockSpec(memory_space=pl.ANY)
     whole = pl.BlockSpec(memory_space=pltpu.VMEM)
     scalars = pl.BlockSpec(memory_space=pltpu.SMEM)
     return pl.pallas_call(
         face_kernel,
-        in_specs=[scalars, scalars, whole, whole, any_spec] + [whole] * 3 + [scalars],
+        in_specs=[scalars, whole, whole, any_spec] + [whole] * 3,
         out_specs=[any_spec, whole],
         out_shape=[
             jax.ShapeDtypeStruct((32, 64, C), jnp.bfloat16),
-            jax.ShapeDtypeStruct((16, E, C), jnp.float32),
+            jax.ShapeDtypeStruct((128, 4, C), jnp.float32),
         ],
         scratch_shapes=[
             pltpu.VMEM((32, 64, C), jnp.float32),
@@ -391,13 +385,11 @@
             pltpu.VMEM((2, 12 * C, 2 * C), jnp.bfloat16),
         ],
         compiler_params=pltpu.CompilerParams(vmem_limit_bytes=32 * MIB),
-    )(places, count, x_low, x_high, partial, sums, occupied, taps, sent)
+    )(routes, x_low, x_high, partial, sums, occupied, taps)
 
 
 def finish_kernel(
-    slot_ref,
-    place_ref,
-    count_ref,
+    route_ref,
     conv_hbm,
     centre_hbm,
     face_ref,
@@ -411,7 +403,7 @@
     in_sems,
     sems,
 ):
-    count = count_ref[0]
+    count = route_ref[COUNT]
 
     def incoming(group):
         rows = pl.ds(group * GROUP, GROUP)
@@ -434,7 +426,7 @@
     bias = bias_ref[...]
 
     def copy(k):
-        return pltpu.make_async_copy(buffer.at[k], out_ref.at[slot_ref[k]], sems.at[k])
+        return pltpu.make_async_copy(buffer.at[k], out_ref.at[route_ref[SLOTS + k]], sems.at[k])
 
     def one(k, carry):
         @pl.when(k % GROUP == 0)
@@ -442,7 +434,7 @@
             for each in incoming(k // GROUP):
                 each.wait()
 
-        bx = place_ref[k] // 32
+        bx = route_ref[k] // 32
         for x in range(E):
             conv = conv_ref[k, x * 64 : (x + 1) * 64, :].astype(jnp.float32)
             if x in (0, E - 1):
@@ -464,12 +456,12 @@
     lax.fori_loop(0, count, drain, 0)
 
 
-def finish(slots, places, count, conv, centre, face, sums, gain, bias):
+def finish(routes, conv, centre, face, sums, gain, bias):
     whole = pl.BlockSpec(memory_space=pltpu.VMEM)
     scalars = pl.BlockSpec(memory_space=pltpu.SMEM)
     return pl.pallas_call(
         finish_kernel,
-        in_specs=[scalars] * 3 + [pl.BlockSpec(memory_space=pl.ANY)] * 2 + [whole] * 4,
+        in_specs=[scalars] + [pl.BlockSpec(memory_space=pl.ANY)] * 2 + [whole] * 4,
         out_specs=pl.BlockSpec(memory_space=pl.ANY),
         scratch_shapes=[
             pltpu.VMEM((32, 512, C), jnp.bfloat16),
@@ -480,21 +472,22 @@
         ],
         out_shape=jax.ShapeDtypeStruct((32, 512, C), jnp.bfloat16),
         compiler_params=pltpu.CompilerParams(vmem_limit_bytes=56 * MIB),
-    )(slots, places, count, conv, centre, face, sums, gain, bias)
+    )(routes, conv, centre, face, sums, gain, bias)
 
 
 def pick_kernel(named_ref, in_ref, out_ref, buffer, sems):
     named = named_ref[:, 3, :]
-    lane = lax.broadcasted_iota(jnp.int32, (16, C), 1)
-    source = 2 * lax.broadcasted_iota(jnp.int32, (16, C), 0) + lane
+    lane = lax.broadcasted_iota(jnp.int32, (128, C), 1)
+    device = lax.broadcasted_iota(jnp.int32, (128, C), 0)
+    source = 2 * (device // 8) + lane
+    beside = (lane < 2) & (device % 8 == lax.axis_index("gy"))
+    named = jnp.where(beside, named, -1.0)
     reads, writes = [], []
     for i in range(O):
-        hit = (named == float(i)) & (lane < 2)
-        index = jnp.sum(jnp.where(hit, source, 0))
+        index = jnp.sum(jnp.where(named == float(i), source, 0))
         reads.append(pltpu.make_async_copy(in_ref.at[index], buffer.at[i], sems.at[0, i]))
+        reads[i].start()
         writes.append(pltpu.make_async_copy(buffer.at[i], out_ref.at[i], sems.at[1, i]))
-    for read in reads:
-        read.start()
     for read, write in zip(reads, writes):
         read.wait()
         write.start()
@@ -543,8 +536,6 @@
     lines_ref,
     first_ref,
     last_ref,
-    ends_first_ref,
-    ends_last_ref,
     raw,
     sems,
 ):
@@ -572,42 +563,40 @@
                     occupancy_ref[at : at + E, :].astype(jnp.float32) * spread[by : by + 1, :]
                 )
     columns = line_columns(lines_ref)
-    for i, (ref, ends) in enumerate(((first_ref, ends_first_ref), (last_ref, ends_last_ref))):
+    for i, ref in enumerate((first_ref, last_ref)):
         copies[i].wait()
         for x in range(16):
-            line = masked_line(raw[i, x], columns, x, 15 * i)
-            ref[x, 0] = line
-            if x in (0, 15):
-                ends[x // 15, 0] = line
+            ref[x, 0] = masked_line(raw[i, x], columns, x, 15 * i)
 
 
 def x_edges_kernel(
-    owner_ref,
-    lines_ref,
-    features_ref,
-    first_ref,
-    last_ref,
-    place_ref,
-    slot_ref,
-    count_ref,
-    sent_ref,
-    raw,
-    met,
-    sems,
+    lines_ref, low_ref, high_ref, features_ref, first_ref, last_ref, raw, ends, sems
 ):
     copies = [
         pltpu.make_async_copy(features_ref.at[15 * i], raw.at[i], sems.at[i]) for i in range(2)
     ]
+    for i in range(2):
+        for j, ref in enumerate((low_ref, high_ref)):
+            copies.append(
+                pltpu.make_async_copy(ref.at[15 * i], ends.at[i, j], sems.at[2 + 2 * i + j])
+            )
     for copy in copies:
         copy.start()
-
+    columns = line_columns(lines_ref)
+    for i, ref in enumerate((first_ref, last_ref)):
+        for j in range(2):
+            copies[2 + 2 * i + j].wait()
+            ref[0, 17 * j : 17 * j + 1] = ends[i, j]
+        copies[i].wait()
+        for y in range(16):
+            ref[0, 1 + y] = masked_line(raw[i, y], columns, 15 * i, y)
+
+
+def routes_kernel(owner_ref, route_ref, met):
     for i in range(17):
         met[i] = 0
-    for i in range(32):
-        sent_ref[i] = -1
-    for i in range(48):
-        place_ref[i] = 0
-        slot_ref[i] = 0
+    for i in range(COUNT):
+        route_ref[i] = 0 if i < SENT else -1
 
     def route(i, carry):
         owned = owner_ref[i // 32, i // 16 % 2, i % 16]
@@ -619,109 +608,73 @@
             rank = met[16]
             met[owner] = met[owner] + 1
             met[16] = rank + 1
-            place_ref[rank] = i
-            slot_ref[rank] = slot
-            sent_ref[slot] = owned % 16
+            route_ref[rank] = i
+            route_ref[SLOTS + rank] = slot
+            route_ref[SENT + slot] = owned % 16
 
         return carry
 
     lax.fori_loop(0, 64, route, 0)
-    count_ref[0] = met[16]
-    count_ref[1] = (met[16] + 2 * GROUP - 1) // (2 * GROUP)
-    columns = line_columns(lines_ref)
-    for i, ref in enumerate((first_ref, last_ref)):
-        copies[i].wait()
-        for y in range(16):
-            ref[0, 1 + y] = masked_line(raw[i, y], columns, 15 * i, y)
+    route_ref[COUNT] = met[16]
+    route_ref[COUNT + 1] = (met[16] + 2 * GROUP - 1) // (2 * GROUP)
+
+
+def find_routes(owner_map):
+    scalars = pl.BlockSpec(memory_space=pltpu.SMEM)
+    return pl.pallas_call(
+        routes_kernel,
+        in_specs=[scalars],
+        out_specs=scalars,
+        out_shape=jax.ShapeDtypeStruct((COUNT + 2,), jnp.int32),
+        scratch_shapes=[pltpu.SMEM((17,), jnp.int32)],
+    )(owner_map)
 
 
 def y_edges(owner_map, occupancy, features):
     whole = pl.BlockSpec(memory_space=pltpu.VMEM)
-    blocks = [(16, 1), (16, 1), (2, 1), (2, 1)]
     return pl.pallas_call(
         y_edges_kernel,
         in_specs=[whole, whole, pl.BlockSpec(memory_space=pl.ANY)],
-        out_specs=[whole] * 5,
+        out_specs=[whole] * 3,
         out_shape=[jax.ShapeDtypeStruct((256, 128), jnp.float32)]
-        + [jax.ShapeDtypeStruct(block + (128, C), jnp.bfloat16) for block in blocks],
+        + [jax.ShapeDtypeStruct((16, 1, 128, C), jnp.bfloat16)] * 2,
         scratch_shapes=[
             pltpu.VMEM((2, 16, 128, C), jnp.bfloat16),
             pltpu.SemaphoreType.DMA((2,)),
         ],
-        compiler_params=pltpu.CompilerParams(vmem_limit_bytes=57 * MIB),
+        compiler_params=pltpu.CompilerParams(vmem_limit_bytes=53 * MIB),
     )(owner_map, occupancy, features)
 
 
-def x_edges(owner_map, lines, features):
+def x_edges(lines, y_low, y_high, features):
     whole = pl.BlockSpec(memory_space=pltpu.VMEM)
-    scalars = pl.BlockSpec(memory_space=pltpu.SMEM)
     return pl.pallas_call(
         x_edges_kernel,
-        in_specs=[scalars, whole, pl.BlockSpec(memory_space=pl.ANY)],
-        out_specs=[whole] * 2 + [scalars] * 4,
-        out_shape=[jax.ShapeDtypeStruct((1, 18, 128, C), jnp.bfloat16)] * 2
-        + [jax.ShapeDtypeStruct((n,), jnp.int32) for n in (48, 48, 2, 32)],
+        in_specs=[whole] + [pl.BlockSpec(memory_space=pl.ANY)] * 3,
+        out_specs=[whole] * 2,
+        out_shape=[jax.ShapeDtypeStruct((1, 18, 128, C), jnp.bfloat16)] * 2,
         scratch_shapes=[
             pltpu.VMEM((2, 16, 128, C), jnp.bfloat16),
-            pltpu.SMEM((17,), jnp.int32),
-            pltpu.SemaphoreType.DMA((2,)),
-        ],
-        compiler_params=pltpu.CompilerParams(vmem_limit_bytes=57 * MIB),
-    )(owner_map, lines, features)
-
-
-def widen_kernel(first_ref, last_ref, low_ref, high_ref, first_out, last_out, sems):
-    copies = []
-    for i, out in enumerate((first_out, last_out)):
-        for j, ref in enumerate((low_ref, high_ref)):
-            copies.append(
-                pltpu.make_async_copy(ref.at[i], out.at[0, 17 * j : 17 * j + 1], sems.at[i, j])
-            )
-    for copy in copies:
-        copy.start()
-    for copy in copies:
-        copy.wait()
-
-
-def widen(first, last, low, high):
-    any_spec = pl.BlockSpec(memory_space=pl.ANY)
-    return pl.pallas_call(
-        widen_kernel,
-        in_specs=[any_spec] * 2 + [pl.BlockSpec(memory_space=pltpu.VMEM)] * 2,
-        out_specs=[any_spec] * 2,
-        out_shape=[jax.ShapeDtypeStruct((1, 18, 128, C), jnp.bfloat16)] * 2,
-        scratch_shapes=[pltpu.SemaphoreType.DMA((2, 2))],
-        input_output_aliases={0: 0, 1: 1},
-    )(first, last, low, high)
+            pltpu.VMEM((2, 2, 1, 128, C), jnp.bfloat16),
+            pltpu.SemaphoreType.DMA((6,)),
+        ],
+        compiler_params=pltpu.CompilerParams(vmem_limit_bytes=51 * MIB),
+    )(lines, y_low, y_high, features)
 
 
 def on_device(features, occupancy, owner_map, kernel, norm_gain, norm_bias):
-    lines, y_first, y_last, ends_first, ends_last = y_edges(
-        owner_map, occupancy.reshape(256, 128), features
-    )
-    line_low, line_high = neighbours(ends_first, ends_last, "gy")
+    lines, y_first, y_last = y_edges(owner_map, occupancy.reshape(256, 128), features)
     y_low, y_high = neighbours(y_first, y_last, "gy")
-    x_first, x_last, places, slot_of, counts, sent = x_edges(owner_map, lines, features)
-    x_low, x_high = neighbours(*widen(x_first, x_last, line_low, line_high), "gx")
-    conv, centre, partial, sums = convolve(places, counts, features, y_low, y_high, lines, kernel)
-    face_conv, spread = correct_faces(
-        places, counts, x_low, x_high, partial, sums, lines, kernel, sent
-    )
-    arrived = swap(spread, "gx")
-    totals = swap(jnp.broadcast_to(jnp.sum(arrived, axis=0)[None], (8, E, C)), "gy")
+    routes = find_routes(owner_map)
+    x_low, x_high = neighbours(*x_edges(lines, y_low, y_high, features), "gx")
+    conv, centre, partial, sums = convolve(routes, features, y_low, y_high, lines, kernel)
+    face_conv, spread = correct_faces(routes, x_low, x_high, partial, sums, lines, kernel)
+    totals = swap(spread, ("gx", "gy"))
     result = finish(
-        slot_of,
-        places,
-        counts,
-        conv,
-        centre,
-        face_conv,
-        totals,
-        norm_gain.reshape(1, C),
-        norm_bias.reshape(1, C),
+        routes, conv, centre, face_conv, totals, norm_gain.reshape(1, C), norm_bias.reshape(1, C)
     )
     received = swap(result.reshape(16, 2, 512, C), "gx").reshape(32, 512, C)
-    return pick(arrived, received).reshape(O, 1, 512, C)
+    return pick(totals, received).reshape(O, 1, 512, C)
 
 
 def solution(mesh):

time: 162 us -> 153 us (0.944)
  blocking collectives: 89.9 us -> 83.5 us
  starting transfers between devices: 13.5 us -> 7.34 us
  Pallas kernels: 54.1 us -> 58.8 us
    all_to_all x3 -> x2, blocking collectives: 89.9 us -> 83.5 us  [swap(): return lax.all_to_all(spread, axis, 0, 0, tiled=True)]
    pallas_call x5, Pallas kernels: 46.9 us -> 52.3 us  [the longest x1 33.6 us: convolve(): pl.pallas_call(conv_kernel, in_specs=[scalars] + [any_spec] * 4 + [whole]...]
    ppermute x3 -> x2, starting transfers between devices: 9.65 us -> 4.75 us  [neighbours(): lax.ppermute(high_block, axis, up)]
    unnamed x20 -> x10, local copies, waits for them, and re-layouts: 3.9 us -> 2.38 us
    ppermute x3 -> x2, starting transfers between devices: 3.88 us -> 2.58 us  [neighbours(): lax.ppermute(low_block, axis, down)]
  transfers between devices with their start and end apart: 6 -> 4, of which waited for: 0 -> 1; matrix products, arithmetic and copies ran while one was open for 0% -> 0% of each run, Pallas kernels for 22% -> 24%
where the time goes in v5:
time: 153 us
  blocking collectives  83.5 us (55%)
  Pallas kernels  58.8 us (38%)
  starting transfers between devices  7.34 us (5%)
  local copies, waits for them, and re-layouts  2.38 us (2%)
    all_to_all x2, blocking collectives, swap(): return lax.all_to_all(spread, axis, 0, 0, tiled=True)  83.5 us
    pallas_call x1, Pallas kernels, convolve(): pl.pallas_call(conv_kernel, in_specs=[scalars] + [any_spec] * 4 + [whole]...  33.6 us
    pallas_call x1, Pallas kernels, finish(): pl.pallas_call(finish_kernel, in_specs=[scalars] + [pl.BlockSpec(memory_s...  7.68 us
    pallas_call x1, Pallas kernels, correct_faces(): pl.pallas_call(face_kernel, in_specs=[scalars, whole, whole, any_spec] +...  5.8 us
    ppermute x2, starting transfers between devices, neighbours(): lax.ppermute(high_block, axis, up)  4.75 us
    pallas_call x1, Pallas kernels, pick(): pl.pallas_call(pick_kernel, in_specs=[pl.BlockSpec(memory_space=pltpu.VME...  3.72 us
    pallas_call x1, Pallas kernels, find_routes(): pl.pallas_call(routes_kernel, in_specs=[scalars], out_specs=scalars, out_...  3.3 us
  transfers between devices with their start and end apart: 4, of which 1 were waited for; matrix products, arithmetic and copies ran while one was open for 0% of the time, Pallas kernels for 24%

profile of v5, /device:TPU:0, one launch (start us, length us, event | category | flops | bytes accessed | tf_op | source)
XLA Modules:
  0.0 153.2 jit_solution(14659794449220479684)
XLA Ops:
  0.0 0.0 copy-start.2
  0.0 0.9 copy-done.2
  0.9 0.0 copy-start.4
  0.9 0.7 copy-done.4
  1.6 2.7 %shard_map.65 = (f32[256,128]{1,0:T(8,128)S(1)}, bf16[16,1,128,128]{3,2,1,0:T(8,128)(2,1)S(1)}, bf16[16,1,128,128]{3,2,1,0:T(8,128)(2,1)}) custom-call(s32[2,2,16]{2,1,0:T(2,128)S(1)} %copy-done.4, s32[256,128]{1,0:T(8,128)S(1)} %bitcast.8, bf16[16,16,128,128]{3,2,1,0:T(8,128)(2,1)} %features_ref.5), custom_call_target="tpu_custom_call" | custom-call | tf_op jit(solution)/shard_map/pallas_call | solution.py:635
  4.3 1.3 collective-permute-start
  5.6 1.3 collective-permute-start.1
  6.9 3.3 %shard_map.64.route_ref = s32[130]{0:T(256)} custom-call(s32[2,2,16]{2,1,0:T(2,128)} %active_ref.1), custom_call_target="tpu_custom_call" | custom-call | tf_op jit(solution)/shard_map/pallas_call | solution.py:624
  10.2 0.0 collective-permute-done.low_ref.y_low_ref
  10.2 1.0 collective-permute-done.1.high_ref.y_high_ref
  11.3 0.0 copy-start
  11.3 0.0 copy-start.3
  11.3 1.9 %shard_map.66 = (bf16[1,18,128,128]{3,2,1,0:T(8,128)(2,1)S(1)}, bf16[1,18,128,128]{3,2,1,0:T(8,128)(2,1)S(1)}) custom-call(f32[256,128]{1,0:T(8,128)S(1)} %get-tuple-element.16.lines_ref.occupied_ref, bf16[16,1,128,128]{3,2,1,0:T(8,128)(2,1)S(1)} %collective-permute-done.low_ref.y_low_ref, ...), custom_call_target="tpu_custom_call" | custom-call | tf_op jit(solution)/shard_map/pallas_call | solution.py:651
  13.2 3.4 %collective-permute-start.2 = (bf16[1,18,128,128]{3,2,1,0:T(8,128)(2,1)S(1)}, bf16[1,18,128,128]{3,2,1,0:T(8,128)(2,1)S(1)}, u32[]{:S(2)}, u32[]{:S(2)}) collective-permute-start(bf16[1,18,128,128]{3,2,1,0:T(8,128)(2,1)S(1)} %get-tuple-element.19), channel_id=1, source_target_pairs={{0,8},{8,16},{16,24},{24,32},{32,40},{40,48},{48,56},{56,64},{64,7... | collective-permute-start | bytes 1769480 | tf_op jit(solution)/shard_map/ppermute | solution.py:519
  16.7 1.3 collective-permute-start.3
  18.0 0.0 copy-done
  18.0 0.0 copy-done.3
  18.0 33.6 %shard_map.67 = (bf16[32,512,128]{2,1,0:T(8,128)(2,1)}, bf16[32,512,128]{2,1,0:T(8,128)(2,1)}, f32[32,64,128]{2,1,0:T(8,128)S(1)}, f32[3,8,128]{2,1,0:T(8,128)S(1)}) custom-call(s32[130]{0:T(256)S(1)} %copy-done.3, bf16[16,16,128,128]{3,2,1,0:T(8,128)(2,1)} %features_ref.5, bf16[16,1,128,128]{3,2,1,0:T(8,128)(2,1)S(1)} %collective-permute-done.low_ref.y_low_ref, ...), custom_call_target="tpu_custom_call" | custom-call | flops 19327352832 | bytes 31457280 | tf_op jit(solution)/shard_map/pallas_call | solution.py:241
  51.6 0.0 collective-permute-done.2.x_low_ref
  51.6 0.0 collective-permute-done.3.x_high_ref
  51.6 5.8 %shard_map.68 = (bf16[32,64,128]{2,1,0:T(8,128)(2,1)S(1)}, f32[128,4,128]{2,1,0:T(4,128)S(1)}) custom-call(s32[130]{0:T(256)S(1)} %copy-done.3, bf16[1,18,128,128]{3,2,1,0:T(8,128)(2,1)S(1)} %collective-permute-done.2.x_low_ref, bf16[1,18,128,128]{3,2,1,0:T(8,128)(2,1)S(1)} %collective-permute-done.3.x_high_ref, ...), custom_call_target="tpu_custom_call" | custom-call | tf_op jit(solution)/shard_map/pallas_call | solution.py:369
  57.5 0.0 copy-start.1
  57.5 0.8 copy-done.1
  58.3 28.1 %all_to_all.10.sums_ref.named_ref = f32[128,4,128]{2,1,0:T(4,128)} all-to-all(f32[128,4,128]{2,1,0:T(4,128)S(1)} %get-tuple-element.23), channel_id=1, replica_groups=mesh['gx'=16,'gy'=8] {'gx','gy'}, dimensions={0} | all-to-all | bytes 524288 | tf_op jit(solution)/shard_map/all_to_all | solution.py:512
  86.4 7.7 %shard_map.69 = bf16[32,512,128]{2,1,0:T(8,128)(2,1)} custom-call(s32[130]{0:T(256)} %shard_map.64.route_ref, bf16[32,512,128]{2,1,0:T(8,128)(2,1)} %get-tuple-element.24.conv_hbm, bf16[32,512,128]{2,1,0:T(8,128)(2,1)} %get-tuple-element.25.centre_hbm, bf16[32,64,128]{2,1,0:T(8,128)(2,1)} %copy-done.1, f32[128,4,128]{2,1,0:T(4,128)} %all_to_all.10.sums_ref.named_ref, ...), custom_call_target="tpu_custom_call" | custom-call | tf_op jit(solution)/shard_map/pallas_call | solution.py:462
  94.1 55.4 %all_to_all.11 = bf16[16,2,512,128]{3,2,1,0:T(8,128)(2,1)} all-to-all(bf16[16,2,512,128]{3,2,1,0:T(8,128)(2,1)} %bitcast.9), channel_id=1, replica_groups=mesh['gx'=16,'gy'=8] {'gx'}, dimensions={0} | all-to-all | bytes 8388608 | tf_op jit(solution)/shard_map/all_to_all | solution.py:512
  149.4 3.7 %shard_map.70 = bf16[16,512,128]{2,1,0:T(8,128)(2,1)} custom-call(f32[128,4,128]{2,1,0:T(4,128)} %all_to_all.10.sums_ref.named_ref, bf16[32,512,128]{2,1,0:T(8,128)(2,1)} %bitcast.10), custom_call_target="tpu_custom_call" | custom-call | tf_op jit(solution)/shard_map/pallas_call | solution.py:499
Async XLA Ops:
  0.0 0.9 copy-start.2
  0.9 0.7 copy-start.4
  4.3 5.9 %collective-permute-start = (bf16[16,1,128,128]{3,2,1,0:T(8,128)(2,1)}, bf16[16,1,128,128]{3,2,1,0:T(8,128)(2,1)S(1)}, u32[]{:S(2)}, u32[]{:S(2)}) collective-permute-start(bf16[16,1,128,128]{3,2,1,0:T(8,128)(2,1)} %get-tuple-element.17), channel_id=1, source_target_pairs={{0,1},{1,2},{2,3},{3,4},{4,5},{5,6},{6,7},{8,9},{9,10},{10,11},{11... | collective-permute-start | bytes 1572872 | tf_op jit(solution)/shard_map/ppermute | solution.py:519
  5.6 5.7 %collective-permute-start.1 = (bf16[16,1,128,128]{3,2,1,0:T(8,128)(2,1)S(1)}, bf16[16,1,128,128]{3,2,1,0:T(8,128)(2,1)S(1)}, u32[]{:S(2)}, u32[]{:S(2)}) collective-permute-start(bf16[16,1,128,128]{3,2,1,0:T(8,128)(2,1)S(1)} %get-tuple-element.18), channel_id=1, source_target_pairs={{1,0},{2,1},{3,2},{4,3},{5,4},{6,5},{7,6},{9,8},{10,9},{11,10},{12... | collective-permute-start | bytes 1572872 | tf_op jit(solution)/shard_map/ppermute | solution.py:519
  11.3 6.7 %copy-start = (bf16[27,128,128]{2,1,0:T(8,128)(2,1)S(1)}, bf16[27,128,128]{2,1,0:T(8,128)(2,1)}, u32[]{:S(2)}) copy-start(bf16[27,128,128]{2,1,0:T(8,128)(2,1)} %taps_ref.1) | copy-start | bytes 2654212
  11.3 6.7 %copy-start.3 = (s32[130]{0:T(256)S(1)}, s32[130]{0:T(256)}, u32[]{:S(2)}) copy-start(s32[130]{0:T(256)} %shard_map.64.route_ref) | copy-start | bytes 1564
  13.2 38.4 %collective-permute-start.2 = (bf16[1,18,128,128]{3,2,1,0:T(8,128)(2,1)S(1)}, bf16[1,18,128,128]{3,2,1,0:T(8,128)(2,1)S(1)}, u32[]{:S(2)}, u32[]{:S(2)}) collective-permute-start(bf16[1,18,128,128]{3,2,1,0:T(8,128)(2,1)S(1)} %get-tuple-element.19), channel_id=1, source_target_pairs={{0,8},{8,16},{16,24},{24,32},{32,40},{40,48},{48,56},{56,64},{64,7... | collective-permute-start | bytes 1769480 | tf_op jit(solution)/shard_map/ppermute | solution.py:519
  16.7 35.0 %collective-permute-start.3 = (bf16[1,18,128,128]{3,2,1,0:T(8,128)(2,1)S(1)}, bf16[1,18,128,128]{3,2,1,0:T(8,128)(2,1)S(1)}, u32[]{:S(2)}, u32[]{:S(2)}) collective-permute-start(bf16[1,18,128,128]{3,2,1,0:T(8,128)(2,1)S(1)} %get-tuple-element.20), channel_id=1, source_target_pairs={{8,0},{16,8},{24,16},{32,24},{40,32},{48,40},{56,48},{64,56},{72,6... | collective-permute-start | bytes 1769480 | tf_op jit(solution)/shard_map/ppermute | solution.py:519
  57.5 0.8 copy-start.1

commit v6 on v5

--- a/solution.py
+++ b/solution.py
@@ -172,10 +172,11 @@
 
         def mask_plane(j, carry, i=i, columns=columns):
             near = pltpu.roll(columns, 128 - 64 * (i % 2) - 16 * j, axis=1)
+            near = near.astype(jnp.bfloat16)
             for y in range(16):
                 live = jnp.broadcast_to(near[:, y : y + 1], (128, C))
                 padded[1 + 4 * i + j, 1 + y, 8:136, :] = (
-                    raw[i % 2, j, y].astype(jnp.float32) * live
+                    (raw[i % 2, j, y] * live).astype(jnp.float32)
                 )
             return carry
 
@@ -274,6 +275,8 @@
     route_ref,
     x_low_ref,
     x_high_ref,
+    corner_low_ref,
+    corner_high_ref,
     partial_hbm,
     sums_ref,
     occupied_ref,
@@ -297,8 +300,11 @@
         columns_ref[i] = jnp.transpose(occupied_ref[128 * i : 128 * i + 128, :])
     padded[:, 0:8, :] = jnp.zeros((18, E, C), jnp.float32)
     padded[:, 136:144, :] = jnp.zeros((18, E, C), jnp.float32)
-    for side, ref in enumerate((x_low_ref, x_high_ref)):
-        padded[:, 8:136, :] = ref[0].astype(jnp.float32)
+    halos = ((x_low_ref, corner_low_ref), (x_high_ref, corner_high_ref))
+    for side, (ref, corner_ref) in enumerate(halos):
+        padded[1:17, 8:136, :] = ref[0].astype(jnp.float32)
+        padded[0:1, 8:136, :] = corner_ref[0].astype(jnp.float32)
+        padded[17:18, 8:136, :] = corner_ref[1].astype(jnp.float32)
         for dz in range(3):
             shifted[dz] = padded[:, 7 + dz : 135 + dz, :].astype(jnp.bfloat16).reshape(
                 9, 2, 128, C
@@ -362,13 +368,13 @@
     lax.fori_loop(0, rounds, drain, 0)
 
 
-def correct_faces(routes, x_low, x_high, partial, sums, occupied, taps):
+def correct_faces(routes, x_low, x_high, corner_low, corner_high, partial, sums, occupied, taps):
     any_spec = pl.BlockSpec(memory_space=pl.ANY)
     whole = pl.BlockSpec(memory_space=pltpu.VMEM)
     scalars = pl.BlockSpec(memory_space=pltpu.SMEM)
     return pl.pallas_call(
         face_kernel,
-        in_specs=[scalars, whole, whole, any_spec] + [whole] * 3,
+        in_specs=[scalars] + [whole] * 4 + [any_spec] + [whole] * 3,
         out_specs=[any_spec, whole],
         out_shape=[
             jax.ShapeDtypeStruct((32, 64, C), jnp.bfloat16),
@@ -385,7 +391,7 @@
             pltpu.VMEM((2, 12 * C, 2 * C), jnp.bfloat16),
         ],
         compiler_params=pltpu.CompilerParams(vmem_limit_bytes=32 * MIB),
-    )(routes, x_low, x_high, partial, sums, occupied, taps)
+    )(routes, x_low, x_high, corner_low, corner_high, partial, sums, occupied, taps)
 
 
 def finish_kernel(
@@ -422,8 +428,8 @@
     sums = jnp.sum(sums_ref[...], axis=0)
     mean = sums[0:1] / sums[2:3]
     variance = sums[1:2] / sums[2:3] - mean * mean
-    factor = gain_ref[...] / jnp.sqrt(variance + EPSILON)
-    bias = bias_ref[...]
+    factor = 0.5 * (gain_ref[...] / jnp.sqrt(variance + EPSILON))
+    bias = 0.5 * bias_ref[...]
 
     def copy(k):
         return pltpu.make_async_copy(buffer.at[k], out_ref.at[route_ref[SLOTS + k]], sems.at[k])
@@ -440,8 +446,8 @@
             if x in (0, E - 1):
                 own = face_ref[k].astype(jnp.float32)
                 conv = jnp.where(bx == (0 if x == 0 else 1), own, conv)
-            scaled = factor * (conv - mean) + bias
-            silu = scaled * (0.5 + 0.5 * jnp.tanh(0.5 * scaled))
+            halved = factor * (conv - mean) + bias
+            silu = halved + halved * jnp.tanh(halved)
             silu = jnp.where(conv > 0.5 * ABSENT, silu, 0.0)
             centre = centre_ref[k, x * 64 : (x + 1) * 64, :].astype(jnp.float32)
             buffer[k, x * 64 : (x + 1) * 64, :] = (centre + silu).astype(jnp.bfloat16)
@@ -529,18 +535,23 @@
     return [jnp.transpose(lines_ref[128 * i : 128 * i + 128, :]) for i in range(2)]
 
 
-def y_edges_kernel(
+def edges_kernel(
     active_ref,
     occupancy_ref,
     features_ref,
     lines_ref,
-    first_ref,
-    last_ref,
+    y_first_ref,
+    y_last_ref,
+    x_first_ref,
+    x_last_ref,
     raw,
     sems,
 ):
     copies = [
         pltpu.make_async_copy(features_ref.at[:, 15 * i], raw.at[i], sems.at[i]) for i in range(2)
+    ] + [
+        pltpu.make_async_copy(features_ref.at[15 * i], raw.at[2 + i], sems.at[2 + i])
+        for i in range(2)
     ]
     for copy in copies:
         copy.start()
@@ -563,33 +574,36 @@
                     occupancy_ref[at : at + E, :].astype(jnp.float32) * spread[by : by + 1, :]
                 )
     columns = line_columns(lines_ref)
-    for i, ref in enumerate((first_ref, last_ref)):
+    for i, ref in enumerate((y_first_ref, y_last_ref)):
         copies[i].wait()
         for x in range(16):
             ref[x, 0] = masked_line(raw[i, x], columns, x, 15 * i)
-
-
-def x_edges_kernel(
-    lines_ref, low_ref, high_ref, features_ref, first_ref, last_ref, raw, ends, sems
-):
+    for i, ref in enumerate((x_first_ref, x_last_ref)):
+        copies[2 + i].wait()
+        for y in range(16):
+            ref[0, y] = masked_line(raw[2 + i, y], columns, 15 * i, y)
+
+
+def corners_kernel(low_ref, high_ref, first_ref, last_ref, sems):
     copies = [
-        pltpu.make_async_copy(features_ref.at[15 * i], raw.at[i], sems.at[i]) for i in range(2)
+        pltpu.make_async_copy(ref.at[15 * i], out.at[j], sems.at[i, j])
+        for i, out in enumerate((first_ref, last_ref))
+        for j, ref in enumerate((low_ref, high_ref))
     ]
-    for i in range(2):
-        for j, ref in enumerate((low_ref, high_ref)):
-            copies.append(
-                pltpu.make_async_copy(ref.at[15 * i], ends.at[i, j], sems.at[2 + 2 * i + j])
-            )
     for copy in copies:
         copy.start()
-    columns = line_columns(lines_ref)
-    for i, ref in enumerate((first_ref, last_ref)):
-        for j in range(2):
-            copies[2 + 2 * i + j].wait()
-            ref[0, 17 * j : 17 * j + 1] = ends[i, j]
-        copies[i].wait()
-        for y in range(16):
-            ref[0, 1 + y] = masked_line(raw[i, y], columns, 15 * i, y)
+    for copy in copies:
+        copy.wait()
+
+
+def corners(y_low, y_high):
+    return pl.pallas_call(
+        corners_kernel,
+        in_specs=[pl.BlockSpec(memory_space=pl.ANY)] * 2,
+        out_specs=[pl.BlockSpec(memory_space=pltpu.VMEM)] * 2,
+        out_shape=[jax.ShapeDtypeStruct((2, 1, 128, C), jnp.bfloat16)] * 2,
+        scratch_shapes=[pltpu.SemaphoreType.DMA((2, 2))],
+    )(y_low, y_high)
 
 
 def routes_kernel(owner_ref, route_ref, met):
@@ -630,45 +644,35 @@
     )(owner_map)
 
 
-def y_edges(owner_map, occupancy, features):
+def edges(owner_map, occupancy, features):
     whole = pl.BlockSpec(memory_space=pltpu.VMEM)
     return pl.pallas_call(
-        y_edges_kernel,
+        edges_kernel,
         in_specs=[whole, whole, pl.BlockSpec(memory_space=pl.ANY)],
-        out_specs=[whole] * 3,
+        out_specs=[whole] * 5,
         out_shape=[jax.ShapeDtypeStruct((256, 128), jnp.float32)]
-        + [jax.ShapeDtypeStruct((16, 1, 128, C), jnp.bfloat16)] * 2,
+        + [jax.ShapeDtypeStruct((16, 1, 128, C), jnp.bfloat16)] * 2
+        + [jax.ShapeDtypeStruct((1, 16, 128, C), jnp.bfloat16)] * 2,
         scratch_shapes=[
-            pltpu.VMEM((2, 16, 128, C), jnp.bfloat16),
-            pltpu.SemaphoreType.DMA((2,)),
+            pltpu.VMEM((4, 16, 128, C), jnp.bfloat16),
+            pltpu.SemaphoreType.DMA((4,)),
         ],
         compiler_params=pltpu.CompilerParams(vmem_limit_bytes=53 * MIB),
     )(owner_map, occupancy, features)
 
 
-def x_edges(lines, y_low, y_high, features):
-    whole = pl.BlockSpec(memory_space=pltpu.VMEM)
-    return pl.pallas_call(
-        x_edges_kernel,
-        in_specs=[whole] + [pl.BlockSpec(memory_space=pl.ANY)] * 3,
-        out_specs=[whole] * 2,
-        out_shape=[jax.ShapeDtypeStruct((1, 18, 128, C), jnp.bfloat16)] * 2,
-        scratch_shapes=[
-            pltpu.VMEM((2, 16, 128, C), jnp.bfloat16),
-            pltpu.VMEM((2, 2, 1, 128, C), jnp.bfloat16),
-            pltpu.SemaphoreType.DMA((6,)),
-        ],
-        compiler_params=pltpu.CompilerParams(vmem_limit_bytes=51 * MIB),
-    )(lines, y_low, y_high, features)
-
-
 def on_device(features, occupancy, owner_map, kernel, norm_gain, norm_bias):
-    lines, y_first, y_last = y_edges(owner_map, occupancy.reshape(256, 128), features)
+    lines, y_first, y_last, x_first, x_last = edges(
+        owner_map, occupancy.reshape(256, 128), features
+    )
     y_low, y_high = neighbours(y_first, y_last, "gy")
+    x_low, x_high = neighbours(x_first, x_last, "gx")
     routes = find_routes(owner_map)
-    x_low, x_high = neighbours(*x_edges(lines, y_low, y_high, features), "gx")
+    corner_low, corner_high = neighbours(*corners(y_low, y_high), "gx")
     conv, centre, partial, sums = convolve(routes, features, y_low, y_high, lines, kernel)
-    face_conv, spread = correct_faces(routes, x_low, x_high, partial, sums, lines, kernel)
+    face_conv, spread = correct_faces(
+        routes, x_low, x_high, corner_low, corner_high, partial, sums, lines, kernel
+    )
     totals = swap(spread, ("gx", "gy"))
     result = finish(
         routes, conv, centre, face_conv, totals, norm_gain.reshape(1, C), norm_bias.reshape(1, C)

time: 153 us -> 161 us (1.052); the launches traced: 153 us -> 159 us
  Pallas kernels: 58.8 us -> 42.5 us
  blocking collectives: 83.5 us -> 95.8 us
  starting transfers between devices: 7.34 us -> 13.7 us
  local copies, waits for them, and re-layouts: 2.38 us -> 6.7 us
    pallas_call x1, Pallas kernels: 33.6 us -> 20.7 us  [convolve(): pl.pallas_call(conv_kernel, in_specs=[scalars] + [any_spec] * 4 + [whole]...]
    all_to_all x2, blocking collectives: 83.5 us -> 95.8 us  [swap(): return lax.all_to_all(spread, axis, 0, 0, tiled=True)]
    ppermute x2 -> x3, starting transfers between devices: 4.75 us -> 9.83 us  [neighbours(): lax.ppermute(high_block, axis, up)]
    unnamed x10 -> x18, local copies, waits for them, and re-layouts: 2.38 us -> 6.7 us
    pallas_call x1, Pallas kernels: 7.68 us -> 5.1 us  [finish(): pl.pallas_call(finish_kernel, in_specs=[scalars] + [pl.BlockSpec(memory_s...]
    ppermute x2 -> x3, starting transfers between devices: 2.58 us -> 3.88 us  [neighbours(): lax.ppermute(low_block, axis, down)]
  transfers between devices with their start and end apart: 4 -> 6, of which waited for: 1 -> 0; matrix products, arithmetic and copies ran while one was open for 0% -> 0% of each run, Pallas kernels for 24% -> 16%
where the time goes in v6:
time: 161 us; the launch traced here: 159 us
  blocking collectives  95.8 us (60%)
  Pallas kernels  42.5 us (26%)
  starting transfers between devices  13.7 us (9%)
  local copies, waits for them, and re-layouts  6.7 us (4%)
    all_to_all x2, blocking collectives, swap(): return lax.all_to_all(spread, axis, 0, 0, tiled=True)  95.8 us
    pallas_call x1, Pallas kernels, convolve(): pl.pallas_call(conv_kernel, in_specs=[scalars] + [any_spec] * 4 + [whole]...  20.7 us
    ppermute x3, starting transfers between devices, neighbours(): lax.ppermute(high_block, axis, up)  9.83 us
    unnamed x18, local copies, waits for them, and re-layouts  6.7 us
    pallas_call x1, Pallas kernels, finish(): pl.pallas_call(finish_kernel, in_specs=[scalars] + [pl.BlockSpec(memory_s...  5.1 us
    pallas_call x1, Pallas kernels, correct_faces(): pl.pallas_call(face_kernel, in_specs=[scalars] + [whole] * 4 + [any_spec]...  4.51 us
    ppermute x3, starting transfers between devices, neighbours(): lax.ppermute(low_block, axis, down)  3.88 us
    pallas_call x1, Pallas kernels, pick(): pl.pallas_call(pick_kernel, in_specs=[pl.BlockSpec(memory_space=pltpu.VME...  3.72 us
  transfers between devices with their start and end apart: 6, of which 0 were waited for; matrix products, arithmetic and copies ran while one was open for 0% of the time, Pallas kernels for 16%

profile of v6, /device:TPU:0, one launch (start us, length us, event | category | flops | bytes accessed | tf_op | source)
XLA Modules:
  0.0 159.0 jit_solution(869954846254728804)
XLA Ops:
  0.0 0.9 copy-done.6
  0.9 0.7 copy-done.8
  1.6 3.6 %shard_map.65 = (f32[256,128]{1,0:T(8,128)S(1)}, bf16[16,1,128,128]{3,2,1,0:T(8,128)(2,1)}, bf16[16,1,128,128]{3,2,1,0:T(8,128)(2,1)}, bf16[1,16,128,128]{3,2,1,0:T(8,128)(2,1)}, bf16[1,16,128,128]{3,2,1,0:T(8,128)(2,1)}) custom-call(s32[2,2,16]{2,1,0:T(2,128)S(1)} %copy-done.8, s32[256,128]{1,0:T(8,128)S(1)} %bitcast.8, bf16[16,16,128,128]{3,2,1,0:T(8,128)(2,1)} %features_ref.3), custom_call_target="tpu_custom_call" | custom-call | tf_op jit(solution)/shard_map/pallas_call | solution.py:649
  5.2 1.3 collective-permute-start.2
  6.6 1.3 collective-permute-start.3
  7.9 4.0 %collective-permute-start = (bf16[1,16,128,128]{3,2,1,0:T(8,128)(2,1)}, bf16[1,16,128,128]{3,2,1,0:T(8,128)(2,1)S(1)}, u32[]{:S(2)}, u32[]{:S(2)}) collective-permute-start(bf16[1,16,128,128]{3,2,1,0:T(8,128)(2,1)} %get-tuple-element.18), channel_id=1, source_target_pairs={{0,8},{8,16},{16,24},{24,32},{32,40},{40,48},{48,56},{56,64},{64,7... | collective-permute-start | bytes 1572872 | tf_op jit(solution)/shard_map/ppermute | solution.py:525
  11.8 1.3 collective-permute-start.1
  13.1 3.3 %shard_map.64.route_ref = s32[130]{0:T(256)} custom-call(s32[2,2,16]{2,1,0:T(2,128)} %active_ref.1), custom_call_target="tpu_custom_call" | custom-call | tf_op jit(solution)/shard_map/pallas_call | solution.py:638
  16.4 0.0 collective-permute-done.2.low_ref.y_low_ref
  16.5 0.0 copy-start.2
  16.5 0.0 collective-permute-done.3.high_ref.y_high_ref
  16.5 0.8 copy-done.2
  17.3 0.8 copy-done.4
  18.1 1.5 shard_map.66
  19.6 4.5 %collective-permute-start.4 = (bf16[2,1,128,128]{3,2,1,0:T(8,128)(2,1)}, bf16[2,1,128,128]{3,2,1,0:T(8,128)(2,1)S(1)}, u32[]{:S(2)}, u32[]{:S(2)}) collective-permute-start(bf16[2,1,128,128]{3,2,1,0:T(8,128)(2,1)} %get-tuple-element.22), channel_id=1, source_target_pairs={{0,8},{8,16},{16,24},{24,32},{32,40},{40,48},{48,56},{56,64},{64,7... | collective-permute-start | bytes 196616 | tf_op jit(solution)/shard_map/ppermute | solution.py:525
  24.1 1.3 collective-permute-start.5
  25.4 0.0 copy-done
  25.4 1.0 copy-done.3
  26.5 1.0 copy-done.5
  27.5 0.7 copy-done.7
  28.2 20.7 %shard_map.67 = (bf16[32,512,128]{2,1,0:T(8,128)(2,1)}, bf16[32,512,128]{2,1,0:T(8,128)(2,1)}, f32[32,64,128]{2,1,0:T(8,128)S(1)}, f32[3,8,128]{2,1,0:T(8,128)S(1)}) custom-call(s32[130]{0:T(256)S(1)} %copy-done.7, bf16[16,16,128,128]{3,2,1,0:T(8,128)(2,1)} %features_ref.3, bf16[16,1,128,128]{3,2,1,0:T(8,128)(2,1)S(1)} %copy-done.3, ...), custom_call_target="tpu_custom_call" | custom-call | flops 19327352832 | bytes 31457280 | tf_op jit(solution)/shard_map/pallas_call | solution.py:242
  48.9 0.0 collective-permute-done.x_low_ref
  48.9 0.0 collective-permute-done.1.x_high_ref
  49.0 0.0 collective-permute-done.4.corner_low_ref
  49.0 0.0 collective-permute-done.5.corner_high_ref
  49.0 4.5 %shard_map.68 = (bf16[32,64,128]{2,1,0:T(8,128)(2,1)S(1)}, f32[128,4,128]{2,1,0:T(4,128)S(1)}) custom-call(s32[130]{0:T(256)S(1)} %copy-done.7, bf16[1,16,128,128]{3,2,1,0:T(8,128)(2,1)S(1)} %collective-permute-done.x_low_ref, bf16[1,16,128,128]{3,2,1,0:T(8,128)(2,1)S(1)} %collective-permute-done.1.x_high_ref, ...), custom_call_target="tpu_custom_call" | custom-call | tf_op jit(solution)/shard_map/pallas_call | solution.py:375
  53.5 0.0 copy-start.1
  53.5 0.8 copy-done.1
  54.3 39.1 %all_to_all.10.sums_ref.named_ref = f32[128,4,128]{2,1,0:T(4,128)} all-to-all(f32[128,4,128]{2,1,0:T(4,128)S(1)} %get-tuple-element.27), channel_id=1, replica_groups=mesh['gx'=16,'gy'=8] {'gx','gy'}, dimensions={0} | all-to-all | bytes 524288 | tf_op jit(solution)/shard_map/all_to_all | solution.py:518
  93.4 5.1 %shard_map.69 = bf16[32,512,128]{2,1,0:T(8,128)(2,1)} custom-call(s32[130]{0:T(256)} %shard_map.64.route_ref, bf16[32,512,128]{2,1,0:T(8,128)(2,1)} %get-tuple-element.28.conv_hbm, bf16[32,512,128]{2,1,0:T(8,128)(2,1)} %get-tuple-element.29.centre_hbm, bf16[32,64,128]{2,1,0:T(8,128)(2,1)} %copy-done.1, f32[128,4,128]{2,1,0:T(4,128)} %all_to_all.10.sums_ref.named_ref, ...), custom_call_target="tpu_custom_call" | custom-call | tf_op jit(solution)/shard_map/pallas_call | solution.py:468
  98.5 56.7 %all_to_all.11 = bf16[16,2,512,128]{3,2,1,0:T(8,128)(2,1)} all-to-all(bf16[16,2,512,128]{3,2,1,0:T(8,128)(2,1)} %bitcast.9), channel_id=1, replica_groups=mesh['gx'=16,'gy'=8] {'gx'}, dimensions={0} | all-to-all | bytes 8388608 | tf_op jit(solution)/shard_map/all_to_all | solution.py:518
  155.2 3.7 %shard_map.70 = bf16[16,512,128]{2,1,0:T(8,128)(2,1)} custom-call(f32[128,4,128]{2,1,0:T(4,128)} %all_to_all.10.sums_ref.named_ref, bf16[32,512,128]{2,1,0:T(8,128)(2,1)} %bitcast.10), custom_call_target="tpu_custom_call" | custom-call | tf_op jit(solution)/shard_map/pallas_call | solution.py:505
  (7 shorter events, 0.0 us)
Async XLA Ops:
  0.0 0.9 copy-start.6
  0.9 0.7 copy-start.8
  1.6 23.8 %copy-start = (bf16[27,128,128]{2,1,0:T(8,128)(2,1)S(1)}, bf16[27,128,128]{2,1,0:T(8,128)(2,1)}, u32[]{:S(2)}) copy-start(bf16[27,128,128]{2,1,0:T(8,128)(2,1)} %taps_ref.1) | copy-start | bytes 2654212
  5.2 11.2 %collective-permute-start.2 = (bf16[16,1,128,128]{3,2,1,0:T(8,128)(2,1)}, bf16[16,1,128,128]{3,2,1,0:T(8,128)(2,1)S(1)}, u32[]{:S(2)}, u32[]{:S(2)}) collective-permute-start(bf16[16,1,128,128]{3,2,1,0:T(8,128)(2,1)} %get-tuple-element.20), channel_id=1, source_target_pairs={{0,1},{1,2},{2,3},{3,4},{4,5},{5,6},{6,7},{8,9},{9,10},{10,11},{11... | collective-permute-start | bytes 1572872 | tf_op jit(solution)/shard_map/ppermute | solution.py:525
  6.6 9.9 %collective-permute-start.3 = (bf16[16,1,128,128]{3,2,1,0:T(8,128)(2,1)}, bf16[16,1,128,128]{3,2,1,0:T(8,128)(2,1)S(1)}, u32[]{:S(2)}, u32[]{:S(2)}) collective-permute-start(bf16[16,1,128,128]{3,2,1,0:T(8,128)(2,1)} %get-tuple-element.21), channel_id=1, source_target_pairs={{1,0},{2,1},{3,2},{4,3},{5,4},{6,5},{7,6},{9,8},{10,9},{11,10},{12... | collective-permute-start | bytes 1572872 | tf_op jit(solution)/shard_map/ppermute | solution.py:525
  7.9 41.1 %collective-permute-start = (bf16[1,16,128,128]{3,2,1,0:T(8,128)(2,1)}, bf16[1,16,128,128]{3,2,1,0:T(8,128)(2,1)S(1)}, u32[]{:S(2)}, u32[]{:S(2)}) collective-permute-start(bf16[1,16,128,128]{3,2,1,0:T(8,128)(2,1)} %get-tuple-element.18), channel_id=1, source_target_pairs={{0,8},{8,16},{16,24},{24,32},{32,40},{40,48},{48,56},{56,64},{64,7... | collective-permute-start | bytes 1572872 | tf_op jit(solution)/shard_map/ppermute | solution.py:525
  11.8 37.1 %collective-permute-start.1 = (bf16[1,16,128,128]{3,2,1,0:T(8,128)(2,1)}, bf16[1,16,128,128]{3,2,1,0:T(8,128)(2,1)S(1)}, u32[]{:S(2)}, u32[]{:S(2)}) collective-permute-start(bf16[1,16,128,128]{3,2,1,0:T(8,128)(2,1)} %get-tuple-element.19), channel_id=1, source_target_pairs={{8,0},{16,8},{24,16},{32,24},{40,32},{48,40},{56,48},{64,56},{72,6... | collective-permute-start | bytes 1572872 | tf_op jit(solution)/shard_map/ppermute | solution.py:525
  16.5 0.8 copy-start.2
  17.3 0.8 copy-start.4
  19.6 29.4 %collective-permute-start.4 = (bf16[2,1,128,128]{3,2,1,0:T(8,128)(2,1)}, bf16[2,1,128,128]{3,2,1,0:T(8,128)(2,1)S(1)}, u32[]{:S(2)}, u32[]{:S(2)}) collective-permute-start(bf16[2,1,128,128]{3,2,1,0:T(8,128)(2,1)} %get-tuple-element.22), channel_id=1, source_target_pairs={{0,8},{8,16},{16,24},{24,32},{32,40},{40,48},{48,56},{56,64},{64,7... | collective-permute-start | bytes 196616 | tf_op jit(solution)/shard_map/ppermute | solution.py:525
  24.1 24.9 %collective-permute-start.5 = (bf16[2,1,128,128]{3,2,1,0:T(8,128)(2,1)}, bf16[2,1,128,128]{3,2,1,0:T(8,128)(2,1)S(1)}, u32[]{:S(2)}, u32[]{:S(2)}) collective-permute-start(bf16[2,1,128,128]{3,2,1,0:T(8,128)(2,1)} %get-tuple-element.23), channel_id=1, source_target_pairs={{8,0},{16,8},{24,16},{32,24},{40,32},{48,40},{56,48},{64,56},{72,6... | collective-permute-start | bytes 196616 | tf_op jit(solution)/shard_map/ppermute | solution.py:525
  25.4 1.0 copy-start.3
  26.5 1.0 copy-start.5
  27.5 0.7 copy-start.7
  53.5 0.8 copy-start.1

commit v7 on v5

--- a/solution.py
+++ b/solution.py
@@ -172,10 +172,11 @@
 
         def mask_plane(j, carry, i=i, columns=columns):
             near = pltpu.roll(columns, 128 - 64 * (i % 2) - 16 * j, axis=1)
+            near = near.astype(jnp.bfloat16)
             for y in range(16):
                 live = jnp.broadcast_to(near[:, y : y + 1], (128, C))
                 padded[1 + 4 * i + j, 1 + y, 8:136, :] = (
-                    raw[i % 2, j, y].astype(jnp.float32) * live
+                    (raw[i % 2, j, y] * live).astype(jnp.float32)
                 )
             return carry
 
@@ -422,8 +423,8 @@
     sums = jnp.sum(sums_ref[...], axis=0)
     mean = sums[0:1] / sums[2:3]
     variance = sums[1:2] / sums[2:3] - mean * mean
-    factor = gain_ref[...] / jnp.sqrt(variance + EPSILON)
-    bias = bias_ref[...]
+    factor = 0.5 * (gain_ref[...] / jnp.sqrt(variance + EPSILON))
+    bias = 0.5 * bias_ref[...]
 
     def copy(k):
         return pltpu.make_async_copy(buffer.at[k], out_ref.at[route_ref[SLOTS + k]], sems.at[k])
@@ -440,8 +441,8 @@
             if x in (0, E - 1):
                 own = face_ref[k].astype(jnp.float32)
                 conv = jnp.where(bx == (0 if x == 0 else 1), own, conv)
-            scaled = factor * (conv - mean) + bias
-            silu = scaled * (0.5 + 0.5 * jnp.tanh(0.5 * scaled))
+            halved = factor * (conv - mean) + bias
+            silu = halved + halved * jnp.tanh(halved)
             silu = jnp.where(conv > 0.5 * ABSENT, silu, 0.0)
             centre = centre_ref[k, x * 64 : (x + 1) * 64, :].astype(jnp.float32)
             buffer[k, x * 64 : (x + 1) * 64, :] = (centre + silu).astype(jnp.bfloat16)

time: 153 us -> 153 us (level); the launches traced: 153 us -> 150 us
  Pallas kernels: 58.8 us -> 41.2 us
  blocking collectives: 83.5 us -> 98 us
    all_to_all x2, blocking collectives: 83.5 us -> 98 us  [swap(): return lax.all_to_all(spread, axis, 0, 0, tiled=True)]
    pallas_call x1, Pallas kernels: 33.6 us -> 20.6 us  [convolve(): pl.pallas_call(conv_kernel, in_specs=[scalars] + [any_spec] * 4 + [whole]...]
    pallas_call x1, Pallas kernels: 7.68 us -> 4.74 us  [finish(): pl.pallas_call(finish_kernel, in_specs=[scalars] + [pl.BlockSpec(memory_s...]
    pallas_call x1, Pallas kernels: 5.8 us -> 4.22 us  [correct_faces(): pl.pallas_call(face_kernel, in_specs=[scalars, whole, whole, any_spec] +...]
  transfers between devices with their start and end apart: 4 -> 4, of which waited for: 1 -> 1; matrix products, arithmetic and copies ran while one was open for 0% -> 0% of each run, Pallas kernels for 24% -> 16%
where the time goes in v7:
time: 153 us; the launch traced here: 150 us
  blocking collectives  98 us (64%)
  Pallas kernels  41.2 us (27%)
  starting transfers between devices  7.34 us (5%)
  local copies, waits for them, and re-layouts  2.38 us (2%)
    all_to_all x2, blocking collectives, swap(): return lax.all_to_all(spread, axis, 0, 0, tiled=True)  98 us
    pallas_call x1, Pallas kernels, convolve(): pl.pallas_call(conv_kernel, in_specs=[scalars] + [any_spec] * 4 + [whole]...  20.6 us
    ppermute x2, starting transfers between devices, neighbours(): lax.ppermute(high_block, axis, up)  4.75 us
    pallas_call x1, Pallas kernels, finish(): pl.pallas_call(finish_kernel, in_specs=[scalars] + [pl.BlockSpec(memory_s...  4.74 us
    pallas_call x1, Pallas kernels, correct_faces(): pl.pallas_call(face_kernel, in_specs=[scalars, whole, whole, any_spec] +...  4.22 us
    pallas_call x1, Pallas kernels, pick(): pl.pallas_call(pick_kernel, in_specs=[pl.BlockSpec(memory_space=pltpu.VME...  3.72 us
    pallas_call x1, Pallas kernels, find_routes(): pl.pallas_call(routes_kernel, in_specs=[scalars], out_specs=scalars, out_...  3.3 us
  transfers between devices with their start and end apart: 4, of which 1 were waited for; matrix products, arithmetic and copies ran while one was open for 0% of the time, Pallas kernels for 16%

profile of v7, /device:TPU:0, one launch (start us, length us, event | category | flops | bytes accessed | tf_op | source)
XLA Modules:
  0.0 150.2 jit_solution(11763271261377246788)
XLA Ops:
  0.0 0.0 copy-start.2
  0.0 0.9 copy-done.2
  0.9 0.0 copy-start.4
  0.9 0.7 copy-done.4
  1.6 2.7 %shard_map.65 = (f32[256,128]{1,0:T(8,128)S(1)}, bf16[16,1,128,128]{3,2,1,0:T(8,128)(2,1)S(1)}, bf16[16,1,128,128]{3,2,1,0:T(8,128)(2,1)}) custom-call(s32[2,2,16]{2,1,0:T(2,128)S(1)} %copy-done.4, s32[256,128]{1,0:T(8,128)S(1)} %bitcast.8, bf16[16,16,128,128]{3,2,1,0:T(8,128)(2,1)} %features_ref.5), custom_call_target="tpu_custom_call" | custom-call | tf_op jit(solution)/shard_map/pallas_call | solution.py:636
  4.3 1.3 collective-permute-start
  5.6 1.3 collective-permute-start.1
  6.9 3.3 %shard_map.64.route_ref = s32[130]{0:T(256)} custom-call(s32[2,2,16]{2,1,0:T(2,128)} %active_ref.1), custom_call_target="tpu_custom_call" | custom-call | tf_op jit(solution)/shard_map/pallas_call | solution.py:625
  10.2 0.0 collective-permute-done.low_ref.y_low_ref
  10.2 1.0 collective-permute-done.1.high_ref.y_high_ref
  11.3 0.0 copy-start
  11.3 0.0 copy-start.3
  11.3 1.9 %shard_map.66 = (bf16[1,18,128,128]{3,2,1,0:T(8,128)(2,1)S(1)}, bf16[1,18,128,128]{3,2,1,0:T(8,128)(2,1)S(1)}) custom-call(f32[256,128]{1,0:T(8,128)S(1)} %get-tuple-element.16.lines_ref.occupied_ref, bf16[16,1,128,128]{3,2,1,0:T(8,128)(2,1)S(1)} %collective-permute-done.low_ref.y_low_ref, ...), custom_call_target="tpu_custom_call" | custom-call | tf_op jit(solution)/shard_map/pallas_call | solution.py:652
  13.2 3.4 %collective-permute-start.2 = (bf16[1,18,128,128]{3,2,1,0:T(8,128)(2,1)S(1)}, bf16[1,18,128,128]{3,2,1,0:T(8,128)(2,1)S(1)}, u32[]{:S(2)}, u32[]{:S(2)}) collective-permute-start(bf16[1,18,128,128]{3,2,1,0:T(8,128)(2,1)S(1)} %get-tuple-element.19), channel_id=1, source_target_pairs={{0,8},{8,16},{16,24},{24,32},{32,40},{40,48},{48,56},{56,64},{64,7... | collective-permute-start | bytes 1769480 | tf_op jit(solution)/shard_map/ppermute | solution.py:520
  16.7 1.3 collective-permute-start.3
  18.0 0.0 copy-done
  18.0 0.0 copy-done.3
  18.0 20.6 %shard_map.67 = (bf16[32,512,128]{2,1,0:T(8,128)(2,1)}, bf16[32,512,128]{2,1,0:T(8,128)(2,1)}, f32[32,64,128]{2,1,0:T(8,128)S(1)}, f32[3,8,128]{2,1,0:T(8,128)S(1)}) custom-call(s32[130]{0:T(256)S(1)} %copy-done.3, bf16[16,16,128,128]{3,2,1,0:T(8,128)(2,1)} %features_ref.5, bf16[16,1,128,128]{3,2,1,0:T(8,128)(2,1)S(1)} %collective-permute-done.low_ref.y_low_ref, ...), custom_call_target="tpu_custom_call" | custom-call | flops 19327352832 | bytes 31457280 | tf_op jit(solution)/shard_map/pallas_call | solution.py:242
  38.6 0.0 collective-permute-done.2.x_low_ref
  38.6 0.0 collective-permute-done.3.x_high_ref
  38.6 4.2 %shard_map.68 = (bf16[32,64,128]{2,1,0:T(8,128)(2,1)S(1)}, f32[128,4,128]{2,1,0:T(4,128)S(1)}) custom-call(s32[130]{0:T(256)S(1)} %copy-done.3, bf16[1,18,128,128]{3,2,1,0:T(8,128)(2,1)S(1)} %collective-permute-done.2.x_low_ref, bf16[1,18,128,128]{3,2,1,0:T(8,128)(2,1)S(1)} %collective-permute-done.3.x_high_ref, ...), custom_call_target="tpu_custom_call" | custom-call | tf_op jit(solution)/shard_map/pallas_call | solution.py:370
  42.9 0.0 copy-start.1
  42.9 0.8 copy-done.1
  43.7 40.8 %all_to_all.10.sums_ref.named_ref = f32[128,4,128]{2,1,0:T(4,128)} all-to-all(f32[128,4,128]{2,1,0:T(4,128)S(1)} %get-tuple-element.23), channel_id=1, replica_groups=mesh['gx'=16,'gy'=8] {'gx','gy'}, dimensions={0} | all-to-all | bytes 524288 | tf_op jit(solution)/shard_map/all_to_all | solution.py:513
  84.4 4.7 %shard_map.69 = bf16[32,512,128]{2,1,0:T(8,128)(2,1)} custom-call(s32[130]{0:T(256)} %shard_map.64.route_ref, bf16[32,512,128]{2,1,0:T(8,128)(2,1)} %get-tuple-element.24.conv_hbm, bf16[32,512,128]{2,1,0:T(8,128)(2,1)} %get-tuple-element.25.centre_hbm, bf16[32,64,128]{2,1,0:T(8,128)(2,1)} %copy-done.1, f32[128,4,128]{2,1,0:T(4,128)} %all_to_all.10.sums_ref.named_ref, ...), custom_call_target="tpu_custom_call" | custom-call | tf_op jit(solution)/shard_map/pallas_call | solution.py:463
  89.2 57.3 %all_to_all.11 = bf16[16,2,512,128]{3,2,1,0:T(8,128)(2,1)} all-to-all(bf16[16,2,512,128]{3,2,1,0:T(8,128)(2,1)} %bitcast.9), channel_id=1, replica_groups=mesh['gx'=16,'gy'=8] {'gx'}, dimensions={0} | all-to-all | bytes 8388608 | tf_op jit(solution)/shard_map/all_to_all | solution.py:513
  146.4 3.7 %shard_map.70 = bf16[16,512,128]{2,1,0:T(8,128)(2,1)} custom-call(f32[128,4,128]{2,1,0:T(4,128)} %all_to_all.10.sums_ref.named_ref, bf16[32,512,128]{2,1,0:T(8,128)(2,1)} %bitcast.10), custom_call_target="tpu_custom_call" | custom-call | tf_op jit(solution)/shard_map/pallas_call | solution.py:500
Async XLA Ops:
  0.0 0.9 copy-start.2
  0.9 0.7 copy-start.4
  4.3 5.9 %collective-permute-start = (bf16[16,1,128,128]{3,2,1,0:T(8,128)(2,1)}, bf16[16,1,128,128]{3,2,1,0:T(8,128)(2,1)S(1)}, u32[]{:S(2)}, u32[]{:S(2)}) collective-permute-start(bf16[16,1,128,128]{3,2,1,0:T(8,128)(2,1)} %get-tuple-element.17), channel_id=1, source_target_pairs={{0,1},{1,2},{2,3},{3,4},{4,5},{5,6},{6,7},{8,9},{9,10},{10,11},{11... | collective-permute-start | bytes 1572872 | tf_op jit(solution)/shard_map/ppermute | solution.py:520
  5.6 5.7 %collective-permute-start.1 = (bf16[16,1,128,128]{3,2,1,0:T(8,128)(2,1)S(1)}, bf16[16,1,128,128]{3,2,1,0:T(8,128)(2,1)S(1)}, u32[]{:S(2)}, u32[]{:S(2)}) collective-permute-start(bf16[16,1,128,128]{3,2,1,0:T(8,128)(2,1)S(1)} %get-tuple-element.18), channel_id=1, source_target_pairs={{1,0},{2,1},{3,2},{4,3},{5,4},{6,5},{7,6},{9,8},{10,9},{11,10},{12... | collective-permute-start | bytes 1572872 | tf_op jit(solution)/shard_map/ppermute | solution.py:520
  11.3 6.7 %copy-start = (bf16[27,128,128]{2,1,0:T(8,128)(2,1)S(1)}, bf16[27,128,128]{2,1,0:T(8,128)(2,1)}, u32[]{:S(2)}) copy-start(bf16[27,128,128]{2,1,0:T(8,128)(2,1)} %taps_ref.1) | copy-start | bytes 2654212
  11.3 6.7 %copy-start.3 = (s32[130]{0:T(256)S(1)}, s32[130]{0:T(256)}, u32[]{:S(2)}) copy-start(s32[130]{0:T(256)} %shard_map.64.route_ref) | copy-start | bytes 1564
  13.2 25.4 %collective-permute-start.2 = (bf16[1,18,128,128]{3,2,1,0:T(8,128)(2,1)S(1)}, bf16[1,18,128,128]{3,2,1,0:T(8,128)(2,1)S(1)}, u32[]{:S(2)}, u32[]{:S(2)}) collective-permute-start(bf16[1,18,128,128]{3,2,1,0:T(8,128)(2,1)S(1)} %get-tuple-element.19), channel_id=1, source_target_pairs={{0,8},{8,16},{16,24},{24,32},{32,40},{40,48},{48,56},{56,64},{64,7... | collective-permute-start | bytes 1769480 | tf_op jit(solution)/shard_map/ppermute | solution.py:520
  16.7 22.0 %collective-permute-start.3 = (bf16[1,18,128,128]{3,2,1,0:T(8,128)(2,1)S(1)}, bf16[1,18,128,128]{3,2,1,0:T(8,128)(2,1)S(1)}, u32[]{:S(2)}, u32[]{:S(2)}) collective-permute-start(bf16[1,18,128,128]{3,2,1,0:T(8,128)(2,1)S(1)} %get-tuple-element.20), channel_id=1, source_target_pairs={{8,0},{16,8},{24,16},{32,24},{40,32},{48,40},{56,48},{64,56},{72,6... | collective-permute-start | bytes 1769480 | tf_op jit(solution)/shard_map/ppermute | solution.py:520
  42.9 0.8 copy-start.1

commit v8 on v7

--- a/solution.py
+++ b/solution.py
@@ -166,6 +166,12 @@
     sums_ref[...] = jnp.zeros_like(sums_ref)
     for i in range(2):
         columns_ref[i] = jnp.transpose(occupied_ref[128 * i : 128 * i + 128, :])
+    eye = jnp.where(
+        lax.broadcasted_iota(jnp.int32, (C, C), 0) == lax.broadcasted_iota(jnp.int32, (C, C), 1),
+        1.0,
+        0.0,
+    )
+    ones = jnp.ones((C, C), jnp.bfloat16)
     for i in range(4):
         chunks[i].wait()
         columns = columns_ref[i // 2]
@@ -174,7 +180,15 @@
             near = pltpu.roll(columns, 128 - 64 * (i % 2) - 16 * j, axis=1)
             near = near.astype(jnp.bfloat16)
             for y in range(16):
-                live = jnp.broadcast_to(near[:, y : y + 1], (128, C))
+                if y % 3 == 1:
+                    line = occupied_ref[pl.ds((4 * i + j) * 16 + y, 1), :]
+                    live = jnp.dot(
+                        (eye * line).astype(jnp.bfloat16),
+                        ones,
+                        preferred_element_type=jnp.float32,
+                    ).astype(jnp.bfloat16)
+                else:
+                    live = jnp.broadcast_to(near[:, y : y + 1], (128, C))
                 padded[1 + 4 * i + j, 1 + y, 8:136, :] = (
                     (raw[i % 2, j, y] * live).astype(jnp.float32)
                 )

time: 153 us -> 152 us (level); the launches traced: 150 us -> 151 us
  Pallas kernels: 41.2 us -> 48 us
  blocking collectives: 98 us -> 92 us
    all_to_all x2, blocking collectives: 98 us -> 92 us  [swap(): return lax.all_to_all(spread, axis, 0, 0, tiled=True)]
    pallas_call x1, Pallas kernels: 20.6 us -> 25.9 us  [convolve(): pl.pallas_call(conv_kernel, in_specs=[scalars] + [any_spec] * 4 + [whole]...]
  transfers between devices with their start and end apart: 4 -> 4, of which waited for: 1 -> 1; matrix products, arithmetic and copies ran while one was open for 0% -> 0% of each run, Pallas kernels for 16% -> 19%
where the time goes in v8:
time: 152 us; the launch traced here: 151 us
  blocking collectives  92 us (61%)
  Pallas kernels  48 us (32%)
  starting transfers between devices  7.34 us (5%)
  local copies, waits for them, and re-layouts  2.38 us (2%)
    all_to_all x2, blocking collectives, swap(): return lax.all_to_all(spread, axis, 0, 0, tiled=True)  92 us
    pallas_call x1, Pallas kernels, convolve(): pl.pallas_call(conv_kernel, in_specs=[scalars] + [any_spec] * 4 + [whole]...  25.9 us
    pallas_call x1, Pallas kernels, finish(): pl.pallas_call(finish_kernel, in_specs=[scalars] + [pl.BlockSpec(memory_s...  5.71 us
    pallas_call x1, Pallas kernels, correct_faces(): pl.pallas_call(face_kernel, in_specs=[scalars, whole, whole, any_spec] +...  4.85 us
    ppermute x2, starting transfers between devices, neighbours(): lax.ppermute(high_block, axis, up)  4.75 us
    pallas_call x1, Pallas kernels, pick(): pl.pallas_call(pick_kernel, in_specs=[pl.BlockSpec(memory_space=pltpu.VME...  3.72 us
    pallas_call x1, Pallas kernels, find_routes(): pl.pallas_call(routes_kernel, in_specs=[scalars], out_specs=scalars, out_...  3.3 us
  transfers between devices with their start and end apart: 4, of which 1 were waited for; matrix products, arithmetic and copies ran while one was open for 0% of the time, Pallas kernels for 19%

profile of v8, /device:TPU:0, one launch (start us, length us, event | category | flops | bytes accessed | tf_op | source)
XLA Modules:
  0.0 151.0 jit_solution(13310179446741106644)
XLA Ops:
  0.0 0.0 copy-start.2
  0.0 0.9 copy-done.2
  0.9 0.0 copy-start.4
  0.9 0.7 copy-done.4
  1.6 2.7 %shard_map.65 = (f32[256,128]{1,0:T(8,128)S(1)}, bf16[16,1,128,128]{3,2,1,0:T(8,128)(2,1)S(1)}, bf16[16,1,128,128]{3,2,1,0:T(8,128)(2,1)}) custom-call(s32[2,2,16]{2,1,0:T(2,128)S(1)} %copy-done.4, s32[256,128]{1,0:T(8,128)S(1)} %bitcast.8, bf16[16,16,128,128]{3,2,1,0:T(8,128)(2,1)} %features_ref.5), custom_call_target="tpu_custom_call" | custom-call | tf_op jit(solution)/shard_map/pallas_call | solution.py:650
  4.3 1.3 collective-permute-start
  5.6 1.3 collective-permute-start.1
  6.9 3.3 %shard_map.64.route_ref = s32[130]{0:T(256)} custom-call(s32[2,2,16]{2,1,0:T(2,128)} %active_ref.1), custom_call_target="tpu_custom_call" | custom-call | tf_op jit(solution)/shard_map/pallas_call | solution.py:639
  10.2 0.0 collective-permute-done.low_ref.y_low_ref
  10.2 1.0 collective-permute-done.1.high_ref.y_high_ref
  11.3 0.0 copy-start
  11.3 0.0 copy-start.3
  11.3 1.9 %shard_map.66 = (bf16[1,18,128,128]{3,2,1,0:T(8,128)(2,1)S(1)}, bf16[1,18,128,128]{3,2,1,0:T(8,128)(2,1)S(1)}) custom-call(f32[256,128]{1,0:T(8,128)S(1)} %get-tuple-element.16.lines_ref.occupied_ref, bf16[16,1,128,128]{3,2,1,0:T(8,128)(2,1)S(1)} %collective-permute-done.low_ref.y_low_ref, ...), custom_call_target="tpu_custom_call" | custom-call | tf_op jit(solution)/shard_map/pallas_call | solution.py:666
  13.2 3.4 %collective-permute-start.2 = (bf16[1,18,128,128]{3,2,1,0:T(8,128)(2,1)S(1)}, bf16[1,18,128,128]{3,2,1,0:T(8,128)(2,1)S(1)}, u32[]{:S(2)}, u32[]{:S(2)}) collective-permute-start(bf16[1,18,128,128]{3,2,1,0:T(8,128)(2,1)S(1)} %get-tuple-element.19), channel_id=1, source_target_pairs={{0,8},{8,16},{16,24},{24,32},{32,40},{40,48},{48,56},{56,64},{64,7... | collective-permute-start | bytes 1769480 | tf_op jit(solution)/shard_map/ppermute | solution.py:534
  16.7 1.3 collective-permute-start.3
  18.0 0.0 copy-done
  18.0 0.0 copy-done.3
  18.0 25.9 %shard_map.67 = (bf16[32,512,128]{2,1,0:T(8,128)(2,1)}, bf16[32,512,128]{2,1,0:T(8,128)(2,1)}, f32[32,64,128]{2,1,0:T(8,128)S(1)}, f32[3,8,128]{2,1,0:T(8,128)S(1)}) custom-call(s32[130]{0:T(256)S(1)} %copy-done.3, bf16[16,16,128,128]{3,2,1,0:T(8,128)(2,1)} %features_ref.5, bf16[16,1,128,128]{3,2,1,0:T(8,128)(2,1)S(1)} %collective-permute-done.low_ref.y_low_ref, ...), custom_call_target="tpu_custom_call" | custom-call | flops 19327352832 | bytes 31457280 | tf_op jit(solution)/shard_map/pallas_call | solution.py:256
  43.8 0.0 collective-permute-done.2.x_low_ref
  43.8 0.0 collective-permute-done.3.x_high_ref
  43.9 4.8 %shard_map.68 = (bf16[32,64,128]{2,1,0:T(8,128)(2,1)S(1)}, f32[128,4,128]{2,1,0:T(4,128)S(1)}) custom-call(s32[130]{0:T(256)S(1)} %copy-done.3, bf16[1,18,128,128]{3,2,1,0:T(8,128)(2,1)S(1)} %collective-permute-done.2.x_low_ref, bf16[1,18,128,128]{3,2,1,0:T(8,128)(2,1)S(1)} %collective-permute-done.3.x_high_ref, ...), custom_call_target="tpu_custom_call" | custom-call | tf_op jit(solution)/shard_map/pallas_call | solution.py:384
  48.7 0.0 copy-start.1
  48.7 0.8 copy-done.1
  49.5 35.4 %all_to_all.10.sums_ref.named_ref = f32[128,4,128]{2,1,0:T(4,128)} all-to-all(f32[128,4,128]{2,1,0:T(4,128)S(1)} %get-tuple-element.23), channel_id=1, replica_groups=mesh['gx'=16,'gy'=8] {'gx','gy'}, dimensions={0} | all-to-all | bytes 524288 | tf_op jit(solution)/shard_map/all_to_all | solution.py:527
  85.0 5.7 %shard_map.69 = bf16[32,512,128]{2,1,0:T(8,128)(2,1)} custom-call(s32[130]{0:T(256)} %shard_map.64.route_ref, bf16[32,512,128]{2,1,0:T(8,128)(2,1)} %get-tuple-element.24.conv_hbm, bf16[32,512,128]{2,1,0:T(8,128)(2,1)} %get-tuple-element.25.centre_hbm, bf16[32,64,128]{2,1,0:T(8,128)(2,1)} %copy-done.1, f32[128,4,128]{2,1,0:T(4,128)} %all_to_all.10.sums_ref.named_ref, ...), custom_call_target="tpu_custom_call" | custom-call | tf_op jit(solution)/shard_map/pallas_call | solution.py:477
  90.7 56.6 %all_to_all.11 = bf16[16,2,512,128]{3,2,1,0:T(8,128)(2,1)} all-to-all(bf16[16,2,512,128]{3,2,1,0:T(8,128)(2,1)} %bitcast.9), channel_id=1, replica_groups=mesh['gx'=16,'gy'=8] {'gx'}, dimensions={0} | all-to-all | bytes 8388608 | tf_op jit(solution)/shard_map/all_to_all | solution.py:527
  147.3 3.7 %shard_map.70 = bf16[16,512,128]{2,1,0:T(8,128)(2,1)} custom-call(f32[128,4,128]{2,1,0:T(4,128)} %all_to_all.10.sums_ref.named_ref, bf16[32,512,128]{2,1,0:T(8,128)(2,1)} %bitcast.10), custom_call_target="tpu_custom_call" | custom-call | tf_op jit(solution)/shard_map/pallas_call | solution.py:514
Async XLA Ops:
  0.0 0.9 copy-start.2
  0.9 0.7 copy-start.4
  4.3 5.9 %collective-permute-start = (bf16[16,1,128,128]{3,2,1,0:T(8,128)(2,1)}, bf16[16,1,128,128]{3,2,1,0:T(8,128)(2,1)S(1)}, u32[]{:S(2)}, u32[]{:S(2)}) collective-permute-start(bf16[16,1,128,128]{3,2,1,0:T(8,128)(2,1)} %get-tuple-element.17), channel_id=1, source_target_pairs={{0,1},{1,2},{2,3},{3,4},{4,5},{5,6},{6,7},{8,9},{9,10},{10,11},{11... | collective-permute-start | bytes 1572872 | tf_op jit(solution)/shard_map/ppermute | solution.py:534
  5.6 5.7 %collective-permute-start.1 = (bf16[16,1,128,128]{3,2,1,0:T(8,128)(2,1)S(1)}, bf16[16,1,128,128]{3,2,1,0:T(8,128)(2,1)S(1)}, u32[]{:S(2)}, u32[]{:S(2)}) collective-permute-start(bf16[16,1,128,128]{3,2,1,0:T(8,128)(2,1)S(1)} %get-tuple-element.18), channel_id=1, source_target_pairs={{1,0},{2,1},{3,2},{4,3},{5,4},{6,5},{7,6},{9,8},{10,9},{11,10},{12... | collective-permute-start | bytes 1572872 | tf_op jit(solution)/shard_map/ppermute | solution.py:534
  11.3 6.7 %copy-start = (bf16[27,128,128]{2,1,0:T(8,128)(2,1)S(1)}, bf16[27,128,128]{2,1,0:T(8,128)(2,1)}, u32[]{:S(2)}) copy-start(bf16[27,128,128]{2,1,0:T(8,128)(2,1)} %taps_ref.1) | copy-start | bytes 2654212
  11.3 6.7 %copy-start.3 = (s32[130]{0:T(256)S(1)}, s32[130]{0:T(256)}, u32[]{:S(2)}) copy-start(s32[130]{0:T(256)} %shard_map.64.route_ref) | copy-start | bytes 1564
  13.2 30.6 %collective-permute-start.2 = (bf16[1,18,128,128]{3,2,1,0:T(8,128)(2,1)S(1)}, bf16[1,18,128,128]{3,2,1,0:T(8,128)(2,1)S(1)}, u32[]{:S(2)}, u32[]{:S(2)}) collective-permute-start(bf16[1,18,128,128]{3,2,1,0:T(8,128)(2,1)S(1)} %get-tuple-element.19), channel_id=1, source_target_pairs={{0,8},{8,16},{16,24},{24,32},{32,40},{40,48},{48,56},{56,64},{64,7... | collective-permute-start | bytes 1769480 | tf_op jit(solution)/shard_map/ppermute | solution.py:534
  16.7 27.2 %collective-permute-start.3 = (bf16[1,18,128,128]{3,2,1,0:T(8,128)(2,1)S(1)}, bf16[1,18,128,128]{3,2,1,0:T(8,128)(2,1)S(1)}, u32[]{:S(2)}, u32[]{:S(2)}) collective-permute-start(bf16[1,18,128,128]{3,2,1,0:T(8,128)(2,1)S(1)} %get-tuple-element.20), channel_id=1, source_target_pairs={{8,0},{16,8},{24,16},{32,24},{40,32},{48,40},{56,48},{64,56},{72,6... | collective-permute-start | bytes 1769480 | tf_op jit(solution)/shard_map/ppermute | solution.py:534
  48.7 0.8 copy-start.1
